TPU v7x, 512 devices: a whole 4x8x8 slice. The times are simulated.
512 devices in a mesh: ctx: 64 (over z, x, core), tp: 8 (over y).
Axes of the slice: x: 4, y: 8, z: 8, core: 2. Of those that a mesh axis runs over, the one named last changes fastest.
Arguments:
- queries: bfloat16 [256, 8192], P('tp', 'ctx'), may hold values from -9 to 9
- keys: bfloat16 [65536, 1024], P('ctx', 'tp'), may hold values from -6 to 6
- values: bfloat16 [65536, 1024], P('ctx', 'tp'), may hold values from -6 to 6
- counts: int32 [64], P('ctx'), may hold values from 1 to 1024, 49152 in all
- resp_len: int32 [1], replicated, may hold values from 128 to 256
Outputs:
- attended: bfloat16 [256, 8192], P('ctx', 'tp')
Inputs may be any that keep to these rules, and one draw needn't show every extreme that they name: `counts`: the largest block count is exactly 1024; every block has at least one valid token.
All inputs are finite; a program needn't handle non-finite values.
Results may differ from a plain program's by a relative error of at most 0.0046.
Values may be sent and summed in bfloat16 or wider, within the bound.
No kernel may reach another device: no remote copies, remote signals or barrier semaphores. Data moves between devices by JAX's collectives and lax.ppermute only.
A program may use at most 64 MiB of HBM per device.

v0:
```python
import jax
import jax.numpy as jnp
from jax import lax
from jax.sharding import PartitionSpec as P

H = 64
KVH = 8
HS = 128


def local(queries, keys, values, counts, resp_len):
    heads_all = lax.all_gather(queries, "ctx", axis=1, tiled=True)
    own_rows = lax.all_to_all(heads_all, "tp", split_axis=1, concat_axis=0, tiled=True)
    row_count = own_rows.shape[0]
    groups = keys.shape[1] // HS
    group_size = H // KVH
    score_scale = 1.0 / HS**0.5
    slot_count = keys.shape[0]
    row_block = min(64, row_count)
    block_count = row_count // row_block
    query_blocks = own_rows.reshape(block_count, row_block, groups, group_size, HS)
    key_slots = keys.reshape(slot_count, groups, HS)
    value_slots = values.reshape(slot_count, groups, HS)
    in_block = jnp.arange(slot_count, dtype=jnp.int32) < counts[0]

    def one_rows(query):
        scores = (
            jnp.einsum("rgqd,lgd->rgql", query, key_slots, preferred_element_type=jnp.float32)
            * score_scale
        )
        scores = jnp.where(in_block, scores, -jnp.inf)
        row_max = jnp.max(scores, axis=-1)
        weights = jnp.exp(scores - row_max[..., None]).astype(jnp.bfloat16)
        row_sum = jnp.sum(weights.astype(jnp.float32), axis=-1)
        output = jnp.einsum(
            "rgql,lgd->rgqd", weights, value_slots, preferred_element_type=jnp.float32
        )
        return (output, row_max, row_sum)

    output, row_max, row_sum = lax.map(one_rows, query_blocks)
    flat_out = output.reshape(row_count, groups * group_size * HS)
    flat_max = row_max.reshape(row_count, groups * group_size)
    flat_sum = row_sum.reshape(row_count, groups * group_size)
    ctx_index = lax.axis_index("ctx")
    own_count = row_count // lax.axis_size("ctx")
    parts_out, parts_max, parts_sum = (
        lax.all_to_all(flat_out[None], "ctx", split_axis=1, concat_axis=0, tiled=True),
        lax.all_to_all(flat_max[None], "ctx", split_axis=1, concat_axis=0, tiled=True),
        lax.all_to_all(flat_sum[None], "ctx", split_axis=1, concat_axis=0, tiled=True),
    )
    peak_all = jnp.max(parts_max, axis=0)
    rescale = jnp.exp(parts_max - peak_all[None])
    source_count = parts_out.shape[0]
    numer = jnp.sum(
        parts_out.reshape(source_count, own_count, -1, HS) * rescale[..., None], axis=0
    ).reshape(own_count, -1)
    denom = jnp.sum(parts_sum * rescale, axis=0)
    result = (numer.reshape(own_count, -1, HS) / denom[..., None]).reshape(own_count, -1)
    row_ids = ctx_index * own_count + jnp.arange(own_count, dtype=jnp.int32)
    live = (row_ids < resp_len[0])[:, None]
    return jnp.where(live, result, 0.0).astype(jnp.bfloat16)


def solution(mesh):
    in_specs = (P("tp", "ctx"), P("ctx", "tp"), P("ctx", "tp"), P("ctx"), P())
    out_specs = P("ctx", "tp")
    return jax.shard_map(local, mesh=mesh, in_specs=in_specs, out_specs=out_specs, check_vma=False)
```

profile of v0, /device:TPU:6, one launch (start us, length us, event | category | flops | bytes accessed | tf_op | source)
XLA Modules:
  0.0 163.1 jit_solution(15678938625647539989)
XLA Ops:
  0.0 56.3 %all_gather.3 = bf16[32,8192]{1,0:T(8,128)(2,1)S(1)} all-gather(bf16[32,128]{1,0:T(8,128)(2,1)} %param.7), channel_id=1, replica_groups=mesh['ctx'=64,'tp'=8] {'ctx'}, dimensions={1}, use_global_device_ids=true | all-gather | bytes 532480 | tf_op jit(solution)/shard_map/all_gather | solution.py:12
  56.3 0.9 copy.29
  57.1 7.1 %all-to-all-start = ((bf16[32,8,1024]{2,0,1:T(8,128)(2,1)}), bf16[32,8,1024]{2,0,1:T(8,128)(2,1)S(1)}, u32[]{:S(2)}, u32[]{:S(2)}) async-start(bf16[32,8,1024]{2,0,1:T(8,128)(2,1)} %bitcast.86), calls=%async_computation | async-start | bytes 1048576 | tf_op jit(solution)/shard_map/all_to_all | solution.py:13
  64.3 18.0 %all-to-all-done = bf16[32,8,1024]{2,0,1:T(8,128)(2,1)S(1)} async-done(((bf16[32,8,1024]{2,0,1:T(8,128)(2,1)}), bf16[32,8,1024]{2,0,1:T(8,128)(2,1)S(1)}, u32[]{:S(2)}, u32[]{:S(2)}) %all-to-all-start) | async-done | bytes 524320 | tf_op jit(solution)/shard_map/all_to_all | solution.py:13
  82.3 0.1 copy.23
  82.4 12.2 %while.15 = (s32[]{:T(128)}, f32[4,64,1,8,128]{4,3,1,2,0:T(8,128)}, f32[4,64,1,8]{3,1,2,0:T(8,128)S(1)}, f32[4,64,1,8]{3,1,2,0:T(8,128)S(1)}, bf16[4,64,1,8,128]...) while((s32[]{:T(128)}, f32[4,64,1,8,128]{4,3,1,2,0:T(8,128)}, ...), condition=%wide.region_3.4_spmd.clone, body=%wide.region_0.3_spmd.clone.sunk | while | flops 275251200 | bytes 7352937 | solution.py:40
  82.4 0.7 iota_compare_fusion.2
  83.0 0.5 fusion.20
  83.6 0.6 convert_reduce_fusion.2
  84.1 1.3 fusion.21
  85.4 0.6 iota_compare_fusion.2
  86.1 0.5 fusion.20
  86.6 0.6 convert_reduce_fusion.2
  87.2 1.3 fusion.21
  88.5 0.6 iota_compare_fusion.2
  89.1 0.5 fusion.20
  89.7 0.6 convert_reduce_fusion.2
  90.2 1.3 fusion.21
  91.6 0.6 iota_compare_fusion.2
  92.2 0.5 fusion.20
  92.7 0.6 convert_reduce_fusion.2
  93.3 1.3 fusion.21
  94.6 15.2 %all_to_all.52 = f32[1,256,8]{2,0,1:T(1,128)S(1)} all-to-all(f32[1,256,8]{2,0,1:T(1,128)S(1)} %bitcast.121), channel_id=1, replica_groups=mesh['ctx'=64,'tp'=8] {'ctx'}, dimensions={1} | all-to-all | bytes 16384 | tf_op jit(solution)/shard_map/all_to_all | solution.py:48
  109.8 14.9 %all_to_all.53 = f32[1,256,8]{2,0,1:T(1,128)S(1)} all-to-all(f32[1,256,8]{2,0,1:T(1,128)S(1)} %bitcast.122), channel_id=1, replica_groups=mesh['ctx'=64,'tp'=8] {'ctx'}, dimensions={1} | all-to-all | bytes 16384 | tf_op jit(solution)/shard_map/all_to_all | solution.py:49
  124.7 6.5 %all-to-all-start.1 = ((f32[1,256,1024]{2,0,1:T(1,128)}), f32[1,256,1024]{2,0,1:T(1,128)S(1)}, u32[]{:S(2)}, u32[]{:S(2)}) async-start(f32[1,256,1024]{2,0,1:T(1,128)} %bitcast.5), calls=%async_computation.1 | async-start | bytes 2097152 | tf_op jit(solution)/shard_map/all_to_all | solution.py:47
  131.9 0.1 reduce_max.18
  131.9 0.1 multiply_reduce_fusion.1
  132.0 0.1 broadcast_bitcast_fusion
  132.1 28.0 %all-to-all-done.1 = f32[1,256,1024]{2,0,1:T(1,128)S(1)} async-done(((f32[1,256,1024]{2,0,1:T(1,128)}), f32[1,256,1024]{2,0,1:T(1,128)S(1)}, u32[]{:S(2)}, u32[]{:S(2)}) %all-to-all-start.1) | async-done | bytes 1048608 | tf_op jit(solution)/shard_map/all_to_all | solution.py:47
  160.1 0.3 mul.40
  160.4 2.0 %multiply_reduce_fusion = f32[4,1024]{1,0:T(4,128)S(1)} fusion(f32[1,64,4,1024]{3,0,2,1:T(1,128)S(1)} %bitcast.113, f32[1,64,4,1024]{3,0,2,1:T(1,128)S(1)} %bitcast.114), kind=kLoop, calls=%fused_computation.20 | loop fusion | flops 520192 | bytes 2113536 | tf_op jit(solution)/shard_map/reduce_sum | solution.py:54
  162.5 0.7 select_convert_fusion
  (12 shorter events, 0.1 us)
Async XLA Ops:
  0.0 82.4 %copy-start = (bf16[1024,128]{1,0:T(8,128)(2,1)S(1)}, bf16[1024,128]{1,0:T(8,128)(2,1)}, u32[]{:S(2)}) copy-start(bf16[1024,128]{1,0:T(8,128)(2,1)} %param.8) | copy-start | bytes 786436
  0.0 82.4 %copy-start.1 = (bf16[1024,128]{1,0:T(8,128)(2,1)S(1)}, bf16[1024,128]{1,0:T(8,128)(2,1)}, u32[]{:S(2)}) copy-start(bf16[1024,128]{1,0:T(8,128)(2,1)} %param.9) | copy-start | bytes 786436
  57.1 25.1 %all-to-all-start = ((bf16[32,8,1024]{2,0,1:T(8,128)(2,1)}), bf16[32,8,1024]{2,0,1:T(8,128)(2,1)S(1)}, u32[]{:S(2)}, u32[]{:S(2)}) async-start(bf16[32,8,1024]{2,0,1:T(8,128)(2,1)} %bitcast.86), calls=%async_computation | async-start | bytes 1048576 | tf_op jit(solution)/shard_map/all_to_all | solution.py:13
  124.7 35.4 %all-to-all-start.1 = ((f32[1,256,1024]{2,0,1:T(1,128)}), f32[1,256,1024]{2,0,1:T(1,128)S(1)}, u32[]{:S(2)}, u32[]{:S(2)}) async-start(f32[1,256,1024]{2,0,1:T(1,128)} %bitcast.5), calls=%async_computation.1 | async-start | bytes 2097152 | tf_op jit(solution)/shard_map/all_to_all | solution.py:47
where the time goes:
time: 164 us; the launch traced here: 163 us
  blocking collectives  86.4 us (53%)
  waiting for transfers between devices  46 us (28%)
  starting transfers between devices  13.6 us (8%)
  other arithmetic  7.71 us (5%)
  matrix products  7.3 us (4%)
    all_gather x1, blocking collectives, local(): heads_all = lax.all_gather(queries, 'ctx', axis=1, tiled=True)  56.3 us
    all_to_all x1, waiting for transfers between devices, local(): lax.all_to_all(flat_out[None], 'ctx', split_axis=1, concat_axis=0, tiled=...  28 us
    all_to_all x1, waiting for transfers between devices, local(): lax.all_to_all(heads_all, 'tp', split_axis=1, concat_axis=0, tiled=True)  18 us
    all_to_all x1, blocking collectives, local(): lax.all_to_all(flat_max[None], 'ctx', split_axis=1, concat_axis=0, tiled=...  15.2 us
    all_to_all x1, blocking collectives, local(): lax.all_to_all(flat_sum[None], 'ctx', split_axis=1, concat_axis=0, tiled=...  14.9 us
    all_to_all x1, starting transfers between devices, local(): lax.all_to_all(heads_all, 'tp', split_axis=1, concat_axis=0, tiled=True)  7.1 us
    all_to_all x1, starting transfers between devices, local(): lax.all_to_all(flat_out[None], 'ctx', split_axis=1, concat_axis=0, tiled=...  6.47 us
    dot_general x4, matrix products, one_rows(): jnp.einsum('rgql,lgd->rgqd', weights, value_slots, preferred_element_type...  5.21 us
  transfers between devices with their start and end apart: 2, of which 2 were waited for; matrix products, arithmetic and copies ran while one was open for 0% of the time, Pallas kernels for 0%

commit v1 on v0

v1 whole, which is shorter than its diff:
```python
import jax
import jax.numpy as jnp
from jax import lax
from jax.experimental import pallas as pl
from jax.experimental.pallas import tpu as pltpu
from jax.sharding import Mesh, PartitionSpec as P

HS = 128
LOG2E = 1.4426950408889634
EXP2_SCALE = LOG2E / HS**0.5
NZ, NX, NC, NY = 8, 4, 2, 8
SLOTS = 1024
SRC = NZ * NX
PAIRS = 32
SLOT_ROWS = 40
COUNT_BASE = 64
MASKED = -1e30


def lane_ids(shape):
    return lax.broadcasted_iota(jnp.int32, shape, len(shape) - 1)


def attend_kernel(count_ref, q_ref, key_ref, value_ref, got_ref, out_ref, wide_ref):
    ones = jnp.ones((SLOTS, HS), jnp.bfloat16)
    for block, rows in enumerate((value_ref[...], got_ref[SLOTS : 2 * SLOTS, :])):
        wide_ref[block, :, :HS] = rows
        wide_ref[block, :, HS:] = ones
    slot = lane_ids((1, SLOTS))
    tail = got_ref[2 * SLOTS + 16 : 2 * SLOTS + 32, :].astype(jnp.float32)
    got_count = tail[0:1] * COUNT_BASE + tail[1:2]
    got_count = jnp.concatenate([got_count] * (SLOTS // HS), axis=1).astype(jnp.int32)
    biases = (
        jnp.where(slot < count_ref[0], 0.0, MASKED),
        jnp.where(slot < got_count, 0.0, MASKED),
    )

    tile = 2 * NX * PAIRS
    pair = lax.broadcasted_iota(jnp.int32, (8, PAIRS, HS), 1)
    lane = lane_ids((8, PAIRS, HS))
    diagonal = (lane % PAIRS) == pair
    part = lane // PAIRS
    sub = lax.broadcasted_iota(jnp.int32, (8, 8, HS), 1)

    def by_slot(x):
        return jnp.swapaxes(x.reshape(NX, 2, NX, 8, HS), 0, 1).swapaxes(1, 2).reshape(8, PAIRS, HS)

    for step in range(NY // 2):
        q = q_ref[:, 2 * step : 2 * step + 2].reshape(tile, HS)
        found = []
        for block in range(2):
            keys = key_ref[...] if block == 0 else got_ref[:SLOTS, :]
            scores = lax.dot_general(
                q, keys, (((1,), (1,)), ((), ())), preferred_element_type=jnp.float32
            )
            scores = scores + biases[block]
            peak = jnp.max(scores, axis=1, keepdims=True)
            weights = jnp.exp2((scores - peak) * EXP2_SCALE).astype(jnp.bfloat16)
            both = jnp.dot(weights, wide_ref[block], preferred_element_type=jnp.float32)
            found.append((both[:, :HS], both[:, HS:], peak))
        (out0, sum0, peak0), (out1, sum1, peak1) = found
        ref = jnp.maximum(peak0, peak1).astype(jnp.bfloat16).astype(jnp.float32)
        scale0 = jnp.exp2((peak0 - ref) * EXP2_SCALE)
        scale1 = jnp.exp2((peak1 - ref) * EXP2_SCALE)
        out = by_slot(out0 * scale0 + out1 * scale1)
        total = by_slot(sum0 * scale0 + sum1 * scale1)
        ref = by_slot(jnp.broadcast_to(ref, (tile, HS)))
        high = total.astype(jnp.bfloat16).astype(jnp.float32)
        stats = jnp.where(part == 0, ref, jnp.where(part == 1, high, total - high))
        stats = jnp.where(diagonal & (part < 3), stats, 0.0)
        stats = jnp.sum(stats, axis=1, keepdims=True)
        stats = jnp.where(sub == 0, stats, 0.0)
        full = jnp.concatenate([out, stats], axis=1).reshape(8 * SLOT_ROWS, HS)
        out_ref[8 * SLOT_ROWS * step : 8 * SLOT_ROWS * (step + 1), :] = full.astype(jnp.bfloat16)


def merge_kernel(live_ref, parts_ref, out_ref):
    parts = parts_ref[...].astype(jnp.float32).reshape(SRC, SLOT_ROWS, HS)
    stats = parts[:, PAIRS, :]
    stats = jnp.concatenate([stats, jnp.zeros((HS - SRC, HS), jnp.float32)], axis=0).T
    valid = lane_ids((PAIRS, HS)) < SRC
    peaks = jnp.where(valid, stats[:PAIRS], -jnp.inf)
    sums = stats[PAIRS : 2 * PAIRS] + stats[2 * PAIRS : 3 * PAIRS]
    peak = jnp.max(peaks, axis=1, keepdims=True)
    scale = jnp.exp2((peaks - peak) * EXP2_SCALE)
    denom = jnp.sum(scale * sums, axis=1, keepdims=True)
    numer = parts[0, :PAIRS] * scale[:, 0:1]
    for src in range(1, SRC):
        numer = numer + parts[src, :PAIRS] * scale[:, src : src + 1]
    result = numer / denom
    rows = PAIRS // 8
    row = lax.broadcasted_iota(jnp.int32, (rows, HS), 0)
    live = row < live_ref[0]
    for head in range(8):
        block = result[rows * head : rows * (head + 1)]
        out_ref[:, HS * head : HS * (head + 1)] = jnp.where(live, block, 0.0).astype(jnp.bfloat16)


def local(queries, keys, values, counts, resp_len):
    core = lax.axis_index("core")
    with jax.named_scope("pair_exchange"):
        halves = queries.reshape(NX, NC, 4, HS)
        first, second = halves[:, 0], halves[:, 1]
        own = jnp.where(core == 0, first, second)
        other = jnp.where(core == 0, second, first).reshape(16, HS)
        count_rows = jnp.stack([counts[0] // COUNT_BASE, counts[0] % COUNT_BASE])
        count_rows = jnp.broadcast_to(count_rows[:, None].astype(jnp.bfloat16), (2, HS))
        tail = jnp.concatenate([count_rows, jnp.zeros((14, HS), jnp.bfloat16)], axis=0)
        send = jnp.concatenate([keys, values, other, tail], axis=0)
        got = lax.ppermute(send, "core", [(0, 1), (1, 0)])
        theirs = got[2 * SLOTS : 2 * SLOTS + 16].reshape(NX, 4, HS)
        block = jnp.stack(
            [jnp.where(core == 0, own, theirs), jnp.where(core == 0, theirs, own)], axis=1
        ).reshape(PAIRS, HS)
    with jax.named_scope("query_spread"):
        groups = lax.all_to_all(
            jnp.broadcast_to(block[None], (NZ, PAIRS, HS)), "z", 0, 0, tiled=True
        )
        groups = jnp.broadcast_to(groups[None], (NX, NY, PAIRS, HS)).reshape(SRC, PAIRS, HS)
        spread = lax.all_to_all(groups, ("x", "tp"), 0, 0, tiled=True)
        spread = spread.reshape(NX, NY, PAIRS, HS)
    vmem = pl.BlockSpec(memory_space=pltpu.VMEM)
    smem = pl.BlockSpec(memory_space=pltpu.SMEM)
    with jax.named_scope("attend"):
        parts = pl.pallas_call(
            attend_kernel,
            out_shape=jax.ShapeDtypeStruct((SRC * SLOT_ROWS, HS), jnp.bfloat16),
            in_specs=[smem, vmem, vmem, vmem, vmem],
            out_specs=vmem,
            scratch_shapes=[pltpu.VMEM((2, SLOTS, 2 * HS), jnp.bfloat16)],
            compiler_params=pltpu.CompilerParams(vmem_limit_bytes=32 * 2**20),
        )(counts, spread, keys, values, got)
    with jax.named_scope("merge"):
        parts = lax.all_to_all(
            parts.reshape(SRC, SLOT_ROWS, HS), ("z", "x"), 0, 0, tiled=True
        ).reshape(SRC * SLOT_ROWS, HS)
        index = lax.axis_index(("z", "x", "core"))
        live = resp_len - index * 4
        return pl.pallas_call(
            merge_kernel,
            out_shape=jax.ShapeDtypeStruct((4, 8 * HS), jnp.bfloat16),
            in_specs=[smem, vmem],
            out_specs=vmem,
            compiler_params=pltpu.CompilerParams(vmem_limit_bytes=32 * 2**20),
        )(live, parts)


def solution(mesh):
    grid = Mesh(mesh.devices.reshape(NZ, NX, NC, NY), ("z", "x", "core", "tp"))
    ctx = ("z", "x", "core")
    in_specs = (P("tp", ctx), P(ctx, "tp"), P(ctx, "tp"), P(ctx), P())
    return jax.shard_map(
        local, mesh=grid, in_specs=in_specs, out_specs=P(ctx, "tp"), check_vma=False
    )
```

time: 164 us -> 68.8 us (0.42)
  the two profiles are of different devices: /device:TPU:6 before, /device:TPU:8 now
where the time goes in v1:
time: 68.8 us; the launch traced here: 68.4 us
  blocking collectives  39.8 us (58%)
  waiting for transfers between devices  13.4 us (19%)
  starting transfers between devices  5.79 us (8%)
  Pallas kernels  5.03 us (7%)
  local copies, waits for them, and re-layouts  2.88 us (4%)
  between operations  1.43 us (2%)
    all_to_all x1, blocking collectives, local(): spread = lax.all_to_all(groups, ('x', 'tp'), 0, 0, tiled=True)  21.3 us
    all_to_all x1, blocking collectives, local(): lax.all_to_all(jnp.broadcast_to(block[None], (NZ, PAIRS, HS)), 'z', 0, 0,...  18.5 us
    all_to_all x1, waiting for transfers between devices, local(): lax.all_to_all(parts.reshape(SRC, SLOT_ROWS, HS), ('z', 'x'), 0, 0, tiled...  11.5 us
    pallas_call x1, Pallas kernels, local(): pl.pallas_call(attend_kernel, out_shape=jax.ShapeDtypeStruct((SRC * SLOT_...  3.89 us
    all_to_all x1, starting transfers between devices, local(): lax.all_to_all(parts.reshape(SRC, SLOT_ROWS, HS), ('z', 'x'), 0, 0, tiled...  3.87 us
    concatenate x1, local copies, waits for them, and re-layouts, local(): send = jnp.concatenate([keys, values, other, tail], axis=0)  2.15 us
    ppermute x1, starting transfers between devices, local(): got = lax.ppermute(send, 'core', [(0, 1), (1, 0)])  1.92 us
    ppermute x1, waiting for transfers between devices, local(): got = lax.ppermute(send, 'core', [(0, 1), (1, 0)])  1.89 us
  transfers between devices with their start and end apart: 2, of which 2 were waited for; matrix products, arithmetic and copies ran while one was open for 0% of the time, Pallas kernels for 0%

profile of v1, /device:TPU:8, one launch (start us, length us, event | category | flops | bytes accessed | tf_op | source)
XLA Modules:
  0.0 68.4 jit_solution(7817590995961975046)
XLA Ops:
  0.7 0.0 copy-start.2
  0.7 0.1 pad_maximum_fusion.1
  0.8 0.6 copy-done.2
  1.4 0.1 broadcast_in_dim.10
  1.5 2.1 %concatenate.8 = bf16[2080,128]{1,0:T(8,128)(2,1)S(1)} concatenate(bf16[1024,128]{1,0:T(8,128)(2,1)} %key_ref.1, bf16[1024,128]{1,0:T(8,128)(2,1)} %value_ref.1, bf16[16,128]{1,0:T(8,128)(2,1)S(1)} %bitcast.24, bf16[2,128]{1,0:T(2,128)(2,1)S(1)} %broadcast_in_dim.10, bf16[14,128]{1,0:T(8,128)(2,1)S(1)} %broadcast_in_dim.11), dimensions={0} | concatenate | bytes 1064960 | tf_op jit(solution)/shard_map/pair_exchange/concatenate | solution.py:109
  3.6 1.9 %collective-permute-start = (bf16[2080,128]{1,0:T(8,128)(2,1)S(1)}, bf16[2080,128]{1,0:T(8,128)(2,1)S(1)}, u32[]{:S(2)}, u32[]{:S(2)}) collective-permute-start(bf16[2080,128]{1,0:T(8,128)(2,1)S(1)} %concatenate.8), channel_id=1, source_target_pairs={{0,8},{8,0},{1,9},{9,1},{2,10},{10,2},{3,11},{11,3},{4,12},{12,4},... | collective-permute-start | bytes 1597448 | tf_op jit(solution)/shard_map/pair_exchange/ppermute | solution.py:110
  5.6 1.9 %collective-permute-done.got_ref = bf16[2080,128]{1,0:T(8,128)(2,1)S(1)} collective-permute-done((bf16[2080,128]{1,0:T(8,128)(2,1)S(1)}, bf16[2080,128]{1,0:T(8,128)(2,1)S(1)}, u32[]{:S(2)}, u32[]{:S(2)}) %collective-permute-start) | collective-permute-done | bytes 532512 | tf_op jit(solution)/shard_map/pair_exchange/ppermute | solution.py:110
  7.5 18.5 %all_to_all.15 = bf16[8,32,128]{2,1,0:T(8,128)(2,1)S(1)} all-to-all(bf16[8,32,128]{2,1,0:T(8,128)(2,1)S(1)} %broadcast_in_dim.25), channel_id=1, replica_groups=mesh['z'=8,'x'=4,'core'=2,'tp'=8] {'z'}, dimensions={0} | all-to-all | bytes 131072 | tf_op jit(solution)/shard_map/query_spread/all_to_all | solution.py:116
  26.0 0.0 copy-start
  26.0 0.0 copy-start.1
  26.0 21.3 %all_to_all.16 = bf16[32,32,128]{2,1,0:T(8,128)(2,1)S(1)} all-to-all(bf16[32,32,128]{2,1,0:T(8,128)(2,1)S(1)} %bitcast.20), channel_id=1, replica_groups=mesh['z'=8,'x'=4,'core'=2,'tp'=8] {'x','tp'}, dimensions={0} | all-to-all | bytes 524288 | tf_op jit(solution)/shard_map/query_spread/all_to_all | solution.py:120
  47.3 0.0 copy-done
  47.3 0.0 copy-done.1
  47.3 3.9 %attend.1 = bf16[1280,128]{1,0:T(8,128)(2,1)} custom-call(s32[1]{0:T(128)} %copy.10.count_ref, bf16[4,8,32,128]{3,2,1,0:T(8,128)(2,1)S(1)} %bitcast.19, bf16[1024,128]{1,0:T(8,128)(2,1)S(1)} %copy-done, bf16[1024,128]{1,0:T(8,128)(2,1)S(1)} %copy-done.1, bf16[2080,128]{1,0:T(8,128)(2,1)S(1)} %collective-permute-done.got_ref), custom_call_target="tpu_custom_call" | custom-call | tf_op jit(solution)/shard_map/attend/pallas_call | solution.py:125
  51.2 3.9 %all-to-all-start.2 = ((bf16[32,40,128]{2,1,0:T(8,128)(2,1)}), bf16[32,40,128]{2,1,0:T(8,128)(2,1)S(1)}, u32[]{:S(2)}, u32[]{:S(2)}) async-start(bf16[32,40,128]{2,1,0:T(8,128)(2,1)} %bitcast.12), calls=%async_computation.2 | async-start | bytes 655360 | tf_op jit(solution)/shard_map/merge/all_to_all | solution.py:134
  55.8 11.5 %all-to-all-done.2 = bf16[32,40,128]{2,1,0:T(8,128)(2,1)S(1)} async-done(((bf16[32,40,128]{2,1,0:T(8,128)(2,1)}), bf16[32,40,128]{2,1,0:T(8,128)(2,1)S(1)}, u32[]{:S(2)}, u32[]{:S(2)}) %all-to-all-start.2) | async-done | bytes 327712 | tf_op jit(solution)/shard_map/merge/all_to_all | solution.py:134
  67.3 1.1 %merge.1 = bf16[4,1024]{1,0:T(4,128)(2,1)} custom-call(s32[1]{0:T(128)S(6)} %sub.11.live_ref, bf16[1280,128]{1,0:T(8,128)(2,1)S(1)} %bitcast.18), custom_call_target="tpu_custom_call" | custom-call | tf_op jit(solution)/shard_map/merge/pallas_call | solution.py:139
  (7 shorter events, 0.1 us)
Async XLA Ops:
  0.7 0.7 %copy-start.2 = (bf16[32,128]{1,0:T(8,128)(2,1)S(1)}, bf16[32,128]{1,0:T(8,128)(2,1)}, u32[]{:S(2)}) copy-start(bf16[32,128]{1,0:T(8,128)(2,1)} %param.5) | copy-start | bytes 24580
  3.6 3.8 %collective-permute-start = (bf16[2080,128]{1,0:T(8,128)(2,1)S(1)}, bf16[2080,128]{1,0:T(8,128)(2,1)S(1)}, u32[]{:S(2)}, u32[]{:S(2)}) collective-permute-start(bf16[2080,128]{1,0:T(8,128)(2,1)S(1)} %concatenate.8), channel_id=1, source_target_pairs={{0,8},{8,0},{1,9},{9,1},{2,10},{10,2},{3,11},{11,3},{4,12},{12,4},... | collective-permute-start | bytes 1597448 | tf_op jit(solution)/shard_map/pair_exchange/ppermute | solution.py:110
  26.0 21.3 %copy-start = (bf16[1024,128]{1,0:T(8,128)(2,1)S(1)}, bf16[1024,128]{1,0:T(8,128)(2,1)}, u32[]{:S(2)}) copy-start(bf16[1024,128]{1,0:T(8,128)(2,1)} %key_ref.1) | copy-start | bytes 786436
  26.0 21.3 %copy-start.1 = (bf16[1024,128]{1,0:T(8,128)(2,1)S(1)}, bf16[1024,128]{1,0:T(8,128)(2,1)}, u32[]{:S(2)}) copy-start(bf16[1024,128]{1,0:T(8,128)(2,1)} %value_ref.1) | copy-start | bytes 786436
  51.2 16.0 %all-to-all-start.2 = ((bf16[32,40,128]{2,1,0:T(8,128)(2,1)}), bf16[32,40,128]{2,1,0:T(8,128)(2,1)S(1)}, u32[]{:S(2)}, u32[]{:S(2)}) async-start(bf16[32,40,128]{2,1,0:T(8,128)(2,1)} %bitcast.12), calls=%async_computation.2 | async-start | bytes 655360 | tf_op jit(solution)/shard_map/merge/all_to_all | solution.py:134

commit v2 on v1

v2 whole, which is shorter than its diff:
```python
import jax
import jax.numpy as jnp
from jax import lax
from jax.experimental import pallas as pl
from jax.experimental.pallas import tpu as pltpu
from jax.sharding import Mesh, PartitionSpec as P

HS = 128
LOG2E = 1.4426950408889634
EXP2_SCALE = LOG2E / HS**0.5
NZ, NX, NC, NY = 8, 4, 2, 8
SLOTS = 1024
SRC = NZ * NX
PAIRS = 32
SLOT_ROWS = 40
SEND_ROWS = 2 * SLOTS + 16
COUNT_BASE = 64
MASKED = -1e30


def lane_ids(shape):
    return lax.broadcasted_iota(jnp.int32, shape, len(shape) - 1)


def interleave(first, second):
    low = jnp.concatenate([first[:, :4], second[:, :4]], axis=1)
    high = jnp.concatenate([first[:, 4:], second[:, 4:]], axis=1)
    return low, high


def pack_kernel(count_ref, query_ref, key_ref, value_ref, send_ref, slots_ref, rows_ref, sems):
    copies = [
        pltpu.make_async_copy(query_ref, rows_ref, sems.at[2]),
        pltpu.make_async_copy(key_ref, send_ref.at[pl.ds(0, SLOTS)], sems.at[0]),
        pltpu.make_async_copy(value_ref, send_ref.at[pl.ds(SLOTS, SLOTS)], sems.at[1]),
    ]
    for copy in copies:
        copy.start()
    count = count_ref[0]
    high = count // COUNT_BASE
    row = lax.broadcasted_iota(jnp.int32, (16, HS), 0)
    tail = jnp.where(row == 0, high, count - high * COUNT_BASE)
    send_ref[2 * SLOTS : SEND_ROWS, :] = tail.astype(jnp.float32).astype(jnp.bfloat16)
    copies[0].wait()
    rows = rows_ref[...].astype(jnp.float32).reshape(2, 2, 8, HS)
    for core, half in enumerate(interleave(rows[:, 0], rows[:, 1])):
        half = half.reshape(16, HS).astype(jnp.bfloat16)
        for z in range(NZ):
            slots_ref[z, core] = half
    for copy in copies[1:]:
        copy.wait()


def attend_kernel(count_ref, q_ref, key_ref, value_ref, got_ref, out_ref, wide_ref):
    ones = jnp.ones((SLOTS, HS), jnp.bfloat16)
    for block, rows in enumerate((value_ref[...], got_ref[SLOTS : 2 * SLOTS, :])):
        wide_ref[block, :, :HS] = rows
        wide_ref[block, :, HS:] = ones
    slot = lane_ids((1, SLOTS))
    tail = got_ref[2 * SLOTS : SEND_ROWS, :].astype(jnp.float32)
    got_count = tail[0:1] * COUNT_BASE + tail[1:2]
    got_count = jnp.concatenate([got_count] * (SLOTS // HS), axis=1).astype(jnp.int32)
    biases = (
        jnp.where(slot < count_ref[0], 0.0, MASKED),
        jnp.where(slot < got_count, 0.0, MASKED),
    )

    tile = 2 * NX * PAIRS
    part = lane_ids((tile, HS)) // PAIRS
    pair = lax.broadcasted_iota(jnp.int32, (8, PAIRS, HS), 1)
    lane = lane_ids((8, PAIRS, HS))
    diagonal = (lane % PAIRS == pair) & (lane < 3 * PAIRS)
    sub = lax.broadcasted_iota(jnp.int32, (8, 8, HS), 1)

    def by_slot(x):
        x = x.reshape(NX * 2, 2, 2, 8, HS)
        low, high = interleave(x[:, 0].reshape(-1, 8, HS), x[:, 1].reshape(-1, 8, HS))
        x = jnp.stack([low, high], axis=1).reshape(NX, 8, 8, HS)
        return jnp.swapaxes(x, 0, 1).reshape(8, PAIRS, HS)

    for step in range(NY // 2):
        q = q_ref[:, 2 * step : 2 * step + 2].reshape(tile, HS)
        found = []
        for block in range(2):
            keys = key_ref[...] if block == 0 else got_ref[:SLOTS, :]
            scores = lax.dot_general(
                q, keys, (((1,), (1,)), ((), ())), preferred_element_type=jnp.float32
            )
            scores = scores + biases[block]
            peak = jnp.max(scores, axis=1, keepdims=True)
            weights = jnp.exp2((scores - peak) * EXP2_SCALE).astype(jnp.bfloat16)
            both = jnp.dot(weights, wide_ref[block], preferred_element_type=jnp.float32)
            found.append((both[:, :HS], both[:, HS:], peak))
        (out0, sum0, peak0), (out1, sum1, peak1) = found
        ref = jnp.maximum(peak0, peak1).astype(jnp.bfloat16).astype(jnp.float32)
        scale0 = jnp.exp2((peak0 - ref) * EXP2_SCALE)
        scale1 = jnp.exp2((peak1 - ref) * EXP2_SCALE)
        out = by_slot(out0 * scale0 + out1 * scale1)
        total = sum0 * scale0 + sum1 * scale1
        high = total.astype(jnp.bfloat16).astype(jnp.float32)
        stats = jnp.where(part == 0, ref, jnp.where(part == 1, high, total - high))
        stats = jnp.where(diagonal, by_slot(stats), 0.0)
        stats = jnp.sum(stats, axis=1, keepdims=True)
        stats = jnp.where(sub == 0, stats, 0.0)
        full = jnp.concatenate([out, stats], axis=1).reshape(8 * SLOT_ROWS, HS)
        out_ref[8 * SLOT_ROWS * step : 8 * SLOT_ROWS * (step + 1), :] = full.astype(jnp.bfloat16)


def merge_kernel(resp_ref, parts_ref, out_ref):
    parts = parts_ref[...].astype(jnp.float32).reshape(SRC, SLOT_ROWS, HS)
    stats = parts[:, PAIRS, :]
    stats = jnp.concatenate([stats, jnp.zeros((HS - SRC, HS), jnp.float32)], axis=0).T
    valid = lane_ids((PAIRS, HS)) < SRC
    peaks = jnp.where(valid, stats[:PAIRS], -jnp.inf)
    sums = stats[PAIRS : 2 * PAIRS] + stats[2 * PAIRS : 3 * PAIRS]
    peak = jnp.max(peaks, axis=1, keepdims=True)
    scale = jnp.exp2((peaks - peak) * EXP2_SCALE)
    denom = jnp.sum(scale * sums, axis=1, keepdims=True)
    numer = parts[0, :PAIRS] * scale[:, 0:1]
    for src in range(1, SRC):
        numer = numer + parts[src, :PAIRS] * scale[:, src : src + 1]
    result = numer / denom
    rows = PAIRS // 8
    row = lax.broadcasted_iota(jnp.int32, (rows, HS), 0)
    live = row < resp_ref[0] - rows * lax.axis_index(("z", "x", "core"))
    for head in range(8):
        block = result[rows * head : rows * (head + 1)]
        out_ref[:, HS * head : HS * (head + 1)] = jnp.where(live, block, 0.0).astype(jnp.bfloat16)


VMEM = pl.BlockSpec(memory_space=pltpu.VMEM)
SMEM = pl.BlockSpec(memory_space=pltpu.SMEM)
HBM = pl.BlockSpec(memory_space=pltpu.HBM)


def pack(counts, queries, keys, values):
    return pl.pallas_call(
        pack_kernel,
        out_shape=(
            jax.ShapeDtypeStruct((SEND_ROWS, HS), jnp.bfloat16),
            jax.ShapeDtypeStruct((NZ, NC, 16, HS), jnp.bfloat16),
        ),
        in_specs=[SMEM, HBM, HBM, HBM],
        out_specs=(VMEM, VMEM),
        scratch_shapes=[pltpu.VMEM((PAIRS, HS), jnp.bfloat16), pltpu.SemaphoreType.DMA((3,))],
        compiler_params=pltpu.CompilerParams(vmem_limit_bytes=4 * 2**20),
    )(counts, queries, keys, values)


def attend(counts, spread, keys, values, got):
    return pl.pallas_call(
        attend_kernel,
        out_shape=jax.ShapeDtypeStruct((SRC * SLOT_ROWS, HS), jnp.bfloat16),
        in_specs=[SMEM, VMEM, VMEM, VMEM, VMEM],
        out_specs=VMEM,
        scratch_shapes=[pltpu.VMEM((2, SLOTS, 2 * HS), jnp.bfloat16)],
        compiler_params=pltpu.CompilerParams(vmem_limit_bytes=12 * 2**20),
    )(counts, spread, keys, values, got)


def merge(resp_len, parts):
    return pl.pallas_call(
        merge_kernel,
        out_shape=jax.ShapeDtypeStruct((4, 8 * HS), jnp.bfloat16),
        in_specs=[SMEM, VMEM],
        out_specs=VMEM,
        compiler_params=pltpu.CompilerParams(vmem_limit_bytes=4 * 2**20),
    )(resp_len, parts)


def local(queries, keys, values, counts, resp_len):
    with jax.named_scope("pair_exchange"):
        send, slots = pack(counts, queries, keys, values)
        got = lax.ppermute(send, "core", [(0, 1), (1, 0)])
    with jax.named_scope("query_spread"):
        groups = lax.all_to_all(
            slots.reshape(NZ * NC, 16, HS), ("z", "core"), 0, 0, tiled=True
        ).reshape(NZ, PAIRS, HS)
        groups = jnp.broadcast_to(groups[None], (NX, NY, PAIRS, HS)).reshape(SRC, PAIRS, HS)
        spread = lax.all_to_all(groups, ("x", "tp"), 0, 0, tiled=True)
        spread = spread.reshape(NX, NY, PAIRS, HS)
    with jax.named_scope("attend"):
        parts = attend(counts, spread, keys, values, got)
    with jax.named_scope("merge"):
        parts = lax.all_to_all(
            parts.reshape(SRC, SLOT_ROWS, HS), ("z", "x"), 0, 0, tiled=True
        ).reshape(SRC * SLOT_ROWS, HS)
        return merge(resp_len, parts)


def solution(mesh):
    grid = Mesh(mesh.devices.reshape(NZ, NX, NC, NY), ("z", "x", "core", "tp"))
    ctx = ("z", "x", "core")
    in_specs = (P("tp", ctx), P(ctx, "tp"), P(ctx, "tp"), P(ctx), P())
    return jax.shard_map(
        local, mesh=grid, in_specs=in_specs, out_specs=P(ctx, "tp"), check_vma=False
    )
```

time: 68.8 us -> 69.5 us (1.010)
  blocking collectives: 39.8 us -> 0 us
  starting transfers between devices: 5.79 us -> 26.9 us
  waiting for transfers between devices: 13.4 us -> 31.7 us
    all_to_all x2 -> x0, blocking collectives: 39.8 us -> none  [the longest x1 21.3 us: local(): spread = lax.all_to_all(groups, ('x', 'tp'), 0, 0, tiled=True)]
    all_to_all x0 -> x2, starting transfers between devices: none -> 20.7 us  [the longest x1 10.4 us: local(): lax.all_to_all(slots.reshape(NZ * NC, 16, HS), ('z', 'core'), 0, 0, tiled...]
    all_to_all x0 -> x2, waiting for transfers between devices: none -> 18.3 us  [the longest x1 12.8 us: local(): spread = lax.all_to_all(groups, ('x', 'tp'), 0, 0, tiled=True)]
    concatenate x1 -> x0, local copies, waits for them, and re-layouts: 2.15 us -> none  [local(): send = jnp.concatenate([keys, values, other, tail], axis=0)]
    unnamed x6 -> x10, local copies, waits for them, and re-layouts: 0.62 us -> 2.6 us
    ppermute x1, waiting for transfers between devices: 1.89 us -> 0.01 us  [local(): got = lax.ppermute(send, 'core', [(0, 1), (1, 0)])]
    all_to_all x1, waiting for transfers between devices: 11.5 us -> 13.3 us  [local(): lax.all_to_all(parts.reshape(SRC, SLOT_ROWS, HS), ('z', 'x'), 0, 0, tiled...]
    broadcast_in_dim x1, local copies, waits for them, and re-layouts: 0.03 us -> 0.74 us  [local(): jnp.broadcast_to(groups[None], (NX, NY, PAIRS, HS)).reshape(SRC, PAIRS, HS)]
  transfers between devices with their start and end apart: 2 -> 4, of which waited for: 2 -> 3; matrix products, arithmetic and copies ran while one was open for 0% -> 1% of each run, Pallas kernels for 0% -> 0%
where the time goes in v2:
time: 69.5 us; the launch traced here: 69 us
  waiting for transfers between devices  31.7 us (46%)
  starting transfers between devices  26.9 us (39%)
  Pallas kernels  5.71 us (8%)
  local copies, waits for them, and re-layouts  3.34 us (5%)
  between operations  1.36 us (2%)
    all_to_all x1, waiting for transfers between devices, local(): lax.all_to_all(parts.reshape(SRC, SLOT_ROWS, HS), ('z', 'x'), 0, 0, tiled...  13.3 us
    all_to_all x1, waiting for transfers between devices, local(): spread = lax.all_to_all(groups, ('x', 'tp'), 0, 0, tiled=True)  12.8 us
    all_to_all x1, starting transfers between devices, local(): lax.all_to_all(slots.reshape(NZ * NC, 16, HS), ('z', 'core'), 0, 0, tiled...  10.4 us
    all_to_all x1, starting transfers between devices, local(): spread = lax.all_to_all(groups, ('x', 'tp'), 0, 0, tiled=True)  10.3 us
    all_to_all x1, waiting for transfers between devices, local(): lax.all_to_all(slots.reshape(NZ * NC, 16, HS), ('z', 'core'), 0, 0, tiled...  5.56 us
    all_to_all x1, starting transfers between devices, local(): lax.all_to_all(parts.reshape(SRC, SLOT_ROWS, HS), ('z', 'x'), 0, 0, tiled...  3.88 us
    pallas_call x1, Pallas kernels, attend(): pl.pallas_call(attend_kernel, out_shape=jax.ShapeDtypeStruct((SRC * SLOT_...  3.86 us
    unnamed x10, local copies, waits for them, and re-layouts  2.6 us
  transfers between devices with their start and end apart: 4, of which 3 were waited for; matrix products, arithmetic and copies ran while one was open for 1% of the time, Pallas kernels for 0%

profile of v2, /device:TPU:8, one launch (start us, length us, event | category | flops | bytes accessed | tf_op | source)
XLA Modules:
  0.0 69.0 jit_solution(12684849869420129098)
XLA Ops:
  0.7 0.0 copy-start
  0.7 0.9 %copy-done = bf16[1024,128]{1,0:T(8,128)(2,1)S(1)} copy-done((bf16[1024,128]{1,0:T(8,128)(2,1)S(1)}, bf16[1024,128]{1,0:T(8,128)(2,1)}, u32[]{:S(2)}) %copy-start) | copy-done | bytes 262168
  1.6 0.0 copy-start.2
  1.6 0.9 %copy-done.2 = bf16[1024,128]{1,0:T(8,128)(2,1)S(1)} copy-done((bf16[1024,128]{1,0:T(8,128)(2,1)S(1)}, bf16[1024,128]{1,0:T(8,128)(2,1)}, u32[]{:S(2)}) %copy-start.2) | copy-done | bytes 262168
  2.6 0.0 copy-start.4
  2.6 0.7 %copy-done.4 = bf16[32,128]{1,0:T(8,128)(2,1)S(1)} copy-done((bf16[32,128]{1,0:T(8,128)(2,1)S(1)}, bf16[32,128]{1,0:T(8,128)(2,1)}, u32[]{:S(2)}) %copy-start.4) | copy-done | bytes 8216
  3.3 0.7 %pair_exchange.1 = (bf16[2064,128]{1,0:T(8,128)(2,1)S(1)}, bf16[8,2,16,128]{3,2,1,0:T(8,128)(2,1)}) custom-call(s32[1]{0:T(128)S(6)} %copy.6.count_ref, bf16[32,128]{1,0:T(8,128)(2,1)S(1)} %copy-done.4, bf16[1024,128]{1,0:T(8,128)(2,1)S(1)} %copy-done, bf16[1024,128]{1,0:T(8,128)(2,1)S(1)} %copy-done.2), custom_call_target="tpu_custom_call" | custom-call | tf_op jit(solution)/shard_map/pair_exchange/pallas_call | solution.py:137
  4.0 10.4 %all-to-all-start = ((bf16[16,16,128]{2,1,0:T(8,128)(2,1)}), bf16[16,16,128]{2,1,0:T(8,128)(2,1)S(1)}, u32[]{:S(2)}, u32[]{:S(2)}) async-start(bf16[16,16,128]{2,1,0:T(8,128)(2,1)} %bitcast), calls=%async_computation | async-start | bytes 131072 | tf_op jit(solution)/shard_map/query_spread/all_to_all | solution.py:176
  14.4 2.3 %collective-permute-start = (bf16[2064,128]{1,0:T(8,128)(2,1)S(1)}, bf16[2064,128]{1,0:T(8,128)(2,1)S(1)}, u32[]{:S(2)}, u32[]{:S(2)}) collective-permute-start(bf16[2064,128]{1,0:T(8,128)(2,1)S(1)} %get-tuple-element.8), channel_id=1, source_target_pairs={{0,8},{8,0},{1,9},{9,1},{2,10},{10,2},{3,11},{11,3},{4,12},{12,4},... | collective-permute-start | bytes 1585160 | tf_op jit(solution)/shard_map/pair_exchange/ppermute | solution.py:174
  16.7 5.6 %all-to-all-done = bf16[16,16,128]{2,1,0:T(8,128)(2,1)S(1)} async-done(((bf16[16,16,128]{2,1,0:T(8,128)(2,1)}), bf16[16,16,128]{2,1,0:T(8,128)(2,1)S(1)}, u32[]{:S(2)}, u32[]{:S(2)}) %all-to-all-start) | async-done | bytes 65568 | tf_op jit(solution)/shard_map/query_spread/all_to_all | solution.py:176
  22.3 0.7 %broadcast_in_dim.8 = bf16[4,8,32,128]{3,2,1,0:T(8,128)(2,1)} broadcast(bf16[8,32,128]{2,1,0:T(8,128)(2,1)S(1)} %bitcast.8), dimensions={1,2,3} | broadcast | bytes 327680 | tf_op jit(solution)/shard_map/query_spread/broadcast_in_dim | solution.py:179
  23.0 0.0 copy-start.1
  23.0 0.0 copy-start.3
  23.0 10.3 %all-to-all-start.1 = ((bf16[32,32,128]{2,1,0:T(8,128)(2,1)}), bf16[32,32,128]{2,1,0:T(8,128)(2,1)S(1)}, u32[]{:S(2)}, u32[]{:S(2)}) async-start(bf16[32,32,128]{2,1,0:T(8,128)(2,1)} %bitcast.2), calls=%async_computation.1 | async-start | bytes 524288 | tf_op jit(solution)/shard_map/query_spread/all_to_all | solution.py:180
  33.3 0.0 collective-permute-done.got_ref
  33.4 12.8 %all-to-all-done.1 = bf16[32,32,128]{2,1,0:T(8,128)(2,1)S(1)} async-done(((bf16[32,32,128]{2,1,0:T(8,128)(2,1)}), bf16[32,32,128]{2,1,0:T(8,128)(2,1)S(1)}, u32[]{:S(2)}, u32[]{:S(2)}) %all-to-all-start.1) | async-done | bytes 262176 | tf_op jit(solution)/shard_map/query_spread/all_to_all | solution.py:180
  46.1 0.0 copy-done.1
  46.1 0.0 copy-done.3
  46.1 3.9 %attend.1 = bf16[1280,128]{1,0:T(8,128)(2,1)} custom-call(s32[1]{0:T(128)S(6)} %copy.6.count_ref, bf16[4,8,32,128]{3,2,1,0:T(8,128)(2,1)S(1)} %bitcast.7, bf16[1024,128]{1,0:T(8,128)(2,1)S(1)} %copy-done.1, bf16[1024,128]{1,0:T(8,128)(2,1)S(1)} %copy-done.3, bf16[2064,128]{1,0:T(8,128)(2,1)S(1)} %collective-permute-done.got_ref), custom_call_target="tpu_custom_call" | custom-call | tf_op jit(solution)/shard_map/attend/pallas_call | solution.py:151
  50.0 3.9 %all-to-all-start.2 = ((bf16[32,40,128]{2,1,0:T(8,128)(2,1)}), bf16[32,40,128]{2,1,0:T(8,128)(2,1)S(1)}, u32[]{:S(2)}, u32[]{:S(2)}) async-start(bf16[32,40,128]{2,1,0:T(8,128)(2,1)} %bitcast.4), calls=%async_computation.2 | async-start | bytes 655360 | tf_op jit(solution)/shard_map/merge/all_to_all | solution.py:185
  54.5 13.3 %all-to-all-done.2 = bf16[32,40,128]{2,1,0:T(8,128)(2,1)S(1)} async-done(((bf16[32,40,128]{2,1,0:T(8,128)(2,1)}), bf16[32,40,128]{2,1,0:T(8,128)(2,1)S(1)}, u32[]{:S(2)}, u32[]{:S(2)}) %all-to-all-start.2) | async-done | bytes 327712 | tf_op jit(solution)/shard_map/merge/all_to_all | solution.py:185
  67.9 1.1 %merge.1 = bf16[4,1024]{1,0:T(4,128)(2,1)} custom-call(s32[1]{0:T(128)S(6)} %copy.7.resp_ref, bf16[1280,128]{1,0:T(8,128)(2,1)S(1)} %bitcast.6), custom_call_target="tpu_custom_call" | custom-call | tf_op jit(solution)/shard_map/merge/pallas_call | solution.py:162
Async XLA Ops:
  0.7 1.0 %copy-start = (bf16[1024,128]{1,0:T(8,128)(2,1)S(1)}, bf16[1024,128]{1,0:T(8,128)(2,1)}, u32[]{:S(2)}) copy-start(bf16[1024,128]{1,0:T(8,128)(2,1)} %key_ref.3) | copy-start | bytes 786436
  1.6 0.9 %copy-start.2 = (bf16[1024,128]{1,0:T(8,128)(2,1)S(1)}, bf16[1024,128]{1,0:T(8,128)(2,1)}, u32[]{:S(2)}) copy-start(bf16[1024,128]{1,0:T(8,128)(2,1)} %value_ref.3) | copy-start | bytes 786436
  2.6 0.7 %copy-start.4 = (bf16[32,128]{1,0:T(8,128)(2,1)S(1)}, bf16[32,128]{1,0:T(8,128)(2,1)}, u32[]{:S(2)}) copy-start(bf16[32,128]{1,0:T(8,128)(2,1)} %query_ref.1) | copy-start | bytes 24580
  4.0 18.3 %all-to-all-start = ((bf16[16,16,128]{2,1,0:T(8,128)(2,1)}), bf16[16,16,128]{2,1,0:T(8,128)(2,1)S(1)}, u32[]{:S(2)}, u32[]{:S(2)}) async-start(bf16[16,16,128]{2,1,0:T(8,128)(2,1)} %bitcast), calls=%async_computation | async-start | bytes 131072 | tf_op jit(solution)/shard_map/query_spread/all_to_all | solution.py:176
  14.4 18.9 %collective-permute-start = (bf16[2064,128]{1,0:T(8,128)(2,1)S(1)}, bf16[2064,128]{1,0:T(8,128)(2,1)S(1)}, u32[]{:S(2)}, u32[]{:S(2)}) collective-permute-start(bf16[2064,128]{1,0:T(8,128)(2,1)S(1)} %get-tuple-element.8), channel_id=1, source_target_pairs={{0,8},{8,0},{1,9},{9,1},{2,10},{10,2},{3,11},{11,3},{4,12},{12,4},... | collective-permute-start | bytes 1585160 | tf_op jit(solution)/shard_map/pair_exchange/ppermute | solution.py:174
  23.0 23.1 %copy-start.1 = (bf16[1024,128]{1,0:T(8,128)(2,1)S(1)}, bf16[1024,128]{1,0:T(8,128)(2,1)}, u32[]{:S(2)}) copy-start(bf16[1024,128]{1,0:T(8,128)(2,1)} %key_ref.3) | copy-start | bytes 786436
  23.0 23.1 %copy-start.3 = (bf16[1024,128]{1,0:T(8,128)(2,1)S(1)}, bf16[1024,128]{1,0:T(8,128)(2,1)}, u32[]{:S(2)}) copy-start(bf16[1024,128]{1,0:T(8,128)(2,1)} %value_ref.3) | copy-start | bytes 786436
  23.0 23.1 %all-to-all-start.1 = ((bf16[32,32,128]{2,1,0:T(8,128)(2,1)}), bf16[32,32,128]{2,1,0:T(8,128)(2,1)S(1)}, u32[]{:S(2)}, u32[]{:S(2)}) async-start(bf16[32,32,128]{2,1,0:T(8,128)(2,1)} %bitcast.2), calls=%async_computation.1 | async-start | bytes 524288 | tf_op jit(solution)/shard_map/query_spread/all_to_all | solution.py:180
  50.0 17.9 %all-to-all-start.2 = ((bf16[32,40,128]{2,1,0:T(8,128)(2,1)}), bf16[32,40,128]{2,1,0:T(8,128)(2,1)S(1)}, u32[]{:S(2)}, u32[]{:S(2)}) async-start(bf16[32,40,128]{2,1,0:T(8,128)(2,1)} %bitcast.4), calls=%async_computation.2 | async-start | bytes 655360 | tf_op jit(solution)/shard_map/merge/all_to_all | solution.py:185

commit v3 on v2

v3 whole, which is shorter than its diff:
```python
import jax
import jax.numpy as jnp
from jax import lax
from jax.experimental import pallas as pl
from jax.experimental.pallas import tpu as pltpu
from jax.sharding import Mesh, PartitionSpec as P

HS = 128
LOG2E = 1.4426950408889634
EXP2_SCALE = LOG2E / HS**0.5
NZ, NX, NC, NY = 8, 4, 2, 8
SLOTS = 1024
SRC = NZ * NX
PAIRS = 32
SLOT_ROWS = 40
SEND_ROWS = 2 * SLOTS + 16
COUNT_BASE = 64
MASKED = -1e30


def lane_ids(shape):
    return lax.broadcasted_iota(jnp.int32, shape, len(shape) - 1)


def interleave(first, second):
    low = jnp.concatenate([first[:, :4], second[:, :4]], axis=1)
    high = jnp.concatenate([first[:, 4:], second[:, 4:]], axis=1)
    return low, high


def pack_kernel(query_ref, key_ref, value_ref, count_ref, resp_ref, slots_ref, send_ref):
    rows = query_ref[...].astype(jnp.float32).reshape(2, 2, 8, HS)
    for core, half in enumerate(interleave(rows[:, 0], rows[:, 1])):
        half = half.reshape(16, HS).astype(jnp.bfloat16)
        for z in range(NZ):
            slots_ref[z, core] = half
    count = count_ref[...]
    row = lax.broadcasted_iota(jnp.int32, (16, HS), 0)
    high = count // COUNT_BASE
    tail = jnp.where(row == 0, high, jnp.where(row == 1, count - high * COUNT_BASE, resp_ref[...]))
    send_ref[:SLOTS, :] = key_ref[...]
    send_ref[SLOTS : 2 * SLOTS, :] = value_ref[...]
    send_ref[2 * SLOTS : SEND_ROWS, :] = tail.astype(jnp.float32).astype(jnp.bfloat16)


def widen_kernel(own_ref, _, wide_ref):
    wide_ref[:, :HS] = own_ref[SLOTS : 2 * SLOTS, :]
    wide_ref[:, HS:] = jnp.ones((SLOTS, HS), jnp.bfloat16)


def attend_kernel(q_ref, own_ref, own_wide_ref, got_ref, out_ref, wide_ref):
    wide_ref[:, :HS] = got_ref[SLOTS : 2 * SLOTS, :]
    wide_ref[:, HS:] = jnp.ones((SLOTS, HS), jnp.bfloat16)
    slot = lane_ids((1, SLOTS))
    biases = []
    for ref in (own_ref, got_ref):
        tail = ref[2 * SLOTS : SEND_ROWS, :].astype(jnp.float32)
        count = tail[0:1] * COUNT_BASE + tail[1:2]
        count = jnp.concatenate([count] * (SLOTS // HS), axis=1).astype(jnp.int32)
        biases.append(jnp.where(slot < count, 0.0, MASKED))
    resp = tail[2:3]

    tile = 2 * NX * PAIRS
    part = lane_ids((tile, HS)) // PAIRS
    pair = lax.broadcasted_iota(jnp.int32, (8, PAIRS, HS), 1)
    lane = lane_ids((8, PAIRS, HS))
    diagonal = lane % PAIRS == pair
    sub = lax.broadcasted_iota(jnp.int32, (8, 8, HS), 1)

    def by_slot(x):
        x = x.reshape(NX * 2, 2, 2, 8, HS)
        low, high = interleave(x[:, 0].reshape(-1, 8, HS), x[:, 1].reshape(-1, 8, HS))
        x = jnp.stack([low, high], axis=1).reshape(NX, 8, 8, HS)
        return jnp.swapaxes(x, 0, 1).reshape(8, PAIRS, HS)

    for step in range(NY // 2):
        q = q_ref[:, 2 * step : 2 * step + 2].reshape(tile, HS)
        found = []
        for block, (keys_ref, values_ref) in enumerate(((own_ref, own_wide_ref), (got_ref, wide_ref))):
            keys = keys_ref[:SLOTS, :]
            scores = lax.dot_general(
                q, keys, (((1,), (1,)), ((), ())), preferred_element_type=jnp.float32
            )
            scores = scores + biases[block]
            peak = jnp.max(scores, axis=1, keepdims=True)
            weights = jnp.exp2((scores - peak) * EXP2_SCALE).astype(jnp.bfloat16)
            both = jnp.dot(weights, values_ref[...], preferred_element_type=jnp.float32)
            found.append((both[:, :HS], both[:, HS:], peak))
        (out0, sum0, peak0), (out1, sum1, peak1) = found
        ref = jnp.maximum(peak0, peak1).astype(jnp.bfloat16).astype(jnp.float32)
        scale0 = jnp.exp2((peak0 - ref) * EXP2_SCALE)
        scale1 = jnp.exp2((peak1 - ref) * EXP2_SCALE)
        out = by_slot(out0 * scale0 + out1 * scale1)
        total = sum0 * scale0 + sum1 * scale1
        high = total.astype(jnp.bfloat16).astype(jnp.float32)
        stats = jnp.where(part == 1, high, jnp.where(part == 2, total - high, resp))
        stats = jnp.where(part == 0, ref, stats)
        stats = jnp.where(diagonal, by_slot(stats), 0.0)
        stats = jnp.sum(stats, axis=1, keepdims=True)
        stats = jnp.where(sub == 0, stats, 0.0)
        full = jnp.concatenate([out, stats], axis=1).reshape(8 * SLOT_ROWS, HS)
        out_ref[8 * SLOT_ROWS * step : 8 * SLOT_ROWS * (step + 1), :] = full.astype(jnp.bfloat16)


def merge_kernel(parts_ref, out_ref):
    parts = parts_ref[...].astype(jnp.float32).reshape(SRC, SLOT_ROWS, HS)
    resp = parts[0, PAIRS : PAIRS + 1, 3 * PAIRS : 3 * PAIRS + 1].astype(jnp.int32)
    stats = parts[:, PAIRS, :]
    stats = jnp.concatenate([stats, jnp.zeros((HS - SRC, HS), jnp.float32)], axis=0).T
    valid = lane_ids((PAIRS, HS)) < SRC
    peaks = jnp.where(valid, stats[:PAIRS], -jnp.inf)
    sums = stats[PAIRS : 2 * PAIRS] + stats[2 * PAIRS : 3 * PAIRS]
    peak = jnp.max(peaks, axis=1, keepdims=True)
    scale = jnp.exp2((peaks - peak) * EXP2_SCALE)
    denom = jnp.sum(scale * sums, axis=1, keepdims=True)
    numer = parts[0, :PAIRS] * scale[:, 0:1]
    for src in range(1, SRC):
        numer = numer + parts[src, :PAIRS] * scale[:, src : src + 1]
    result = numer / denom
    rows = PAIRS // 8
    row = lax.broadcasted_iota(jnp.int32, (rows, HS), 0)
    live = row + rows * lax.axis_index(("z", "x", "core")) < resp
    for head in range(8):
        block = result[rows * head : rows * (head + 1)]
        out_ref[:, HS * head : HS * (head + 1)] = jnp.where(live, block, 0.0).astype(jnp.bfloat16)


VMEM = pl.BlockSpec(memory_space=pltpu.VMEM)
HBM = pl.BlockSpec(memory_space=pltpu.HBM)


def pack(queries, keys, values, counts, resp_len):
    return pl.pallas_call(
        pack_kernel,
        out_shape=(
            jax.ShapeDtypeStruct((NZ, NC, 16, HS), jnp.bfloat16),
            jax.ShapeDtypeStruct((SEND_ROWS, HS), jnp.bfloat16),
        ),
        in_specs=[VMEM] * 5,
        out_specs=(VMEM, VMEM),
        compiler_params=pltpu.CompilerParams(vmem_limit_bytes=60 * 2**20),
    )(queries, keys, values, counts.reshape(1, 1), resp_len.reshape(1, 1))


def widen(own, after):
    return pl.pallas_call(
        widen_kernel,
        out_shape=jax.ShapeDtypeStruct((SLOTS, 2 * HS), jnp.bfloat16),
        in_specs=[VMEM, HBM],
        out_specs=VMEM,
        compiler_params=pltpu.CompilerParams(vmem_limit_bytes=2**20),
    )(own, after)


def attend(spread, own, wide, got):
    return pl.pallas_call(
        attend_kernel,
        out_shape=jax.ShapeDtypeStruct((SRC * SLOT_ROWS, HS), jnp.bfloat16),
        in_specs=[VMEM, VMEM, VMEM, VMEM],
        out_specs=VMEM,
        scratch_shapes=[pltpu.VMEM((SLOTS, 2 * HS), jnp.bfloat16)],
        compiler_params=pltpu.CompilerParams(vmem_limit_bytes=12 * 2**20),
    )(spread, own, wide, got)


def merge(parts):
    return pl.pallas_call(
        merge_kernel,
        out_shape=jax.ShapeDtypeStruct((4, 8 * HS), jnp.bfloat16),
        in_specs=[VMEM],
        out_specs=VMEM,
        compiler_params=pltpu.CompilerParams(vmem_limit_bytes=4 * 2**20),
    )(parts)


def local(queries, keys, values, counts, resp_len):
    with jax.named_scope("query_spread"):
        slots, own = pack(queries, keys, values, counts, resp_len)
        halves = slots.reshape(NZ * NC, 16, HS)
        groups = lax.all_to_all(halves, ("z", "core"), 0, 0, tiled=True).reshape(NZ, PAIRS, HS)
    with jax.named_scope("pair_exchange"):
        got = lax.ppermute(own, "core", [(0, 1), (1, 0)])
    groups, own = lax.optimization_barrier((groups, own))
    with jax.named_scope("query_spread"):
        groups = jnp.broadcast_to(groups[None], (NX, NY, PAIRS, HS)).reshape(SRC, PAIRS, HS)
        spread = lax.all_to_all(groups, ("x", "tp"), 0, 0, tiled=True)
        spread = spread.reshape(NX, NY, PAIRS, HS)
    with jax.named_scope("attend"):
        wide = widen(own, spread)
        parts = attend(spread, own, wide, got)
    with jax.named_scope("merge"):
        parts = lax.all_to_all(
            parts.reshape(SRC, SLOT_ROWS, HS), ("z", "x"), 0, 0, tiled=True
        ).reshape(SRC * SLOT_ROWS, HS)
        return merge(parts)


def solution(mesh):
    grid = Mesh(mesh.devices.reshape(NZ, NX, NC, NY), ("z", "x", "core", "tp"))
    ctx = ("z", "x", "core")
    in_specs = (P("tp", ctx), P(ctx, "tp"), P(ctx, "tp"), P(ctx), P())
    return jax.shard_map(
        local, mesh=grid, in_specs=in_specs, out_specs=P(ctx, "tp"), check_vma=False
    )
```

time: 69.5 us -> 66.3 us (0.954)
  blocking collectives: 0 us -> 39.7 us
  waiting for transfers between devices: 31.7 us -> 5.56 us
  starting transfers between devices: 26.9 us -> 12.9 us
  local copies, waits for them, and re-layouts: 3.34 us -> 0.04 us
  Pallas kernels: 5.71 us -> 6.52 us
    all_to_all x0 -> x2, blocking collectives: none -> 39.7 us  [the longest x1 22.8 us: local(): spread = lax.all_to_all(groups, ('x', 'tp'), 0, 0, tiled=True)]
    all_to_all x3 -> x1, waiting for transfers between devices: 31.7 us -> 5.56 us  [local(): lax.all_to_all(halves, ('z', 'core'), 0, 0, tiled=True)]
    all_to_all x3 -> x1, starting transfers between devices: 24.6 us -> 10.6 us  [local(): lax.all_to_all(halves, ('z', 'core'), 0, 0, tiled=True)]
    unnamed x10 -> x2, local copies, waits for them, and re-layouts: 2.6 us -> 0.01 us
    pallas_call x1 -> x2, Pallas kernels: 0.72 us -> 2 us  [the longest x1 1.93 us: pack(): pl.pallas_call(pack_kernel, out_shape=(jax.ShapeDtypeStruct((NZ, NC, 16,...]
    broadcast_in_dim x1, local copies, waits for them, and re-layouts: 0.74 us -> 0.03 us  [local(): jnp.broadcast_to(groups[None], (NX, NY, PAIRS, HS)).reshape(SRC, PAIRS, HS)]
  transfers between devices with their start and end apart: 4 -> 2, of which waited for: 3 -> 1; matrix products, arithmetic and copies ran while one was open for 1% -> 0% of each run, Pallas kernels for 0% -> 0%
where the time goes in v3:
time: 66.3 us; the launch traced here: 66 us
  blocking collectives  39.7 us (60%)
  starting transfers between devices  12.9 us (19%)
  Pallas kernels  6.52 us (10%)
  waiting for transfers between devices  5.56 us (8%)
  between operations  1.34 us (2%)
    all_to_all x1, blocking collectives, local(): spread = lax.all_to_all(groups, ('x', 'tp'), 0, 0, tiled=True)  22.8 us
    all_to_all x1, blocking collectives, local(): lax.all_to_all(parts.reshape(SRC, SLOT_ROWS, HS), ('z', 'x'), 0, 0, tiled...  17 us
    all_to_all x1, starting transfers between devices, local(): lax.all_to_all(halves, ('z', 'core'), 0, 0, tiled=True)  10.6 us
    all_to_all x1, waiting for transfers between devices, local(): lax.all_to_all(halves, ('z', 'core'), 0, 0, tiled=True)  5.56 us
    pallas_call x1, Pallas kernels, attend(): pl.pallas_call(attend_kernel, out_shape=jax.ShapeDtypeStruct((SRC * SLOT_...  3.37 us
    ppermute x1, starting transfers between devices, local(): got = lax.ppermute(own, 'core', [(0, 1), (1, 0)])  2.31 us
    pallas_call x1, Pallas kernels, pack(): pl.pallas_call(pack_kernel, out_shape=(jax.ShapeDtypeStruct((NZ, NC, 16,...  1.93 us
  transfers between devices with their start and end apart: 2, of which 1 were waited for; matrix products, arithmetic and copies ran while one was open for 0% of the time, Pallas kernels for 0%

profile of v3, /device:TPU:8, one launch (start us, length us, event | category | flops | bytes accessed | tf_op | source)
XLA Modules:
  0.0 66.0 jit_solution(8365540792456034923)
XLA Ops:
  1.3 1.9 %query_spread.1 = (bf16[8,2,16,128]{3,2,1,0:T(8,128)(2,1)}, bf16[2064,128]{1,0:T(8,128)(2,1)}) custom-call(bf16[32,128]{1,0:T(8,128)(2,1)} %query_ref.1, bf16[1024,128]{1,0:T(8,128)(2,1)} %key_ref.1, bf16[1024,128]{1,0:T(8,128)(2,1)} %value_ref.1, s32[1,1]{1,0:T(1,128)} %bitcast.8.count_ref, s32[1,1]{1,0:T(1,128)} %bitcast.9.resp_ref), custom_call_target="tpu_custom_call" | custom-call | tf_op jit(solution)/shard_map/query_spread/pallas_call | solution.py:133
  3.2 0.0 copy-start
  3.2 10.6 %all-to-all-start = ((bf16[16,16,128]{2,1,0:T(8,128)(2,1)}), bf16[16,16,128]{2,1,0:T(8,128)(2,1)S(1)}, u32[]{:S(2)}, u32[]{:S(2)}) async-start(bf16[16,16,128]{2,1,0:T(8,128)(2,1)} %bitcast.16), calls=%async_computation | async-start | bytes 131072 | tf_op jit(solution)/shard_map/query_spread/all_to_all | solution.py:180
  13.8 2.3 %collective-permute-start = (bf16[2064,128]{1,0:T(8,128)(2,1)}, bf16[2064,128]{1,0:T(8,128)(2,1)S(1)}, u32[]{:S(2)}, u32[]{:S(2)}) collective-permute-start(bf16[2064,128]{1,0:T(8,128)(2,1)} %get-tuple-element.12.own_ref), channel_id=1, source_target_pairs={{0,8},{8,0},{1,9},{9,1},{2,10},{10,2},{3,11},{11,3},{4,12},{12,4},... | collective-permute-start | bytes 1585160 | tf_op jit(solution)/shard_map/pair_exchange/ppermute | solution.py:182
  16.1 5.6 %all-to-all-done = bf16[16,16,128]{2,1,0:T(8,128)(2,1)S(1)} async-done(((bf16[16,16,128]{2,1,0:T(8,128)(2,1)}), bf16[16,16,128]{2,1,0:T(8,128)(2,1)S(1)}, u32[]{:S(2)}, u32[]{:S(2)}) %all-to-all-start) | async-done | bytes 65568 | tf_op jit(solution)/shard_map/query_spread/all_to_all | solution.py:180
  21.7 22.8 %all_to_all.15 = bf16[32,32,128]{2,1,0:T(8,128)(2,1)S(1)} all-to-all(bf16[32,32,128]{2,1,0:T(8,128)(2,1)S(1)} %bitcast.14), channel_id=1, replica_groups=mesh['z'=8,'x'=4,'core'=2,'tp'=8] {'x','tp'}, dimensions={0} | all-to-all | bytes 524288 | tf_op jit(solution)/shard_map/query_spread/all_to_all | solution.py:186
  44.5 0.0 copy-done
  44.5 0.1 attend.2.own_wide_ref
  44.5 0.0 collective-permute-done.got_ref
  44.6 3.4 %attend.3 = bf16[1280,128]{1,0:T(8,128)(2,1)S(1)} custom-call(bf16[4,8,32,128]{3,2,1,0:T(8,128)(2,1)S(1)} %bitcast.11, bf16[2064,128]{1,0:T(8,128)(2,1)S(1)} %copy-done, bf16[1024,256]{1,0:T(8,128)(2,1)S(1)} %attend.2.own_wide_ref, bf16[2064,128]{1,0:T(8,128)(2,1)S(1)} %collective-permute-done.got_ref), custom_call_target="tpu_custom_call" | custom-call | tf_op jit(solution)/shard_map/attend/pallas_call | solution.py:156
  47.9 17.0 %all_to_all.16 = bf16[32,40,128]{2,1,0:T(8,128)(2,1)S(1)} all-to-all(bf16[32,40,128]{2,1,0:T(8,128)(2,1)S(1)} %bitcast.13), channel_id=1, replica_groups=mesh['z'=8,'x'=4,'core'=2,'tp'=8] {'z','x'}, dimensions={0} | all-to-all | bytes 655360 | tf_op jit(solution)/shard_map/merge/all_to_all | solution.py:192
  64.9 1.1 %merge.1 = bf16[4,1024]{1,0:T(4,128)(2,1)} custom-call(bf16[1280,128]{1,0:T(8,128)(2,1)S(1)} %bitcast.12), custom_call_target="tpu_custom_call" | custom-call | tf_op jit(solution)/shard_map/merge/pallas_call | solution.py:167
  (1 shorter events, 0.0 us)
Async XLA Ops:
  3.2 41.2 %copy-start = (bf16[2064,128]{1,0:T(8,128)(2,1)S(1)}, bf16[2064,128]{1,0:T(8,128)(2,1)}, u32[]{:S(2)}) copy-start(bf16[2064,128]{1,0:T(8,128)(2,1)} %get-tuple-element.12.own_ref) | copy-start | bytes 1585156
  3.2 18.4 %all-to-all-start = ((bf16[16,16,128]{2,1,0:T(8,128)(2,1)}), bf16[16,16,128]{2,1,0:T(8,128)(2,1)S(1)}, u32[]{:S(2)}, u32[]{:S(2)}) async-start(bf16[16,16,128]{2,1,0:T(8,128)(2,1)} %bitcast.16), calls=%async_computation | async-start | bytes 131072 | tf_op jit(solution)/shard_map/query_spread/all_to_all | solution.py:180
  13.8 30.8 %collective-permute-start = (bf16[2064,128]{1,0:T(8,128)(2,1)}, bf16[2064,128]{1,0:T(8,128)(2,1)S(1)}, u32[]{:S(2)}, u32[]{:S(2)}) collective-permute-start(bf16[2064,128]{1,0:T(8,128)(2,1)} %get-tuple-element.12.own_ref), channel_id=1, source_target_pairs={{0,8},{8,0},{1,9},{9,1},{2,10},{10,2},{3,11},{11,3},{4,12},{12,4},... | collective-permute-start | bytes 1585160 | tf_op jit(solution)/shard_map/pair_exchange/ppermute | solution.py:182

commit v4 on v3

--- a/solution.py
+++ b/solution.py
@@ -15,11 +15,45 @@
 SLOT_ROWS = 40
 SEND_ROWS = 2 * SLOTS + 16
 COUNT_BASE = 64
+FIRST_X, FIRST_YZ = 2, 4
 MASKED = -1e30
 
 
 def lane_ids(shape):
     return lax.broadcasted_iota(jnp.int32, shape, len(shape) - 1)
+
+
+def device(z, x, core, y):
+    return ((z % NZ * NX + x % NX) * NC + core) * NY + y % NY
+
+
+def groups_zc():
+    return [
+        [device(z + FIRST_YZ, x, core, y) for z in range(NZ) for core in range(NC)]
+        for x in range(NX)
+        for y in range(NY)
+    ]
+
+
+def groups_xy():
+    return [
+        [device(z, x + FIRST_X, core, y + FIRST_YZ) for x in range(NX) for y in range(NY)]
+        for z in range(NZ)
+        for core in range(NC)
+    ]
+
+
+def groups_zx():
+    return [
+        [device(z + FIRST_YZ, x + FIRST_X, core, y) for z in range(NZ) for x in range(NX)]
+        for core in range(NC)
+        for y in range(NY)
+    ]
+
+
+def exchange(blocks, groups):
+    axes = ("z", "x", "core", "tp")
+    return lax.all_to_all(blocks, axes, 0, 0, axis_index_groups=groups, tiled=True)
 
 
 def interleave(first, second):
@@ -70,7 +104,8 @@
     def by_slot(x):
         x = x.reshape(NX * 2, 2, 2, 8, HS)
         low, high = interleave(x[:, 0].reshape(-1, 8, HS), x[:, 1].reshape(-1, 8, HS))
-        x = jnp.stack([low, high], axis=1).reshape(NX, 8, 8, HS)
+        x = jnp.stack([low, high], axis=1).reshape(NX, 2, NX, 8, HS)
+        x = jnp.concatenate([x[:, :, FIRST_X:], x[:, :, :FIRST_X]], axis=2).reshape(NX, 8, 8, HS)
         return jnp.swapaxes(x, 0, 1).reshape(8, PAIRS, HS)
 
     for step in range(NY // 2):
@@ -120,8 +155,9 @@
     rows = PAIRS // 8
     row = lax.broadcasted_iota(jnp.int32, (rows, HS), 0)
     live = row + rows * lax.axis_index(("z", "x", "core")) < resp
-    for head in range(8):
-        block = result[rows * head : rows * (head + 1)]
+    for place in range(8):
+        block = result[rows * place : rows * (place + 1)]
+        head = (place + NC * FIRST_X) % 8
         out_ref[:, HS * head : HS * (head + 1)] = jnp.where(live, block, 0.0).astype(jnp.bfloat16)
 
 
@@ -177,21 +213,20 @@
     with jax.named_scope("query_spread"):
         slots, own = pack(queries, keys, values, counts, resp_len)
         halves = slots.reshape(NZ * NC, 16, HS)
-        groups = lax.all_to_all(halves, ("z", "core"), 0, 0, tiled=True).reshape(NZ, PAIRS, HS)
+        groups = exchange(halves, groups_zc()).reshape(NZ, PAIRS, HS)
     with jax.named_scope("pair_exchange"):
         got = lax.ppermute(own, "core", [(0, 1), (1, 0)])
     groups, own = lax.optimization_barrier((groups, own))
     with jax.named_scope("query_spread"):
         groups = jnp.broadcast_to(groups[None], (NX, NY, PAIRS, HS)).reshape(SRC, PAIRS, HS)
-        spread = lax.all_to_all(groups, ("x", "tp"), 0, 0, tiled=True)
+        spread = exchange(groups, groups_xy())
         spread = spread.reshape(NX, NY, PAIRS, HS)
     with jax.named_scope("attend"):
         wide = widen(own, spread)
         parts = attend(spread, own, wide, got)
     with jax.named_scope("merge"):
-        parts = lax.all_to_all(
-            parts.reshape(SRC, SLOT_ROWS, HS), ("z", "x"), 0, 0, tiled=True
-        ).reshape(SRC * SLOT_ROWS, HS)
+        parts = exchange(parts.reshape(SRC, SLOT_ROWS, HS), groups_zx())
+        parts = parts.reshape(SRC * SLOT_ROWS, HS)
         return merge(parts)
 
 

time: 66.3 us -> 61.1 us (0.922)
  the two profiles are of different devices: /device:TPU:8 before, /device:TPU:6 now
where the time goes in v4:
time: 61.1 us; the launch traced here: 60.6 us
  blocking collectives  35.8 us (59%)
  starting transfers between devices  15.8 us (26%)
  Pallas kernels  6.52 us (11%)
  between operations  1.34 us (2%)
  waiting for transfers between devices  1.07 us (2%)
    all_to_all x2, blocking collectives, exchange(): lax.all_to_all(blocks, axes, 0, 0, axis_index_groups=groups, tiled=True)  35.8 us
    all_to_all x1, starting transfers between devices, exchange(): lax.all_to_all(blocks, axes, 0, 0, axis_index_groups=groups, tiled=True)  13.7 us
    pallas_call x1, Pallas kernels, attend(): pl.pallas_call(attend_kernel, out_shape=jax.ShapeDtypeStruct((SRC * SLOT_...  3.37 us
    ppermute x1, starting transfers between devices, local(): got = lax.ppermute(own, 'core', [(0, 1), (1, 0)])  2.04 us
    pallas_call x1, Pallas kernels, pack(): pl.pallas_call(pack_kernel, out_shape=(jax.ShapeDtypeStruct((NZ, NC, 16,...  1.93 us
  transfers between devices with their start and end apart: 2, of which 1 were waited for; matrix products, arithmetic and copies ran while one was open for 0% of the time, Pallas kernels for 0%

profile of v4, /device:TPU:6, one launch (start us, length us, event | category | flops | bytes accessed | tf_op | source)
XLA Modules:
  0.0 60.6 jit_solution(14662591889967146487)
XLA Ops:
  1.3 1.9 %query_spread.1 = (bf16[8,2,16,128]{3,2,1,0:T(8,128)(2,1)}, bf16[2064,128]{1,0:T(8,128)(2,1)}) custom-call(bf16[32,128]{1,0:T(8,128)(2,1)} %query_ref.1, bf16[1024,128]{1,0:T(8,128)(2,1)} %key_ref.1, bf16[1024,128]{1,0:T(8,128)(2,1)} %value_ref.1, s32[1,1]{1,0:T(1,128)} %bitcast.8.count_ref, s32[1,1]{1,0:T(1,128)} %bitcast.9.resp_ref), custom_call_target="tpu_custom_call" | custom-call | tf_op jit(solution)/shard_map/query_spread/pallas_call | solution.py:169
  3.2 0.0 copy-start
  3.2 13.7 %all-to-all-start = ((bf16[16,16,128]{2,1,0:T(8,128)(2,1)}), bf16[16,16,128]{2,1,0:T(8,128)(2,1)S(1)}, u32[]{:S(2)}, u32[]{:S(2)}) async-start(bf16[16,16,128]{2,1,0:T(8,128)(2,1)} %bitcast.16), calls=%async_computation | async-start | bytes 131072 | tf_op jit(solution)/shard_map/query_spread/all_to_all | solution.py:56
  17.0 2.0 %collective-permute-start = (bf16[2064,128]{1,0:T(8,128)(2,1)}, bf16[2064,128]{1,0:T(8,128)(2,1)S(1)}, u32[]{:S(2)}, u32[]{:S(2)}) collective-permute-start(bf16[2064,128]{1,0:T(8,128)(2,1)} %get-tuple-element.12.own_ref), channel_id=1, source_target_pairs={{0,8},{8,0},{1,9},{9,1},{2,10},{10,2},{3,11},{11,3},{4,12},{12,4},... | collective-permute-start | bytes 1585160 | tf_op jit(solution)/shard_map/pair_exchange/ppermute | solution.py:218
  19.0 1.1 %all-to-all-done = bf16[16,16,128]{2,1,0:T(8,128)(2,1)S(1)} async-done(((bf16[16,16,128]{2,1,0:T(8,128)(2,1)}), bf16[16,16,128]{2,1,0:T(8,128)(2,1)S(1)}, u32[]{:S(2)}, u32[]{:S(2)}) %all-to-all-start) | async-done | bytes 65568 | tf_op jit(solution)/shard_map/query_spread/all_to_all | solution.py:56
  20.1 17.8 %all_to_all.15 = bf16[32,32,128]{2,1,0:T(8,128)(2,1)S(1)} all-to-all(bf16[32,32,128]{2,1,0:T(8,128)(2,1)S(1)} %bitcast.14), channel_id=1, replica_groups={{36,37,38,39,32,33,34,35,52,53,54,55,48,49,50,51,4,5,6,7,0,1,2,3,20,21,..., dimensions={0} | all-to-all | bytes 524288 | tf_op jit(solution)/shard_map/query_spread/all_to_all | solution.py:56
  37.9 0.0 copy-done
  37.9 0.1 attend.2.own_wide_ref
  38.0 0.0 collective-permute-done.got_ref
  38.0 3.4 %attend.3 = bf16[1280,128]{1,0:T(8,128)(2,1)S(1)} custom-call(bf16[4,8,32,128]{3,2,1,0:T(8,128)(2,1)S(1)} %bitcast.11, bf16[2064,128]{1,0:T(8,128)(2,1)S(1)} %copy-done, bf16[1024,256]{1,0:T(8,128)(2,1)S(1)} %attend.2.own_wide_ref, bf16[2064,128]{1,0:T(8,128)(2,1)S(1)} %collective-permute-done.got_ref), custom_call_target="tpu_custom_call" | custom-call | tf_op jit(solution)/shard_map/attend/pallas_call | solution.py:192
  41.4 18.0 %all_to_all.16 = bf16[32,40,128]{2,1,0:T(8,128)(2,1)S(1)} all-to-all(bf16[32,40,128]{2,1,0:T(8,128)(2,1)S(1)} %bitcast.13), channel_id=1, replica_groups={{288,304,256,272,352,368,320,336,416,432,384,400,480,496,448,464,32,48,..., dimensions={0} | all-to-all | bytes 655360 | tf_op jit(solution)/shard_map/merge/all_to_all | solution.py:56
  59.4 1.1 %merge.1 = bf16[4,1024]{1,0:T(4,128)(2,1)} custom-call(bf16[1280,128]{1,0:T(8,128)(2,1)S(1)} %bitcast.12), custom_call_target="tpu_custom_call" | custom-call | tf_op jit(solution)/shard_map/merge/pallas_call | solution.py:203
  (1 shorter events, 0.0 us)
Async XLA Ops:
  3.2 34.7 %copy-start = (bf16[2064,128]{1,0:T(8,128)(2,1)S(1)}, bf16[2064,128]{1,0:T(8,128)(2,1)}, u32[]{:S(2)}) copy-start(bf16[2064,128]{1,0:T(8,128)(2,1)} %get-tuple-element.12.own_ref) | copy-start | bytes 1585156
  3.2 16.8 %all-to-all-start = ((bf16[16,16,128]{2,1,0:T(8,128)(2,1)}), bf16[16,16,128]{2,1,0:T(8,128)(2,1)S(1)}, u32[]{:S(2)}, u32[]{:S(2)}) async-start(bf16[16,16,128]{2,1,0:T(8,128)(2,1)} %bitcast.16), calls=%async_computation | async-start | bytes 131072 | tf_op jit(solution)/shard_map/query_spread/all_to_all | solution.py:56
  17.0 21.1 %collective-permute-start = (bf16[2064,128]{1,0:T(8,128)(2,1)}, bf16[2064,128]{1,0:T(8,128)(2,1)S(1)}, u32[]{:S(2)}, u32[]{:S(2)}) collective-permute-start(bf16[2064,128]{1,0:T(8,128)(2,1)} %get-tuple-element.12.own_ref), channel_id=1, source_target_pairs={{0,8},{8,0},{1,9},{9,1},{2,10},{10,2},{3,11},{11,3},{4,12},{12,4},... | collective-permute-start | bytes 1585160 | tf_op jit(solution)/shard_map/pair_exchange/ppermute | solution.py:218

commit v5 on v4

--- a/solution.py
+++ b/solution.py
@@ -15,7 +15,7 @@
 SLOT_ROWS = 40
 SEND_ROWS = 2 * SLOTS + 16
 COUNT_BASE = 64
-FIRST_X, FIRST_YZ = 2, 4
+FIRST_Z, FIRST_X, FIRST_Y, LAST_Z, LAST_X = 6, 2, 4, 4, 2
 MASKED = -1e30
 
 
@@ -29,7 +29,7 @@
 
 def groups_zc():
     return [
-        [device(z + FIRST_YZ, x, core, y) for z in range(NZ) for core in range(NC)]
+        [device(z + FIRST_Z, x, core, y) for z in range(NZ) for core in range(NC)]
         for x in range(NX)
         for y in range(NY)
     ]
@@ -37,7 +37,7 @@
 
 def groups_xy():
     return [
-        [device(z, x + FIRST_X, core, y + FIRST_YZ) for x in range(NX) for y in range(NY)]
+        [device(z, x + FIRST_X, core, y + FIRST_Y) for x in range(NX) for y in range(NY)]
         for z in range(NZ)
         for core in range(NC)
     ]
@@ -45,7 +45,7 @@
 
 def groups_zx():
     return [
-        [device(z + FIRST_YZ, x + FIRST_X, core, y) for z in range(NZ) for x in range(NX)]
+        [device(z + LAST_Z, x + LAST_X, core, y) for z in range(NZ) for x in range(NX)]
         for core in range(NC)
         for y in range(NY)
     ]
@@ -62,19 +62,26 @@
     return low, high
 
 
-def pack_kernel(query_ref, key_ref, value_ref, count_ref, resp_ref, slots_ref, send_ref):
+def pack_kernel(query_ref, key_ref, value_ref, slots_ref, send_ref):
     rows = query_ref[...].astype(jnp.float32).reshape(2, 2, 8, HS)
     for core, half in enumerate(interleave(rows[:, 0], rows[:, 1])):
         half = half.reshape(16, HS).astype(jnp.bfloat16)
         for z in range(NZ):
             slots_ref[z, core] = half
-    count = count_ref[...]
+    send_ref[:SLOTS, :] = key_ref[...]
+    send_ref[SLOTS : 2 * SLOTS, :] = value_ref[...]
+    send_ref[2 * SLOTS : SEND_ROWS, :] = jnp.zeros((16, HS), jnp.bfloat16)
+
+
+def note_kernel(count_ref, resp_ref, _, send_ref, tail_ref, sem):
+    count = count_ref[0]
     row = lax.broadcasted_iota(jnp.int32, (16, HS), 0)
     high = count // COUNT_BASE
-    tail = jnp.where(row == 0, high, jnp.where(row == 1, count - high * COUNT_BASE, resp_ref[...]))
-    send_ref[:SLOTS, :] = key_ref[...]
-    send_ref[SLOTS : 2 * SLOTS, :] = value_ref[...]
-    send_ref[2 * SLOTS : SEND_ROWS, :] = tail.astype(jnp.float32).astype(jnp.bfloat16)
+    tail = jnp.where(row == 0, high, jnp.where(row == 1, count - high * COUNT_BASE, resp_ref[0]))
+    tail_ref[...] = tail.astype(jnp.float32).astype(jnp.bfloat16)
+    copy = pltpu.make_async_copy(tail_ref, send_ref.at[pl.ds(2 * SLOTS, 16)], sem)
+    copy.start()
+    copy.wait()
 
 
 def widen_kernel(own_ref, _, wide_ref):
@@ -94,22 +101,22 @@
         biases.append(jnp.where(slot < count, 0.0, MASKED))
     resp = tail[2:3]
 
-    tile = 2 * NX * PAIRS
+    tile = NX * PAIRS
     part = lane_ids((tile, HS)) // PAIRS
-    pair = lax.broadcasted_iota(jnp.int32, (8, PAIRS, HS), 1)
-    lane = lane_ids((8, PAIRS, HS))
+    pair = lax.broadcasted_iota(jnp.int32, (NX, PAIRS, HS), 1)
+    lane = lane_ids((NX, PAIRS, HS))
     diagonal = lane % PAIRS == pair
-    sub = lax.broadcasted_iota(jnp.int32, (8, 8, HS), 1)
+    sub = lax.broadcasted_iota(jnp.int32, (NX, 8, HS), 1)
 
     def by_slot(x):
-        x = x.reshape(NX * 2, 2, 2, 8, HS)
+        x = x.reshape(NX, 2, 2, 8, HS)
         low, high = interleave(x[:, 0].reshape(-1, 8, HS), x[:, 1].reshape(-1, 8, HS))
-        x = jnp.stack([low, high], axis=1).reshape(NX, 2, NX, 8, HS)
-        x = jnp.concatenate([x[:, :, FIRST_X:], x[:, :, :FIRST_X]], axis=2).reshape(NX, 8, 8, HS)
-        return jnp.swapaxes(x, 0, 1).reshape(8, PAIRS, HS)
-
-    for step in range(NY // 2):
-        q = q_ref[:, 2 * step : 2 * step + 2].reshape(tile, HS)
+        x = jnp.stack([low, high], axis=1).reshape(NX, NX, 8, HS)
+        x = jnp.concatenate([x[:, LAST_X:], x[:, :LAST_X]], axis=1)
+        return jnp.swapaxes(x, 0, 1).reshape(NX, PAIRS, HS)
+
+    for step in range(NY):
+        q = q_ref[:, step].reshape(tile, HS)
         found = []
         for block, (keys_ref, values_ref) in enumerate(((own_ref, own_wide_ref), (got_ref, wide_ref))):
             keys = keys_ref[:SLOTS, :]
@@ -133,8 +140,9 @@
         stats = jnp.where(diagonal, by_slot(stats), 0.0)
         stats = jnp.sum(stats, axis=1, keepdims=True)
         stats = jnp.where(sub == 0, stats, 0.0)
-        full = jnp.concatenate([out, stats], axis=1).reshape(8 * SLOT_ROWS, HS)
-        out_ref[8 * SLOT_ROWS * step : 8 * SLOT_ROWS * (step + 1), :] = full.astype(jnp.bfloat16)
+        full = jnp.concatenate([out, stats], axis=1).reshape(NX * SLOT_ROWS, HS)
+        place = (step + FIRST_Y - LAST_Z) % NZ * NX * SLOT_ROWS
+        out_ref[place : place + NX * SLOT_ROWS, :] = full.astype(jnp.bfloat16)
 
 
 def merge_kernel(parts_ref, out_ref):
@@ -162,20 +170,33 @@
 
 
 VMEM = pl.BlockSpec(memory_space=pltpu.VMEM)
+SMEM = pl.BlockSpec(memory_space=pltpu.SMEM)
 HBM = pl.BlockSpec(memory_space=pltpu.HBM)
 
 
-def pack(queries, keys, values, counts, resp_len):
+def pack(queries, keys, values):
     return pl.pallas_call(
         pack_kernel,
         out_shape=(
             jax.ShapeDtypeStruct((NZ, NC, 16, HS), jnp.bfloat16),
             jax.ShapeDtypeStruct((SEND_ROWS, HS), jnp.bfloat16),
         ),
-        in_specs=[VMEM] * 5,
+        in_specs=[VMEM] * 3,
         out_specs=(VMEM, VMEM),
         compiler_params=pltpu.CompilerParams(vmem_limit_bytes=60 * 2**20),
-    )(queries, keys, values, counts.reshape(1, 1), resp_len.reshape(1, 1))
+    )(queries, keys, values)
+
+
+def note(counts, resp_len, own):
+    return pl.pallas_call(
+        note_kernel,
+        out_shape=jax.ShapeDtypeStruct((SEND_ROWS, HS), jnp.bfloat16),
+        in_specs=[SMEM, SMEM, HBM],
+        out_specs=HBM,
+        input_output_aliases={2: 0},
+        scratch_shapes=[pltpu.VMEM((16, HS), jnp.bfloat16), pltpu.SemaphoreType.DMA],
+        compiler_params=pltpu.CompilerParams(vmem_limit_bytes=60 * 2**20),
+    )(counts, resp_len, own)
 
 
 def widen(own, after):
@@ -211,13 +232,15 @@
 
 def local(queries, keys, values, counts, resp_len):
     with jax.named_scope("query_spread"):
-        slots, own = pack(queries, keys, values, counts, resp_len)
+        slots, own = pack(queries, keys, values)
         halves = slots.reshape(NZ * NC, 16, HS)
         groups = exchange(halves, groups_zc()).reshape(NZ, PAIRS, HS)
     with jax.named_scope("pair_exchange"):
+        own = note(counts, resp_len, own)
         got = lax.ppermute(own, "core", [(0, 1), (1, 0)])
     groups, own = lax.optimization_barrier((groups, own))
     with jax.named_scope("query_spread"):
+        groups = jnp.roll(groups, FIRST_Z - FIRST_Y, axis=0)
         groups = jnp.broadcast_to(groups[None], (NX, NY, PAIRS, HS)).reshape(SRC, PAIRS, HS)
         spread = exchange(groups, groups_xy())
         spread = spread.reshape(NX, NY, PAIRS, HS)

time: 61.1 us -> 59.7 us (0.977)
  starting transfers between devices: 15.8 us -> 14.4 us
    all_to_all x1, starting transfers between devices: 13.7 us -> 12.3 us  [exchange(): lax.all_to_all(blocks, axes, 0, 0, axis_index_groups=groups, tiled=True)]
    pallas_call x0 -> x1, Pallas kernels: none -> 0.61 us  [note(): pl.pallas_call(note_kernel, out_shape=jax.ShapeDtypeStruct((SEND_ROWS, HS...]
  transfers between devices with their start and end apart: 2 -> 2, of which waited for: 1 -> 1; matrix products, arithmetic and copies ran while one was open for 0% -> 0% of each run, Pallas kernels for 0% -> 1%
where the time goes in v5:
time: 59.7 us; the launch traced here: 59.2 us
  blocking collectives  35.9 us (60%)
  starting transfers between devices  14.4 us (24%)
  Pallas kernels  6.92 us (12%)
  between operations  1.35 us (2%)
  waiting for transfers between devices  0.63 us (1%)
    all_to_all x2, blocking collectives, exchange(): lax.all_to_all(blocks, axes, 0, 0, axis_index_groups=groups, tiled=True)  35.9 us
    all_to_all x1, starting transfers between devices, exchange(): lax.all_to_all(blocks, axes, 0, 0, axis_index_groups=groups, tiled=True)  12.3 us
    pallas_call x1, Pallas kernels, attend(): pl.pallas_call(attend_kernel, out_shape=jax.ShapeDtypeStruct((SRC * SLOT_...  3.21 us
    ppermute x1, starting transfers between devices, local(): got = lax.ppermute(own, 'core', [(0, 1), (1, 0)])  2.06 us
    pallas_call x1, Pallas kernels, pack(): pl.pallas_call(pack_kernel, out_shape=(jax.ShapeDtypeStruct((NZ, NC, 16,...  1.88 us
  transfers between devices with their start and end apart: 2, of which 1 were waited for; matrix products, arithmetic and copies ran while one was open for 0% of the time, Pallas kernels for 1%

profile of v5, /device:TPU:6, one launch (start us, length us, event | category | flops | bytes accessed | tf_op | source)
XLA Modules:
  0.0 59.2 jit_solution(14210277164123166189)
XLA Ops:
  0.0 1.9 %query_spread.1 = (bf16[8,2,16,128]{3,2,1,0:T(8,128)(2,1)}, bf16[2064,128]{1,0:T(8,128)(2,1)}) custom-call(bf16[32,128]{1,0:T(8,128)(2,1)} %query_ref.1, bf16[1024,128]{1,0:T(8,128)(2,1)} %key_ref.1, bf16[1024,128]{1,0:T(8,128)(2,1)} %value_ref.1), custom_call_target="tpu_custom_call" | custom-call | tf_op jit(solution)/shard_map/query_spread/pallas_call | solution.py:178
  1.9 12.3 %all-to-all-start = ((bf16[16,16,128]{2,1,0:T(8,128)(2,1)}), bf16[16,16,128]{2,1,0:T(8,128)(2,1)S(1)}, u32[]{:S(2)}, u32[]{:S(2)}) async-start(bf16[16,16,128]{2,1,0:T(8,128)(2,1)} %bitcast.13), calls=%async_computation | async-start | bytes 131072 | tf_op jit(solution)/shard_map/query_spread/all_to_all | solution.py:56
  15.5 0.6 %pair_exchange.1.own_ref = bf16[2064,128]{1,0:T(8,128)(2,1)} custom-call(s32[1]{0:T(128)S(6)} %copy.8.count_ref, s32[1]{0:T(128)S(6)} %copy.9.resp_ref, bf16[2064,128]{1,0:T(8,128)(2,1)} %get-tuple-element.10._), custom_call_target="tpu_custom_call", output_to_operand_aliasing={{}: (2, {})} | custom-call | tf_op jit(solution)/shard_map/pair_exchange/pallas_call | solution.py:191
  16.1 2.1 %collective-permute-start = (bf16[2064,128]{1,0:T(8,128)(2,1)}, bf16[2064,128]{1,0:T(8,128)(2,1)S(1)}, u32[]{:S(2)}, u32[]{:S(2)}) collective-permute-start(bf16[2064,128]{1,0:T(8,128)(2,1)} %pair_exchange.1.own_ref), channel_id=1, source_target_pairs={{0,8},{8,0},{1,9},{9,1},{2,10},{10,2},{3,11},{11,3},{4,12},{12,4},... | collective-permute-start | bytes 1585160 | tf_op jit(solution)/shard_map/pair_exchange/ppermute | solution.py:240
  18.2 0.6 %all-to-all-done = bf16[16,16,128]{2,1,0:T(8,128)(2,1)S(1)} async-done(((bf16[16,16,128]{2,1,0:T(8,128)(2,1)}), bf16[16,16,128]{2,1,0:T(8,128)(2,1)S(1)}, u32[]{:S(2)}, u32[]{:S(2)}) %all-to-all-start) | async-done | bytes 65568 | tf_op jit(solution)/shard_map/query_spread/all_to_all | solution.py:56
  18.8 0.0 copy-start
  18.9 18.0 %all_to_all.15 = bf16[32,32,128]{2,1,0:T(8,128)(2,1)S(1)} all-to-all(bf16[32,32,128]{2,1,0:T(8,128)(2,1)S(1)} %bitcast.10), channel_id=1, replica_groups={{36,37,38,39,32,33,34,35,52,53,54,55,48,49,50,51,4,5,6,7,0,1,2,3,20,21,..., dimensions={0} | all-to-all | bytes 524288 | tf_op jit(solution)/shard_map/query_spread/all_to_all | solution.py:56
  36.9 0.0 copy-done
  36.9 0.1 attend.2.own_wide_ref
  36.9 0.0 collective-permute-done.got_ref
  36.9 3.2 %attend.3 = bf16[1280,128]{1,0:T(8,128)(2,1)S(1)} custom-call(bf16[4,8,32,128]{3,2,1,0:T(8,128)(2,1)S(1)} %bitcast.7, bf16[2064,128]{1,0:T(8,128)(2,1)S(1)} %copy-done, bf16[1024,256]{1,0:T(8,128)(2,1)S(1)} %attend.2.own_wide_ref, bf16[2064,128]{1,0:T(8,128)(2,1)S(1)} %collective-permute-done.got_ref), custom_call_target="tpu_custom_call" | custom-call | tf_op jit(solution)/shard_map/attend/pallas_call | solution.py:213
  40.2 17.9 %all_to_all.16 = bf16[32,40,128]{2,1,0:T(8,128)(2,1)S(1)} all-to-all(bf16[32,40,128]{2,1,0:T(8,128)(2,1)S(1)} %bitcast.9), channel_id=1, replica_groups={{288,304,256,272,352,368,320,336,416,432,384,400,480,496,448,464,32,48,..., dimensions={0} | all-to-all | bytes 655360 | tf_op jit(solution)/shard_map/merge/all_to_all | solution.py:56
  58.1 1.1 %merge.1 = bf16[4,1024]{1,0:T(4,128)(2,1)} custom-call(bf16[1280,128]{1,0:T(8,128)(2,1)S(1)} %bitcast.8), custom_call_target="tpu_custom_call" | custom-call | tf_op jit(solution)/shard_map/merge/pallas_call | solution.py:224
  (4 shorter events, 0.1 us)
Async XLA Ops:
  1.9 16.9 %all-to-all-start = ((bf16[16,16,128]{2,1,0:T(8,128)(2,1)}), bf16[16,16,128]{2,1,0:T(8,128)(2,1)S(1)}, u32[]{:S(2)}, u32[]{:S(2)}) async-start(bf16[16,16,128]{2,1,0:T(8,128)(2,1)} %bitcast.13), calls=%async_computation | async-start | bytes 131072 | tf_op jit(solution)/shard_map/query_spread/all_to_all | solution.py:56
  16.1 20.8 %collective-permute-start = (bf16[2064,128]{1,0:T(8,128)(2,1)}, bf16[2064,128]{1,0:T(8,128)(2,1)S(1)}, u32[]{:S(2)}, u32[]{:S(2)}) collective-permute-start(bf16[2064,128]{1,0:T(8,128)(2,1)} %pair_exchange.1.own_ref), channel_id=1, source_target_pairs={{0,8},{8,0},{1,9},{9,1},{2,10},{10,2},{3,11},{11,3},{4,12},{12,4},... | collective-permute-start | bytes 1585160 | tf_op jit(solution)/shard_map/pair_exchange/ppermute | solution.py:240
  18.8 18.0 %copy-start = (bf16[2064,128]{1,0:T(8,128)(2,1)S(1)}, bf16[2064,128]{1,0:T(8,128)(2,1)}, u32[]{:S(2)}) copy-start(bf16[2064,128]{1,0:T(8,128)(2,1)} %pair_exchange.1.own_ref) | copy-start | bytes 1585156

commit v6 on v5

--- a/solution.py
+++ b/solution.py
@@ -15,7 +15,7 @@
 SLOT_ROWS = 40
 SEND_ROWS = 2 * SLOTS + 16
 COUNT_BASE = 64
-FIRST_Z, FIRST_X, FIRST_Y, LAST_Z, LAST_X = 6, 2, 4, 4, 2
+FIRST_Z, FIRST_X, FIRST_Y, LAST_Z, LAST_X = 6, 3, 4, 4, 2
 MASKED = -1e30
 
 
@@ -62,15 +62,30 @@
     return low, high
 
 
-def pack_kernel(query_ref, key_ref, value_ref, slots_ref, send_ref):
-    rows = query_ref[...].astype(jnp.float32).reshape(2, 2, 8, HS)
-    for core, half in enumerate(interleave(rows[:, 0], rows[:, 1])):
+def pack_kernel(query_ref, key_ref, value_ref, slots_ref, send_ref, rows, slots, both, sems):
+    def copy(source, target, which):
+        made = pltpu.make_async_copy(source, target, sems.at[which])
+        made.start()
+        return made
+
+    first, second = pl.ds(0, SLOTS), pl.ds(SLOTS, SLOTS)
+    loads = (
+        copy(query_ref, rows, 0),
+        copy(key_ref, both.at[first], 1),
+        copy(value_ref, both.at[second], 2),
+    )
+    loads[0].wait()
+    halves = rows[...].astype(jnp.float32).reshape(2, 2, 8, HS)
+    for core, half in enumerate(interleave(halves[:, 0], halves[:, 1])):
         half = half.reshape(16, HS).astype(jnp.bfloat16)
         for z in range(NZ):
-            slots_ref[z, core] = half
-    send_ref[:SLOTS, :] = key_ref[...]
-    send_ref[SLOTS : 2 * SLOTS, :] = value_ref[...]
-    send_ref[2 * SLOTS : SEND_ROWS, :] = jnp.zeros((16, HS), jnp.bfloat16)
+            slots[z, core] = half
+    stores = [copy(slots, slots_ref, 3)]
+    for which, part in enumerate((first, second)):
+        loads[1 + which].wait()
+        stores.append(copy(both.at[part], send_ref.at[part], 4 + which))
+    for store in stores:
+        store.wait()
 
 
 def note_kernel(count_ref, resp_ref, _, send_ref, tail_ref, sem):
@@ -181,8 +196,14 @@
             jax.ShapeDtypeStruct((NZ, NC, 16, HS), jnp.bfloat16),
             jax.ShapeDtypeStruct((SEND_ROWS, HS), jnp.bfloat16),
         ),
-        in_specs=[VMEM] * 3,
-        out_specs=(VMEM, VMEM),
+        in_specs=[HBM] * 3,
+        out_specs=(HBM, HBM),
+        scratch_shapes=[
+            pltpu.VMEM((PAIRS, HS), jnp.bfloat16),
+            pltpu.VMEM((NZ, NC, 16, HS), jnp.bfloat16),
+            pltpu.VMEM((2 * SLOTS, HS), jnp.bfloat16),
+            pltpu.SemaphoreType.DMA((6,)),
+        ],
         compiler_params=pltpu.CompilerParams(vmem_limit_bytes=60 * 2**20),
     )(queries, keys, values)
 

time: 59.7 us -> 59.3 us (level)
  no operation moved by 1% of the time
where the time goes in v6:
time: 59.3 us; the launch traced here: 59 us
  blocking collectives  35.7 us (60%)
  starting transfers between devices  14.4 us (24%)
  Pallas kernels  6.85 us (12%)
  between operations  1.36 us (2%)
  waiting for transfers between devices  0.63 us (1%)
    all_to_all x2, blocking collectives, exchange(): lax.all_to_all(blocks, axes, 0, 0, axis_index_groups=groups, tiled=True)  35.7 us
    all_to_all x1, starting transfers between devices, exchange(): lax.all_to_all(blocks, axes, 0, 0, axis_index_groups=groups, tiled=True)  12.3 us
    pallas_call x1, Pallas kernels, attend(): pl.pallas_call(attend_kernel, out_shape=jax.ShapeDtypeStruct((SRC * SLOT_...  3.21 us
    ppermute x1, starting transfers between devices, local(): got = lax.ppermute(own, 'core', [(0, 1), (1, 0)])  2.06 us
    pallas_call x1, Pallas kernels, pack(): pl.pallas_call(pack_kernel, out_shape=(jax.ShapeDtypeStruct((NZ, NC, 16,...  1.81 us
  transfers between devices with their start and end apart: 2, of which 1 were waited for; matrix products, arithmetic and copies ran while one was open for 0% of the time, Pallas kernels for 1%

profile of v6, /device:TPU:6, one launch (start us, length us, event | category | flops | bytes accessed | tf_op | source)
XLA Modules:
  0.0 59.0 jit_solution(10416198617372571991)
XLA Ops:
  0.0 1.8 %query_spread.1 = (bf16[8,2,16,128]{3,2,1,0:T(8,128)(2,1)}, bf16[2064,128]{1,0:T(8,128)(2,1)}) custom-call(bf16[32,128]{1,0:T(8,128)(2,1)} %query_ref.1, bf16[1024,128]{1,0:T(8,128)(2,1)} %key_ref.1, bf16[1024,128]{1,0:T(8,128)(2,1)} %value_ref.1), custom_call_target="tpu_custom_call" | custom-call | tf_op jit(solution)/shard_map/query_spread/pallas_call | solution.py:193
  1.8 12.3 %all-to-all-start = ((bf16[16,16,128]{2,1,0:T(8,128)(2,1)}), bf16[16,16,128]{2,1,0:T(8,128)(2,1)S(1)}, u32[]{:S(2)}, u32[]{:S(2)}) async-start(bf16[16,16,128]{2,1,0:T(8,128)(2,1)} %bitcast.13), calls=%async_computation | async-start | bytes 131072 | tf_op jit(solution)/shard_map/query_spread/all_to_all | solution.py:56
  15.5 0.6 %pair_exchange.1.own_ref = bf16[2064,128]{1,0:T(8,128)(2,1)} custom-call(s32[1]{0:T(128)S(6)} %copy.8.count_ref, s32[1]{0:T(128)S(6)} %copy.9.resp_ref, bf16[2064,128]{1,0:T(8,128)(2,1)} %get-tuple-element.10._), custom_call_target="tpu_custom_call", output_to_operand_aliasing={{}: (2, {})} | custom-call | tf_op jit(solution)/shard_map/pair_exchange/pallas_call | solution.py:212
  16.1 2.1 %collective-permute-start = (bf16[2064,128]{1,0:T(8,128)(2,1)}, bf16[2064,128]{1,0:T(8,128)(2,1)S(1)}, u32[]{:S(2)}, u32[]{:S(2)}) collective-permute-start(bf16[2064,128]{1,0:T(8,128)(2,1)} %pair_exchange.1.own_ref), channel_id=1, source_target_pairs={{0,8},{8,0},{1,9},{9,1},{2,10},{10,2},{3,11},{11,3},{4,12},{12,4},... | collective-permute-start | bytes 1585160 | tf_op jit(solution)/shard_map/pair_exchange/ppermute | solution.py:261
  18.1 0.6 %all-to-all-done = bf16[16,16,128]{2,1,0:T(8,128)(2,1)S(1)} async-done(((bf16[16,16,128]{2,1,0:T(8,128)(2,1)}), bf16[16,16,128]{2,1,0:T(8,128)(2,1)S(1)}, u32[]{:S(2)}, u32[]{:S(2)}) %all-to-all-start) | async-done | bytes 65568 | tf_op jit(solution)/shard_map/query_spread/all_to_all | solution.py:56
  18.8 0.0 copy-start
  18.8 17.9 %all_to_all.15 = bf16[32,32,128]{2,1,0:T(8,128)(2,1)S(1)} all-to-all(bf16[32,32,128]{2,1,0:T(8,128)(2,1)S(1)} %bitcast.10), channel_id=1, replica_groups={{52,53,54,55,48,49,50,51,4,5,6,7,0,1,2,3,20,21,22,23,16,17,18,19,36,37,..., dimensions={0} | all-to-all | bytes 524288 | tf_op jit(solution)/shard_map/query_spread/all_to_all | solution.py:56
  36.7 0.0 copy-done
  36.7 0.1 attend.2.own_wide_ref
  36.8 0.0 collective-permute-done.got_ref
  36.8 3.2 %attend.3 = bf16[1280,128]{1,0:T(8,128)(2,1)S(1)} custom-call(bf16[4,8,32,128]{3,2,1,0:T(8,128)(2,1)S(1)} %bitcast.7, bf16[2064,128]{1,0:T(8,128)(2,1)S(1)} %copy-done, bf16[1024,256]{1,0:T(8,128)(2,1)S(1)} %attend.2.own_wide_ref, bf16[2064,128]{1,0:T(8,128)(2,1)S(1)} %collective-permute-done.got_ref), custom_call_target="tpu_custom_call" | custom-call | tf_op jit(solution)/shard_map/attend/pallas_call | solution.py:234
  40.0 17.8 %all_to_all.16 = bf16[32,40,128]{2,1,0:T(8,128)(2,1)S(1)} all-to-all(bf16[32,40,128]{2,1,0:T(8,128)(2,1)S(1)} %bitcast.9), channel_id=1, replica_groups={{288,304,256,272,352,368,320,336,416,432,384,400,480,496,448,464,32,48,..., dimensions={0} | all-to-all | bytes 655360 | tf_op jit(solution)/shard_map/merge/all_to_all | solution.py:56
  57.9 1.1 %merge.1 = bf16[4,1024]{1,0:T(4,128)(2,1)} custom-call(bf16[1280,128]{1,0:T(8,128)(2,1)S(1)} %bitcast.8), custom_call_target="tpu_custom_call" | custom-call | tf_op jit(solution)/shard_map/merge/pallas_call | solution.py:245
  (4 shorter events, 0.1 us)
Async XLA Ops:
  1.8 16.9 %all-to-all-start = ((bf16[16,16,128]{2,1,0:T(8,128)(2,1)}), bf16[16,16,128]{2,1,0:T(8,128)(2,1)S(1)}, u32[]{:S(2)}, u32[]{:S(2)}) async-start(bf16[16,16,128]{2,1,0:T(8,128)(2,1)} %bitcast.13), calls=%async_computation | async-start | bytes 131072 | tf_op jit(solution)/shard_map/query_spread/all_to_all | solution.py:56
  16.1 20.8 %collective-permute-start = (bf16[2064,128]{1,0:T(8,128)(2,1)}, bf16[2064,128]{1,0:T(8,128)(2,1)S(1)}, u32[]{:S(2)}, u32[]{:S(2)}) collective-permute-start(bf16[2064,128]{1,0:T(8,128)(2,1)} %pair_exchange.1.own_ref), channel_id=1, source_target_pairs={{0,8},{8,0},{1,9},{9,1},{2,10},{10,2},{3,11},{11,3},{4,12},{12,4},... | collective-permute-start | bytes 1585160 | tf_op jit(solution)/shard_map/pair_exchange/ppermute | solution.py:261
  18.8 18.0 %copy-start = (bf16[2064,128]{1,0:T(8,128)(2,1)S(1)}, bf16[2064,128]{1,0:T(8,128)(2,1)}, u32[]{:S(2)}) copy-start(bf16[2064,128]{1,0:T(8,128)(2,1)} %pair_exchange.1.own_ref) | copy-start | bytes 1585156

commit v7 on v5

--- a/solution.py
+++ b/solution.py
@@ -15,7 +15,7 @@
 SLOT_ROWS = 40
 SEND_ROWS = 2 * SLOTS + 16
 COUNT_BASE = 64
-FIRST_Z, FIRST_X, FIRST_Y, LAST_Z, LAST_X = 6, 2, 4, 4, 2
+FIRST_Z, FIRST_X, FIRST_Y, LAST_Z, LAST_X = 6, 3, 4, 4, 2
 MASKED = -1e30
 
 
@@ -62,26 +62,28 @@
     return low, high
 
 
-def pack_kernel(query_ref, key_ref, value_ref, slots_ref, send_ref):
+def halves_kernel(query_ref, slots_ref):
     rows = query_ref[...].astype(jnp.float32).reshape(2, 2, 8, HS)
     for core, half in enumerate(interleave(rows[:, 0], rows[:, 1])):
         half = half.reshape(16, HS).astype(jnp.bfloat16)
         for z in range(NZ):
             slots_ref[z, core] = half
-    send_ref[:SLOTS, :] = key_ref[...]
-    send_ref[SLOTS : 2 * SLOTS, :] = value_ref[...]
-    send_ref[2 * SLOTS : SEND_ROWS, :] = jnp.zeros((16, HS), jnp.bfloat16)
-
-
-def note_kernel(count_ref, resp_ref, _, send_ref, tail_ref, sem):
+
+
+def pack_kernel(count_ref, resp_ref, key_ref, value_ref, _, send_ref, sems):
+    copies = [
+        pltpu.make_async_copy(key_ref, send_ref.at[pl.ds(0, SLOTS)], sems.at[0]),
+        pltpu.make_async_copy(value_ref, send_ref.at[pl.ds(SLOTS, SLOTS)], sems.at[1]),
+    ]
+    for copy in copies:
+        copy.start()
     count = count_ref[0]
+    high = count // COUNT_BASE
     row = lax.broadcasted_iota(jnp.int32, (16, HS), 0)
-    high = count // COUNT_BASE
     tail = jnp.where(row == 0, high, jnp.where(row == 1, count - high * COUNT_BASE, resp_ref[0]))
-    tail_ref[...] = tail.astype(jnp.float32).astype(jnp.bfloat16)
-    copy = pltpu.make_async_copy(tail_ref, send_ref.at[pl.ds(2 * SLOTS, 16)], sem)
-    copy.start()
-    copy.wait()
+    send_ref[2 * SLOTS : SEND_ROWS, :] = tail.astype(jnp.float32).astype(jnp.bfloat16)
+    for copy in copies:
+        copy.wait()
 
 
 def widen_kernel(own_ref, _, wide_ref):
@@ -174,29 +176,26 @@
 HBM = pl.BlockSpec(memory_space=pltpu.HBM)
 
 
-def pack(queries, keys, values):
+def split_halves(queries):
+    return pl.pallas_call(
+        halves_kernel,
+        out_shape=jax.ShapeDtypeStruct((NZ, NC, 16, HS), jnp.bfloat16),
+        in_specs=[VMEM],
+        out_specs=VMEM,
+        compiler_params=pltpu.CompilerParams(vmem_limit_bytes=2**20),
+    )(queries)
+
+
+def pack(counts, resp_len, keys, values, after):
     return pl.pallas_call(
         pack_kernel,
-        out_shape=(
-            jax.ShapeDtypeStruct((NZ, NC, 16, HS), jnp.bfloat16),
-            jax.ShapeDtypeStruct((SEND_ROWS, HS), jnp.bfloat16),
-        ),
-        in_specs=[VMEM] * 3,
-        out_specs=(VMEM, VMEM),
-        compiler_params=pltpu.CompilerParams(vmem_limit_bytes=60 * 2**20),
-    )(queries, keys, values)
-
-
-def note(counts, resp_len, own):
-    return pl.pallas_call(
-        note_kernel,
         out_shape=jax.ShapeDtypeStruct((SEND_ROWS, HS), jnp.bfloat16),
-        in_specs=[SMEM, SMEM, HBM],
-        out_specs=HBM,
-        input_output_aliases={2: 0},
-        scratch_shapes=[pltpu.VMEM((16, HS), jnp.bfloat16), pltpu.SemaphoreType.DMA],
-        compiler_params=pltpu.CompilerParams(vmem_limit_bytes=60 * 2**20),
-    )(counts, resp_len, own)
+        in_specs=[SMEM, SMEM, HBM, HBM, HBM],
+        out_specs=VMEM,
+        scratch_shapes=[pltpu.SemaphoreType.DMA((2,))],
+        compiler_params=pltpu.CompilerParams(vmem_limit_bytes=2 * 2**20),
+        cost_estimate=pl.CostEstimate(flops=0, bytes_accessed=2**23, transcendentals=0),
+    )(counts, resp_len, keys, values, after)
 
 
 def widen(own, after):
@@ -206,6 +205,7 @@
         in_specs=[VMEM, HBM],
         out_specs=VMEM,
         compiler_params=pltpu.CompilerParams(vmem_limit_bytes=2**20),
+        cost_estimate=pl.CostEstimate(flops=2**33, bytes_accessed=2**21, transcendentals=0),
     )(own, after)
 
 
@@ -232,18 +232,14 @@
 
 def local(queries, keys, values, counts, resp_len):
     with jax.named_scope("query_spread"):
-        slots, own = pack(queries, keys, values)
-        halves = slots.reshape(NZ * NC, 16, HS)
+        halves = split_halves(queries).reshape(NZ * NC, 16, HS)
         groups = exchange(halves, groups_zc()).reshape(NZ, PAIRS, HS)
-    with jax.named_scope("pair_exchange"):
-        own = note(counts, resp_len, own)
-        got = lax.ppermute(own, "core", [(0, 1), (1, 0)])
-    groups, own = lax.optimization_barrier((groups, own))
-    with jax.named_scope("query_spread"):
         groups = jnp.roll(groups, FIRST_Z - FIRST_Y, axis=0)
         groups = jnp.broadcast_to(groups[None], (NX, NY, PAIRS, HS)).reshape(SRC, PAIRS, HS)
-        spread = exchange(groups, groups_xy())
-        spread = spread.reshape(NX, NY, PAIRS, HS)
+        spread = exchange(groups, groups_xy()).reshape(NX, NY, PAIRS, HS)
+    with jax.named_scope("pair_exchange"):
+        own = pack(counts, resp_len, keys, values, groups)
+        got = lax.ppermute(own, "core", [(0, 1), (1, 0)])
     with jax.named_scope("attend"):
         wide = widen(own, spread)
         parts = attend(spread, own, wide, got)

time: 59.7 us -> 59.1 us (0.990)
  waiting for transfers between devices: 0.63 us -> 5.9 us
  starting transfers between devices: 14.4 us -> 11.4 us
  Pallas kernels: 6.92 us -> 4.44 us
  blocking collectives: 35.9 us -> 34.1 us
  local copies, waits for them, and re-layouts: 0.05 us -> 1.45 us
    all_to_all x1, waiting for transfers between devices: 0.62 us -> 5.89 us  [exchange(): lax.all_to_all(blocks, axes, 0, 0, axis_index_groups=groups, tiled=True)]
    all_to_all x1, starting transfers between devices: 12.3 us -> 9.5 us  [exchange(): lax.all_to_all(blocks, axes, 0, 0, axis_index_groups=groups, tiled=True)]
    pallas_call x2, Pallas kernels: 2.49 us -> 0.08 us  [the longest x1 0.08 us: pack(): pl.pallas_call(pack_kernel, out_shape=jax.ShapeDtypeStruct((SEND_ROWS, HS...]
    all_to_all x2, blocking collectives: 35.9 us -> 34.1 us  [exchange(): lax.all_to_all(blocks, axes, 0, 0, axis_index_groups=groups, tiled=True)]
    broadcast_in_dim x1, local copies, waits for them, and re-layouts: 0.04 us -> 0.74 us  [local(): jnp.broadcast_to(groups[None], (NX, NY, PAIRS, HS)).reshape(SRC, PAIRS, HS)]
    unnamed x2 -> x6, local copies, waits for them, and re-layouts: 0.01 us -> 0.7 us
  transfers between devices with their start and end apart: 2 -> 2, of which waited for: 1 -> 1; matrix products, arithmetic and copies ran while one was open for 0% -> 0% of each run, Pallas kernels for 1% -> 0%
where the time goes in v7:
time: 59.1 us; the launch traced here: 58.7 us
  blocking collectives  34.1 us (58%)
  starting transfers between devices  11.4 us (19%)
  waiting for transfers between devices  5.9 us (10%)
  Pallas kernels  4.44 us (8%)
  local copies, waits for them, and re-layouts  1.45 us (2%)
  between operations  1.36 us (2%)
    all_to_all x2, blocking collectives, exchange(): lax.all_to_all(blocks, axes, 0, 0, axis_index_groups=groups, tiled=True)  34.1 us
    all_to_all x1, starting transfers between devices, exchange(): lax.all_to_all(blocks, axes, 0, 0, axis_index_groups=groups, tiled=True)  9.5 us
    all_to_all x1, waiting for transfers between devices, exchange(): lax.all_to_all(blocks, axes, 0, 0, axis_index_groups=groups, tiled=True)  5.89 us
    pallas_call x1, Pallas kernels, attend(): pl.pallas_call(attend_kernel, out_shape=jax.ShapeDtypeStruct((SRC * SLOT_...  3.14 us
    ppermute x1, starting transfers between devices, local(): got = lax.ppermute(own, 'core', [(0, 1), (1, 0)])  1.92 us
  transfers between devices with their start and end apart: 2, of which 1 were waited for; matrix products, arithmetic and copies ran while one was open for 0% of the time, Pallas kernels for 0%

profile of v7, /device:TPU:6, one launch (start us, length us, event | category | flops | bytes accessed | tf_op | source)
XLA Modules:
  0.0 58.7 jit_solution(18188575353885763545)
XLA Ops:
  0.0 0.0 copy-start.2
  0.0 0.7 %copy-done.2 = bf16[32,128]{1,0:T(8,128)(2,1)S(1)} copy-done((bf16[32,128]{1,0:T(8,128)(2,1)S(1)}, bf16[32,128]{1,0:T(8,128)(2,1)}, u32[]{:S(2)}) %copy-start.2) | copy-done | bytes 8216
  0.7 16.2 %all_to_all.15 = bf16[16,16,128]{2,1,0:T(8,128)(2,1)S(1)} all-to-all(bf16[16,16,128]{2,1,0:T(8,128)(2,1)S(1)} %bitcast.11), channel_id=1, replica_groups={{384,392,448,456,0,8,64,72,128,136,192,200,256,264,320,328},{385,393,44..., dimensions={0} | all-to-all | bytes 131072 | tf_op jit(solution)/shard_map/query_spread/all_to_all | solution.py:56
  16.9 0.7 %broadcast_in_dim.2 = bf16[4,8,32,128]{3,2,1,0:T(8,128)(2,1)} broadcast(bf16[8,32,128]{2,1,0:T(8,128)(2,1)S(1)} %pad_maximum_fusion), dimensions={1,2,3} | broadcast | bytes 327680 | tf_op jit(solution)/shard_map/query_spread/broadcast_in_dim | solution.py:238
  17.6 0.0 copy-start
  17.6 0.0 copy-start.1
  17.6 9.5 %all-to-all-start.1 = ((bf16[32,32,128]{2,1,0:T(8,128)(2,1)}), bf16[32,32,128]{2,1,0:T(8,128)(2,1)S(1)}, u32[]{:S(2)}, u32[]{:S(2)}) async-start(bf16[32,32,128]{2,1,0:T(8,128)(2,1)} %bitcast.3._), calls=%async_computation.1 | async-start | bytes 524288 | tf_op jit(solution)/shard_map/query_spread/all_to_all | solution.py:56
  28.4 0.0 copy-done
  28.4 0.0 copy-done.1
  28.4 0.1 pair_exchange.1.own_ref
  28.5 1.9 %collective-permute-start = (bf16[2064,128]{1,0:T(8,128)(2,1)S(1)}, bf16[2064,128]{1,0:T(8,128)(2,1)S(1)}, u32[]{:S(2)}, u32[]{:S(2)}) collective-permute-start(bf16[2064,128]{1,0:T(8,128)(2,1)S(1)} %pair_exchange.1.own_ref), channel_id=1, source_target_pairs={{0,8},{8,0},{1,9},{9,1},{2,10},{10,2},{3,11},{11,3},{4,12},{12,4},... | collective-permute-start | bytes 1585160 | tf_op jit(solution)/shard_map/pair_exchange/ppermute | solution.py:242
  30.5 5.9 %all-to-all-done.1 = bf16[32,32,128]{2,1,0:T(8,128)(2,1)S(1)} async-done(((bf16[32,32,128]{2,1,0:T(8,128)(2,1)}), bf16[32,32,128]{2,1,0:T(8,128)(2,1)S(1)}, u32[]{:S(2)}, u32[]{:S(2)}) %all-to-all-start.1) | async-done | bytes 262176 | tf_op jit(solution)/shard_map/query_spread/all_to_all | solution.py:56
  36.4 0.1 attend.2.own_wide_ref
  36.4 0.0 collective-permute-done.got_ref
  36.4 3.1 %attend.3 = bf16[1280,128]{1,0:T(8,128)(2,1)S(1)} custom-call(bf16[4,8,32,128]{3,2,1,0:T(8,128)(2,1)S(1)} %bitcast.10, bf16[2064,128]{1,0:T(8,128)(2,1)S(1)} %pair_exchange.1.own_ref, bf16[1024,256]{1,0:T(8,128)(2,1)S(1)} %attend.2.own_wide_ref, bf16[2064,128]{1,0:T(8,128)(2,1)S(1)} %collective-permute-done.got_ref), custom_call_target="tpu_custom_call" | custom-call | tf_op jit(solution)/shard_map/attend/pallas_call | solution.py:213
  39.6 17.9 %all_to_all.16 = bf16[32,40,128]{2,1,0:T(8,128)(2,1)S(1)} all-to-all(bf16[32,40,128]{2,1,0:T(8,128)(2,1)S(1)} %bitcast.8), channel_id=1, replica_groups={{288,304,256,272,352,368,320,336,416,432,384,400,480,496,448,464,32,48,..., dimensions={0} | all-to-all | bytes 655360 | tf_op jit(solution)/shard_map/merge/all_to_all | solution.py:56
  57.5 1.1 %merge.1 = bf16[4,1024]{1,0:T(4,128)(2,1)} custom-call(bf16[1280,128]{1,0:T(8,128)(2,1)S(1)} %bitcast.7), custom_call_target="tpu_custom_call" | custom-call | tf_op jit(solution)/shard_map/merge/pallas_call | solution.py:224
  (4 shorter events, 0.0 us)
Async XLA Ops:
  0.0 0.7 %copy-start.2 = (bf16[32,128]{1,0:T(8,128)(2,1)S(1)}, bf16[32,128]{1,0:T(8,128)(2,1)}, u32[]{:S(2)}) copy-start(bf16[32,128]{1,0:T(8,128)(2,1)} %query_ref.1) | copy-start | bytes 24580
  17.6 10.8 %copy-start = (bf16[1024,128]{1,0:T(8,128)(2,1)S(1)}, bf16[1024,128]{1,0:T(8,128)(2,1)}, u32[]{:S(2)}) copy-start(bf16[1024,128]{1,0:T(8,128)(2,1)} %key_ref.1) | copy-start | bytes 786436
  17.6 10.8 %copy-start.1 = (bf16[1024,128]{1,0:T(8,128)(2,1)S(1)}, bf16[1024,128]{1,0:T(8,128)(2,1)}, u32[]{:S(2)}) copy-start(bf16[1024,128]{1,0:T(8,128)(2,1)} %value_ref.1) | copy-start | bytes 786436
  17.6 18.7 %all-to-all-start.1 = ((bf16[32,32,128]{2,1,0:T(8,128)(2,1)}), bf16[32,32,128]{2,1,0:T(8,128)(2,1)S(1)}, u32[]{:S(2)}, u32[]{:S(2)}) async-start(bf16[32,32,128]{2,1,0:T(8,128)(2,1)} %bitcast.3._), calls=%async_computation.1 | async-start | bytes 524288 | tf_op jit(solution)/shard_map/query_spread/all_to_all | solution.py:56
  28.5 7.9 %collective-permute-start = (bf16[2064,128]{1,0:T(8,128)(2,1)S(1)}, bf16[2064,128]{1,0:T(8,128)(2,1)S(1)}, u32[]{:S(2)}, u32[]{:S(2)}) collective-permute-start(bf16[2064,128]{1,0:T(8,128)(2,1)S(1)} %pair_exchange.1.own_ref), channel_id=1, source_target_pairs={{0,8},{8,0},{1,9},{9,1},{2,10},{10,2},{3,11},{11,3},{4,12},{12,4},... | collective-permute-start | bytes 1585160 | tf_op jit(solution)/shard_map/pair_exchange/ppermute | solution.py:242

commit v8 on v7

v8 whole, which is shorter than its diff:
```python
import jax
import jax.numpy as jnp
from jax import lax
from jax.experimental import pallas as pl
from jax.experimental.pallas import tpu as pltpu
from jax.sharding import Mesh, PartitionSpec as P

HS = 128
LOG2E = 1.4426950408889634
EXP2_SCALE = LOG2E / HS**0.5
NZ, NX, NC, NY = 8, 4, 2, 8
SLOTS = 1024
TILE = 128
TILES = 4
PAIRS = 32
SLOT_ROWS = 40
SRC = NZ * 2
SEND_ROWS = 2 * SLOTS + 16
COUNT_BASE = 64
MASKED = -1e30
FIRST_Z, FIRST_Y, LAST_Z = 6, 4, 4
SHARERS = ((0, 1), (3, 2))
CLASSES = ((3, 0), (2, 1))
HEAD_X = (3, 2, 0, 1)


def lane_ids(shape):
    return lax.broadcasted_iota(jnp.int32, shape, len(shape) - 1)


def device(z, x, core, y):
    return ((z % NZ * NX + x % NX) * NC + core) * NY + y % NY


def groups_spread():
    return [
        [device(z + FIRST_Z, x, core, y) for z in range(NZ) for x in pair for core in range(NC)]
        for pair in SHARERS
        for y in range(NY)
    ]


def groups_turn():
    return [
        [device(z, x, core, y + FIRST_Y) for x in pair for y in range(NY)]
        for z in range(NZ)
        for core in range(NC)
        for pair in CLASSES
    ]


def groups_merge():
    return [
        [device(z + LAST_Z, x, core, y) for z in range(NZ) for x in pair]
        for core in range(NC)
        for y in range(NY)
        for pair in CLASSES
    ]


def exchange(blocks, groups):
    axes = ("z", "x", "core", "tp")
    return lax.all_to_all(blocks, axes, 0, 0, axis_index_groups=groups, tiled=True)


def interleave(first, second):
    low = jnp.concatenate([first[:, :4], second[:, :4]], axis=1)
    high = jnp.concatenate([first[:, 4:], second[:, 4:]], axis=1)
    return low, high


def slots_kernel(query_ref, slots_ref):
    by_x = query_ref[...].astype(jnp.float32).reshape(NX, 8, HS)
    parts = []
    for upper, lower in CLASSES:
        parts += interleave(by_x[upper : upper + 1], by_x[lower : lower + 1])
    block = jnp.concatenate(parts, axis=0).reshape(PAIRS, HS).astype(jnp.bfloat16)
    for z in range(NZ):
        slots_ref[z] = block


def pack_kernel(count_ref, resp_ref, key_ref, value_ref, _, send_ref, sems):
    copies = [
        pltpu.make_async_copy(key_ref, send_ref.at[pl.ds(0, SLOTS)], sems.at[0]),
        pltpu.make_async_copy(value_ref, send_ref.at[pl.ds(SLOTS, SLOTS)], sems.at[1]),
    ]
    for copy in copies:
        copy.start()
    count = count_ref[0]
    high = count // COUNT_BASE
    row = lax.broadcasted_iota(jnp.int32, (16, HS), 0)
    tail = jnp.where(row == 0, high, jnp.where(row == 1, count - high * COUNT_BASE, resp_ref[0]))
    send_ref[2 * SLOTS : SEND_ROWS, :] = tail.astype(jnp.float32).astype(jnp.bfloat16)
    for copy in copies:
        copy.wait()


def turn_kernel(groups_ref, turned_ref):
    for place in range(NY):
        block = groups_ref[(place + FIRST_Y - FIRST_Z) % NZ]
        for x in range(2):
            turned_ref[x, place] = block


def widen_into(wide_ref, ref):
    wide_ref[:, :HS] = ref[SLOTS : 2 * SLOTS, :]
    wide_ref[:, HS:] = jnp.ones((SLOTS, HS), jnp.bfloat16)


def tail_rows(ref):
    return ref[2 * SLOTS : SEND_ROWS, :].astype(jnp.float32)


def bias_row(ref):
    tail = tail_rows(ref)
    count = tail[0:1] * COUNT_BASE + tail[1:2]
    count = jnp.concatenate([count] * (SLOTS // HS), axis=1).astype(jnp.int32)
    return jnp.where(lane_ids((1, SLOTS)) < count, 0.0, MASKED)


def one_block(q, ref, wide_ref, bias):
    scores = lax.dot_general(
        q, ref[:SLOTS, :], (((1,), (1,)), ((), ())), preferred_element_type=jnp.float32
    )
    scores = scores + bias
    peak = jnp.max(scores, axis=1, keepdims=True)
    weights = jnp.exp2((scores - peak) * EXP2_SCALE).astype(jnp.bfloat16)
    both = jnp.dot(weights, wide_ref[...], preferred_element_type=jnp.float32)
    return both[:, :HS], both[:, HS:], jnp.broadcast_to(peak, (TILE, HS))


def combine(found, ref):
    out, total = 0.0, 0.0
    for block_out, block_sum, peak in found:
        scale = jnp.exp2((peak - ref) * EXP2_SCALE)
        out = out + block_out * scale
        total = total + block_sum * scale
    return out, total


def query_tile(q_ref, step):
    return q_ref[:, 2 * step : 2 * step + 2].reshape(TILE, HS)


def attend_kernel(q_ref, own_ref, near_ref, out_ref, own_wide_ref, near_wide_ref):
    widen_into(own_wide_ref, own_ref)
    widen_into(near_wide_ref, near_ref)
    blocks = ((own_ref, own_wide_ref), (near_ref, near_wide_ref))
    biases = [bias_row(ref) for ref, _ in blocks]
    for step in range(TILES):
        q = query_tile(q_ref, step)
        found = [one_block(q, *block, bias) for block, bias in zip(blocks, biases)]
        peak = jnp.maximum(found[0][2], found[1][2])
        out, total = combine(found, peak)
        out_ref[0, step] = out
        out_ref[1, step] = total
        out_ref[2, step] = peak


def finish_kernel(q_ref, got_ref, far_ref, so_far_ref, out_ref, got_wide_ref, far_wide_ref):
    widen_into(got_wide_ref, got_ref)
    widen_into(far_wide_ref, far_ref)
    got_bias, far_bias = bias_row(got_ref), bias_row(far_ref)
    resp = tail_rows(far_ref)[2:3]
    part = lane_ids((TILE, HS)) // PAIRS
    pair = lax.broadcasted_iota(jnp.int32, (4, PAIRS, HS), 1)
    diagonal = lane_ids((4, PAIRS, HS)) % PAIRS == pair
    sub = lax.broadcasted_iota(jnp.int32, (4, 8, HS), 1)

    def by_slot(x):
        x = x.reshape(8, 2, 8, HS)
        low, high = interleave(x[:, 0], x[:, 1])
        x = jnp.stack([low.reshape(2, 2, 2, 8, HS), high.reshape(2, 2, 2, 8, HS)], axis=1)
        return x.transpose(2, 1, 0, 3, 4, 5).reshape(4, PAIRS, HS)

    for step in range(TILES):
        q = query_tile(q_ref, step)
        found = [
            (so_far_ref[0, step], so_far_ref[1, step], so_far_ref[2, step]),
            one_block(q, got_ref, got_wide_ref, got_bias),
            one_block(q, far_ref, far_wide_ref, far_bias),
        ]
        ref = jnp.maximum(jnp.maximum(found[0][2], found[1][2]), found[2][2]).astype(jnp.bfloat16).astype(jnp.float32)
        out, total = combine(found, ref)
        high = total.astype(jnp.bfloat16).astype(jnp.float32)
        stats = jnp.where(part == 1, high, jnp.where(part == 2, total - high, resp))
        stats = jnp.where(part == 0, ref, stats)
        stats = jnp.where(diagonal, by_slot(stats), 0.0)
        stats = jnp.sum(stats, axis=1, keepdims=True)
        stats = jnp.where(sub == 0, stats, 0.0)
        full = jnp.concatenate([by_slot(out), stats], axis=1).reshape(4 * SLOT_ROWS, HS)
        place = (2 * step + FIRST_Y - LAST_Z) % NZ * 2 * SLOT_ROWS
        out_ref[place : place + 4 * SLOT_ROWS, :] = full.astype(jnp.bfloat16)


def merge_kernel(parts_ref, out_ref):
    parts = parts_ref[...].astype(jnp.float32).reshape(SRC, SLOT_ROWS, HS)
    resp = parts[0, PAIRS : PAIRS + 1, 3 * PAIRS : 3 * PAIRS + 1].astype(jnp.int32)
    stats = parts[:, PAIRS, :]
    stats = jnp.concatenate([stats, jnp.zeros((HS - SRC, HS), jnp.float32)], axis=0).T
    valid = lane_ids((PAIRS, HS)) < SRC
    peaks = jnp.where(valid, stats[:PAIRS], -jnp.inf)
    sums = stats[PAIRS : 2 * PAIRS] + stats[2 * PAIRS : 3 * PAIRS]
    peak = jnp.max(peaks, axis=1, keepdims=True)
    scale = jnp.exp2((peaks - peak) * EXP2_SCALE)
    denom = jnp.sum(scale * sums, axis=1, keepdims=True)
    numer = parts[0, :PAIRS] * scale[:, 0:1]
    for src in range(1, SRC):
        numer = numer + parts[src, :PAIRS] * scale[:, src : src + 1]
    result = numer / denom
    rows = PAIRS // 8
    row = lax.broadcasted_iota(jnp.int32, (rows, HS), 0)
    live = row + rows * lax.axis_index(("z", "x", "core")) < resp
    for place in range(8):
        block = result[rows * place : rows * (place + 1)]
        head = NC * HEAD_X[place // NC] + place % NC
        out_ref[:, HS * head : HS * (head + 1)] = jnp.where(live, block, 0.0).astype(jnp.bfloat16)


VMEM = pl.BlockSpec(memory_space=pltpu.VMEM)
SMEM = pl.BlockSpec(memory_space=pltpu.SMEM)
HBM = pl.BlockSpec(memory_space=pltpu.HBM)


def query_slots(queries):
    return pl.pallas_call(
        slots_kernel,
        out_shape=jax.ShapeDtypeStruct((NZ, PAIRS, HS), jnp.bfloat16),
        in_specs=[VMEM],
        out_specs=VMEM,
        compiler_params=pltpu.CompilerParams(vmem_limit_bytes=2**20),
    )(queries)


def pack(counts, resp_len, keys, values, after):
    return pl.pallas_call(
        pack_kernel,
        out_shape=jax.ShapeDtypeStruct((SEND_ROWS, HS), jnp.bfloat16),
        in_specs=[SMEM, SMEM, HBM, HBM, HBM],
        out_specs=VMEM,
        scratch_shapes=[pltpu.SemaphoreType.DMA((2,))],
        compiler_params=pltpu.CompilerParams(vmem_limit_bytes=2 * 2**20),
        cost_estimate=pl.CostEstimate(flops=0, bytes_accessed=2**23, transcendentals=0),
    )(counts, resp_len, keys, values, after)


def turn(groups):
    return pl.pallas_call(
        turn_kernel,
        out_shape=jax.ShapeDtypeStruct((2, NY, PAIRS, HS), jnp.bfloat16),
        in_specs=[VMEM],
        out_specs=VMEM,
        compiler_params=pltpu.CompilerParams(vmem_limit_bytes=2**20),
        cost_estimate=pl.CostEstimate(flops=2**36, bytes_accessed=2**21, transcendentals=0),
    )(groups)


def attend(spread, own, near):
    return pl.pallas_call(
        attend_kernel,
        out_shape=jax.ShapeDtypeStruct((3, TILES, TILE, HS), jnp.float32),
        in_specs=[VMEM] * 3,
        out_specs=VMEM,
        scratch_shapes=[pltpu.VMEM((SLOTS, 2 * HS), jnp.bfloat16)] * 2,
        compiler_params=pltpu.CompilerParams(vmem_limit_bytes=12 * 2**20),
        cost_estimate=pl.CostEstimate(flops=2**34, bytes_accessed=2**21, transcendentals=0),
    )(spread, own, near)


def finish(spread, got, far, so_far):
    return pl.pallas_call(
        finish_kernel,
        out_shape=jax.ShapeDtypeStruct((SRC * SLOT_ROWS, HS), jnp.bfloat16),
        in_specs=[VMEM] * 4,
        out_specs=VMEM,
        scratch_shapes=[pltpu.VMEM((SLOTS, 2 * HS), jnp.bfloat16)] * 2,
        compiler_params=pltpu.CompilerParams(vmem_limit_bytes=8 * 2**20),
    )(spread, got, far, so_far)


def merge(parts):
    return pl.pallas_call(
        merge_kernel,
        out_shape=jax.ShapeDtypeStruct((4, 8 * HS), jnp.bfloat16),
        in_specs=[VMEM],
        out_specs=VMEM,
        compiler_params=pltpu.CompilerParams(vmem_limit_bytes=4 * 2**20),
    )(parts)


def local(queries, keys, values, counts, resp_len):
    swap_cores = [(0, 1), (1, 0)]
    swap_chips = [way for a, b in SHARERS for way in ((a, b), (b, a))]
    with jax.named_scope("query_spread"):
        slots = query_slots(queries)
        groups = exchange(slots.reshape(NZ * 4, 8, HS), groups_spread()).reshape(NZ, PAIRS, HS)
    with jax.named_scope("block_exchange"):
        own = pack(counts, resp_len, keys, values, slots)
        near = lax.ppermute(own, "x", swap_chips)
        got = lax.ppermute(own, "core", swap_cores)
        far = lax.ppermute(near, "core", swap_cores)
    groups, own = lax.optimization_barrier((groups, own))
    with jax.named_scope("query_turn"):
        groups = turn(groups).reshape(SRC, PAIRS, HS)
        spread = exchange(groups, groups_turn()).reshape(2, NY, PAIRS, HS)
    with jax.named_scope("attend"):
        so_far = attend(spread, own, near)
        parts = finish(spread, got, far, so_far)
    with jax.named_scope("merge"):
        parts = exchange(parts.reshape(SRC, SLOT_ROWS, HS), groups_merge())
        return merge(parts.reshape(SRC * SLOT_ROWS, HS))


def solution(mesh):
    grid = Mesh(mesh.devices.reshape(NZ, NX, NC, NY), ("z", "x", "core", "tp"))
    ctx = ("z", "x", "core")
    in_specs = (P("tp", ctx), P(ctx, "tp"), P(ctx, "tp"), P(ctx), P())
    return jax.shard_map(
        local, mesh=grid, in_specs=in_specs, out_specs=P(ctx, "tp"), check_vma=False
    )
```

time: 59.1 us -> 56.1 us (0.949)
  blocking collectives: 34.1 us -> 14.4 us
  starting transfers between devices: 11.4 us -> 28.9 us
  waiting for transfers between devices: 5.9 us -> 2.05 us
  Pallas kernels: 4.44 us -> 6.2 us
  local copies, waits for them, and re-layouts: 1.45 us -> 2.59 us
    all_to_all x2 -> x1, blocking collectives: 34.1 us -> 14.4 us  [exchange(): lax.all_to_all(blocks, axes, 0, 0, axis_index_groups=groups, tiled=True)]
    all_to_all x1 -> x2, starting transfers between devices: 9.5 us -> 21.7 us  [exchange(): lax.all_to_all(blocks, axes, 0, 0, axis_index_groups=groups, tiled=True)]
    ppermute x1 -> x3, starting transfers between devices: 1.92 us -> 7.2 us  [the longest x1 3.38 us: local(): near = lax.ppermute(own, 'x', swap_chips)]
    all_to_all x1 -> x2, waiting for transfers between devices: 5.89 us -> 1.21 us  [exchange(): lax.all_to_all(blocks, axes, 0, 0, axis_index_groups=groups, tiled=True)]
    unnamed x6, local copies, waits for them, and re-layouts: 0.7 us -> 2.59 us
    pallas_call x3 -> x4, Pallas kernels: 3.22 us -> 5.06 us  [the longest x1 1.94 us: finish(): pl.pallas_call(finish_kernel, out_shape=jax.ShapeDtypeStruct((SRC * SLOT_...]
    ppermute x1 -> x3, waiting for transfers between devices: 0.01 us -> 0.84 us  [the longest x1 0.83 us: local(): near = lax.ppermute(own, 'x', swap_chips)]
    broadcast_in_dim x1 -> x0, local copies, waits for them, and re-layouts: 0.74 us -> none  [local(): jnp.broadcast_to(groups[None], (NX, NY, PAIRS, HS)).reshape(SRC, PAIRS, HS)]
  transfers between devices with their start and end apart: 2 -> 5, of which waited for: 1 -> 2; matrix products, arithmetic and copies ran while one was open for 0% -> 0% of each run, Pallas kernels for 0% -> 5%
where the time goes in v8:
time: 56.1 us; the launch traced here: 55.5 us
  starting transfers between devices  28.9 us (52%)
  blocking collectives  14.4 us (26%)
  Pallas kernels  6.2 us (11%)
  local copies, waits for them, and re-layouts  2.59 us (5%)
  waiting for transfers between devices  2.05 us (4%)
  between operations  1.39 us (2%)
    all_to_all x2, starting transfers between devices, exchange(): lax.all_to_all(blocks, axes, 0, 0, axis_index_groups=groups, tiled=True)  21.7 us
    all_to_all x1, blocking collectives, exchange(): lax.all_to_all(blocks, axes, 0, 0, axis_index_groups=groups, tiled=True)  14.4 us
    ppermute x1, starting transfers between devices, local(): near = lax.ppermute(own, 'x', swap_chips)  3.38 us
    unnamed x6, local copies, waits for them, and re-layouts  2.59 us
    pallas_call x1, Pallas kernels, finish(): pl.pallas_call(finish_kernel, out_shape=jax.ShapeDtypeStruct((SRC * SLOT_...  1.94 us
    ppermute x1, starting transfers between devices, local(): far = lax.ppermute(near, 'core', swap_cores)  1.91 us
    ppermute x1, starting transfers between devices, local(): got = lax.ppermute(own, 'core', swap_cores)  1.91 us
    pallas_call x1, Pallas kernels, attend(): pl.pallas_call(attend_kernel, out_shape=jax.ShapeDtypeStruct((3, TILES, T...  1.83 us
  transfers between devices with their start and end apart: 5, of which 2 were waited for; matrix products, arithmetic and copies ran while one was open for 0% of the time, Pallas kernels for 5%

profile of v8, /device:TPU:6, one launch (start us, length us, event | category | flops | bytes accessed | tf_op | source)
XLA Modules:
  0.0 55.5 jit_solution(13443117250556593846)
XLA Ops:
  0.0 0.0 copy-start.2
  0.0 0.7 %copy-done.2 = bf16[32,128]{1,0:T(8,128)(2,1)S(1)} copy-done((bf16[32,128]{1,0:T(8,128)(2,1)S(1)}, bf16[32,128]{1,0:T(8,128)(2,1)}, u32[]{:S(2)}) %copy-start.2) | copy-done | bytes 8216
  0.7 0.6 %query_spread.1._ = bf16[8,32,128]{2,1,0:T(8,128)(2,1)} custom-call(bf16[32,128]{1,0:T(8,128)(2,1)S(1)} %copy-done.2), custom_call_target="tpu_custom_call" | custom-call | tf_op jit(solution)/shard_map/query_spread/pallas_call | solution.py:226
  1.3 12.6 %all-to-all-start = ((bf16[32,8,128]{2,1,0:T(8,128)(2,1)}), bf16[32,8,128]{2,1,0:T(8,128)(2,1)S(1)}, u32[]{:S(2)}, u32[]{:S(2)}) async-start(bf16[32,8,128]{2,1,0:T(8,128)(2,1)} %bitcast), calls=%async_computation | async-start | bytes 131072 | tf_op jit(solution)/shard_map/query_spread/all_to_all | solution.py:63
  15.2 0.0 copy-start
  15.2 0.9 %copy-done = bf16[1024,128]{1,0:T(8,128)(2,1)S(1)} copy-done((bf16[1024,128]{1,0:T(8,128)(2,1)S(1)}, bf16[1024,128]{1,0:T(8,128)(2,1)}, u32[]{:S(2)}) %copy-start) | copy-done | bytes 262168
  16.1 0.0 copy-start.1
  16.1 0.9 %copy-done.1 = bf16[1024,128]{1,0:T(8,128)(2,1)S(1)} copy-done((bf16[1024,128]{1,0:T(8,128)(2,1)S(1)}, bf16[1024,128]{1,0:T(8,128)(2,1)}, u32[]{:S(2)}) %copy-start.1) | copy-done | bytes 262168
  17.1 0.1 block_exchange.1.own_ref
  17.2 3.4 %collective-permute-start.1 = (bf16[2064,128]{1,0:T(8,128)(2,1)S(1)}, bf16[2064,128]{1,0:T(8,128)(2,1)S(1)}, u32[]{:S(2)}, u32[]{:S(2)}) collective-permute-start(bf16[2064,128]{1,0:T(8,128)(2,1)S(1)} %block_exchange.1.own_ref), channel_id=1, source_target_pairs={{0,16},{16,0},{48,32},{32,48},{1,17},{17,1},{49,33},{33,49},{2,18}... | collective-permute-start | bytes 1585160 | tf_op jit(solution)/shard_map/block_exchange/ppermute | solution.py:299
  20.6 0.0 all-to-all-done
  20.6 0.7 %query_turn.1 = bf16[2,8,32,128]{3,2,1,0:T(8,128)(2,1)} custom-call(bf16[8,32,128]{2,1,0:T(8,128)(2,1)S(1)} %bitcast.10), custom_call_target="tpu_custom_call" | custom-call | flops 68719476736 | bytes 2097152 | tf_op jit(solution)/shard_map/query_turn/pallas_call | solution.py:248
  21.2 9.1 %all-to-all-start.1 = ((bf16[16,32,128]{2,1,0:T(8,128)(2,1)}), bf16[16,32,128]{2,1,0:T(8,128)(2,1)S(1)}, u32[]{:S(2)}, u32[]{:S(2)}) async-start(bf16[16,32,128]{2,1,0:T(8,128)(2,1)} %bitcast.2), calls=%async_computation.1 | async-start | bytes 262144 | tf_op jit(solution)/shard_map/query_turn/all_to_all | solution.py:63
  30.4 1.9 %collective-permute-start = (bf16[2064,128]{1,0:T(8,128)(2,1)S(1)}, bf16[2064,128]{1,0:T(8,128)(2,1)S(1)}, u32[]{:S(2)}, u32[]{:S(2)}) collective-permute-start(bf16[2064,128]{1,0:T(8,128)(2,1)S(1)} %block_exchange.1.own_ref), channel_id=1, source_target_pairs={{0,8},{8,0},{1,9},{9,1},{2,10},{10,2},{3,11},{11,3},{4,12},{12,4},... | collective-permute-start | bytes 1585160 | tf_op jit(solution)/shard_map/block_exchange/ppermute | solution.py:300
  32.3 0.8 %collective-permute-done.1.near_ref = bf16[2064,128]{1,0:T(8,128)(2,1)S(1)} collective-permute-done((bf16[2064,128]{1,0:T(8,128)(2,1)S(1)}, bf16[2064,128]{1,0:T(8,128)(2,1)S(1)}, u32[]{:S(2)}, u32[]{:S(2)}) %collective-permute-start.1) | collective-permute-done | bytes 528416 | tf_op jit(solution)/shard_map/block_exchange/ppermute | solution.py:299
  33.1 1.9 %collective-permute-start.2 = (bf16[2064,128]{1,0:T(8,128)(2,1)S(1)}, bf16[2064,128]{1,0:T(8,128)(2,1)S(1)}, u32[]{:S(2)}, u32[]{:S(2)}) collective-permute-start(bf16[2064,128]{1,0:T(8,128)(2,1)S(1)} %collective-permute-done.1.near_ref), channel_id=1, source_target_pairs={{0,8},{8,0},{1,9},{9,1},{2,10},{10,2},{3,11},{11,3},{4,12},{12,4},... | collective-permute-start | bytes 1585160 | tf_op jit(solution)/shard_map/block_exchange/ppermute | solution.py:301
  35.0 1.2 %all-to-all-done.1 = bf16[16,32,128]{2,1,0:T(8,128)(2,1)S(1)} async-done(((bf16[16,32,128]{2,1,0:T(8,128)(2,1)}), bf16[16,32,128]{2,1,0:T(8,128)(2,1)S(1)}, u32[]{:S(2)}, u32[]{:S(2)}) %all-to-all-start.1) | async-done | bytes 131104 | tf_op jit(solution)/shard_map/query_turn/all_to_all | solution.py:63
  36.2 1.8 %attend.2.so_far_ref = f32[3,4,128,128]{3,2,1,0:T(8,128)S(1)} custom-call(bf16[2,8,32,128]{3,2,1,0:T(8,128)(2,1)S(1)} %bitcast.8, bf16[2064,128]{1,0:T(8,128)(2,1)S(1)} %block_exchange.1.own_ref, bf16[2064,128]{1,0:T(8,128)(2,1)S(1)} %collective-permute-done.1.near_ref), custom_call_target="tpu_custom_call" | custom-call | flops 17179869184 | bytes 2097152 | tf_op jit(solution)/shard_map/attend/pallas_call | solution.py:259
  38.1 0.0 collective-permute-done.got_ref
  38.1 0.0 collective-permute-done.2.far_ref
  38.1 1.9 %attend.3 = bf16[640,128]{1,0:T(8,128)(2,1)S(1)} custom-call(bf16[2,8,32,128]{3,2,1,0:T(8,128)(2,1)S(1)} %bitcast.9, bf16[2064,128]{1,0:T(8,128)(2,1)S(1)} %collective-permute-done.got_ref, bf16[2064,128]{1,0:T(8,128)(2,1)S(1)} %collective-permute-done.2.far_ref, f32[3,4,128,128]{3,2,1,0:T(8,128)S(1)} %attend.2.so_far_ref), custom_call_target="tpu_custom_call" | custom-call | tf_op jit(solution)/shard_map/attend/pallas_call | solution.py:271
  40.1 14.4 %all_to_all.15 = bf16[16,40,128]{2,1,0:T(8,128)(2,1)S(1)} all-to-all(bf16[16,40,128]{2,1,0:T(8,128)(2,1)S(1)} %bitcast.6), channel_id=1, replica_groups={{304,256,368,320,432,384,496,448,48,0,112,64,176,128,240,192},{288,272,..., dimensions={0} | all-to-all | bytes 327680 | tf_op jit(solution)/shard_map/merge/all_to_all | solution.py:63
  54.5 1.1 %merge.1 = bf16[4,1024]{1,0:T(4,128)(2,1)} custom-call(bf16[640,128]{1,0:T(8,128)(2,1)S(1)} %bitcast.7), custom_call_target="tpu_custom_call" | custom-call | tf_op jit(solution)/shard_map/merge/pallas_call | solution.py:282
Async XLA Ops:
  0.0 0.7 %copy-start.2 = (bf16[32,128]{1,0:T(8,128)(2,1)S(1)}, bf16[32,128]{1,0:T(8,128)(2,1)}, u32[]{:S(2)}) copy-start(bf16[32,128]{1,0:T(8,128)(2,1)} %query_ref.1) | copy-start | bytes 24580
  1.3 19.2 %all-to-all-start = ((bf16[32,8,128]{2,1,0:T(8,128)(2,1)}), bf16[32,8,128]{2,1,0:T(8,128)(2,1)S(1)}, u32[]{:S(2)}, u32[]{:S(2)}) async-start(bf16[32,8,128]{2,1,0:T(8,128)(2,1)} %bitcast), calls=%async_computation | async-start | bytes 131072 | tf_op jit(solution)/shard_map/query_spread/all_to_all | solution.py:63
  15.2 1.0 %copy-start = (bf16[1024,128]{1,0:T(8,128)(2,1)S(1)}, bf16[1024,128]{1,0:T(8,128)(2,1)}, u32[]{:S(2)}) copy-start(bf16[1024,128]{1,0:T(8,128)(2,1)} %key_ref.1) | copy-start | bytes 786436
  16.1 0.9 %copy-start.1 = (bf16[1024,128]{1,0:T(8,128)(2,1)S(1)}, bf16[1024,128]{1,0:T(8,128)(2,1)}, u32[]{:S(2)}) copy-start(bf16[1024,128]{1,0:T(8,128)(2,1)} %value_ref.1) | copy-start | bytes 786436
  17.2 16.0 %collective-permute-start.1 = (bf16[2064,128]{1,0:T(8,128)(2,1)S(1)}, bf16[2064,128]{1,0:T(8,128)(2,1)S(1)}, u32[]{:S(2)}, u32[]{:S(2)}) collective-permute-start(bf16[2064,128]{1,0:T(8,128)(2,1)S(1)} %block_exchange.1.own_ref), channel_id=1, source_target_pairs={{0,16},{16,0},{48,32},{32,48},{1,17},{17,1},{49,33},{33,49},{2,18}... | collective-permute-start | bytes 1585160 | tf_op jit(solution)/shard_map/block_exchange/ppermute | solution.py:299
  21.2 15.0 %all-to-all-start.1 = ((bf16[16,32,128]{2,1,0:T(8,128)(2,1)}), bf16[16,32,128]{2,1,0:T(8,128)(2,1)S(1)}, u32[]{:S(2)}, u32[]{:S(2)}) async-start(bf16[16,32,128]{2,1,0:T(8,128)(2,1)} %bitcast.2), calls=%async_computation.1 | async-start | bytes 262144 | tf_op jit(solution)/shard_map/query_turn/all_to_all | solution.py:63
  30.4 7.7 %collective-permute-start = (bf16[2064,128]{1,0:T(8,128)(2,1)S(1)}, bf16[2064,128]{1,0:T(8,128)(2,1)S(1)}, u32[]{:S(2)}, u32[]{:S(2)}) collective-permute-start(bf16[2064,128]{1,0:T(8,128)(2,1)S(1)} %block_exchange.1.own_ref), channel_id=1, source_target_pairs={{0,8},{8,0},{1,9},{9,1},{2,10},{10,2},{3,11},{11,3},{4,12},{12,4},... | collective-permute-start | bytes 1585160 | tf_op jit(solution)/shard_map/block_exchange/ppermute | solution.py:300
  33.1 5.0 %collective-permute-start.2 = (bf16[2064,128]{1,0:T(8,128)(2,1)S(1)}, bf16[2064,128]{1,0:T(8,128)(2,1)S(1)}, u32[]{:S(2)}, u32[]{:S(2)}) collective-permute-start(bf16[2064,128]{1,0:T(8,128)(2,1)S(1)} %collective-permute-done.1.near_ref), channel_id=1, source_target_pairs={{0,8},{8,0},{1,9},{9,1},{2,10},{10,2},{3,11},{11,3},{4,12},{12,4},... | collective-permute-start | bytes 1585160 | tf_op jit(solution)/shard_map/block_exchange/ppermute | solution.py:301

commit v9 on v8

--- a/solution.py
+++ b/solution.py
@@ -69,30 +69,43 @@
     return low, high
 
 
-def slots_kernel(query_ref, slots_ref):
-    by_x = query_ref[...].astype(jnp.float32).reshape(NX, 8, HS)
+def pack_kernel(query_ref, key_ref, value_ref, slots_ref, send_ref, rows, slots, both, sems):
+    def copy(source, target, which):
+        made = pltpu.make_async_copy(source, target, sems.at[which])
+        made.start()
+        return made
+
+    first, second = pl.ds(0, SLOTS), pl.ds(SLOTS, SLOTS)
+    loads = (
+        copy(query_ref, rows, 0),
+        copy(key_ref, both.at[first], 1),
+        copy(value_ref, both.at[second], 2),
+    )
+    loads[0].wait()
+    by_x = rows[...].astype(jnp.float32).reshape(NX, 8, HS)
     parts = []
     for upper, lower in CLASSES:
         parts += interleave(by_x[upper : upper + 1], by_x[lower : lower + 1])
     block = jnp.concatenate(parts, axis=0).reshape(PAIRS, HS).astype(jnp.bfloat16)
     for z in range(NZ):
-        slots_ref[z] = block
-
-
-def pack_kernel(count_ref, resp_ref, key_ref, value_ref, _, send_ref, sems):
-    copies = [
-        pltpu.make_async_copy(key_ref, send_ref.at[pl.ds(0, SLOTS)], sems.at[0]),
-        pltpu.make_async_copy(value_ref, send_ref.at[pl.ds(SLOTS, SLOTS)], sems.at[1]),
-    ]
-    for copy in copies:
-        copy.start()
+        slots[z] = block
+    stores = [copy(slots, slots_ref, 3)]
+    for which, part in enumerate((first, second)):
+        loads[1 + which].wait()
+        stores.append(copy(both.at[part], send_ref.at[part], 4 + which))
+    for store in stores:
+        store.wait()
+
+
+def note_kernel(count_ref, resp_ref, _, send_ref, tail_ref, sem):
     count = count_ref[0]
+    row = lax.broadcasted_iota(jnp.int32, (16, HS), 0)
     high = count // COUNT_BASE
-    row = lax.broadcasted_iota(jnp.int32, (16, HS), 0)
     tail = jnp.where(row == 0, high, jnp.where(row == 1, count - high * COUNT_BASE, resp_ref[0]))
-    send_ref[2 * SLOTS : SEND_ROWS, :] = tail.astype(jnp.float32).astype(jnp.bfloat16)
-    for copy in copies:
-        copy.wait()
+    tail_ref[...] = tail.astype(jnp.float32).astype(jnp.bfloat16)
+    copy = pltpu.make_async_copy(tail_ref, send_ref.at[pl.ds(2 * SLOTS, 16)], sem)
+    copy.start()
+    copy.wait()
 
 
 def turn_kernel(groups_ref, turned_ref):
@@ -222,26 +235,35 @@
 HBM = pl.BlockSpec(memory_space=pltpu.HBM)
 
 
-def query_slots(queries):
-    return pl.pallas_call(
-        slots_kernel,
-        out_shape=jax.ShapeDtypeStruct((NZ, PAIRS, HS), jnp.bfloat16),
-        in_specs=[VMEM],
-        out_specs=VMEM,
-        compiler_params=pltpu.CompilerParams(vmem_limit_bytes=2**20),
-    )(queries)
-
-
-def pack(counts, resp_len, keys, values, after):
+def pack(queries, keys, values):
     return pl.pallas_call(
         pack_kernel,
+        out_shape=(
+            jax.ShapeDtypeStruct((NZ, PAIRS, HS), jnp.bfloat16),
+            jax.ShapeDtypeStruct((SEND_ROWS, HS), jnp.bfloat16),
+        ),
+        in_specs=[HBM] * 3,
+        out_specs=(HBM, HBM),
+        scratch_shapes=[
+            pltpu.VMEM((PAIRS, HS), jnp.bfloat16),
+            pltpu.VMEM((NZ, PAIRS, HS), jnp.bfloat16),
+            pltpu.VMEM((2 * SLOTS, HS), jnp.bfloat16),
+            pltpu.SemaphoreType.DMA((6,)),
+        ],
+        compiler_params=pltpu.CompilerParams(vmem_limit_bytes=60 * 2**20),
+    )(queries, keys, values)
+
+
+def note(counts, resp_len, own):
+    return pl.pallas_call(
+        note_kernel,
         out_shape=jax.ShapeDtypeStruct((SEND_ROWS, HS), jnp.bfloat16),
-        in_specs=[SMEM, SMEM, HBM, HBM, HBM],
-        out_specs=VMEM,
-        scratch_shapes=[pltpu.SemaphoreType.DMA((2,))],
-        compiler_params=pltpu.CompilerParams(vmem_limit_bytes=2 * 2**20),
-        cost_estimate=pl.CostEstimate(flops=0, bytes_accessed=2**23, transcendentals=0),
-    )(counts, resp_len, keys, values, after)
+        in_specs=[SMEM, SMEM, HBM],
+        out_specs=HBM,
+        input_output_aliases={2: 0},
+        scratch_shapes=[pltpu.VMEM((16, HS), jnp.bfloat16), pltpu.SemaphoreType.DMA],
+        compiler_params=pltpu.CompilerParams(vmem_limit_bytes=60 * 2**20),
+    )(counts, resp_len, own)
 
 
 def turn(groups):
@@ -292,10 +314,10 @@
     swap_cores = [(0, 1), (1, 0)]
     swap_chips = [way for a, b in SHARERS for way in ((a, b), (b, a))]
     with jax.named_scope("query_spread"):
-        slots = query_slots(queries)
+        slots, own = pack(queries, keys, values)
         groups = exchange(slots.reshape(NZ * 4, 8, HS), groups_spread()).reshape(NZ, PAIRS, HS)
     with jax.named_scope("block_exchange"):
-        own = pack(counts, resp_len, keys, values, slots)
+        own = note(counts, resp_len, own)
         near = lax.ppermute(own, "x", swap_chips)
         got = lax.ppermute(own, "core", swap_cores)
         far = lax.ppermute(near, "core", swap_cores)

time: 56.1 us -> 55.7 us (level)
  local copies, waits for them, and re-layouts: 2.59 us -> 0.01 us
  Pallas kernels: 6.2 us -> 7.88 us
    unnamed x6 -> x2, local copies, waits for them, and re-layouts: 2.59 us -> 0.01 us
    pallas_call x2, Pallas kernels: 0.69 us -> 2.43 us  [the longest x1 1.82 us: pack(): pl.pallas_call(pack_kernel, out_shape=(jax.ShapeDtypeStruct((NZ, PAIRS, H...]
    all_to_all x2, waiting for transfers between devices: 1.21 us -> 1.9 us  [exchange(): lax.all_to_all(blocks, axes, 0, 0, axis_index_groups=groups, tiled=True)]
  transfers between devices with their start and end apart: 5 -> 5, of which waited for: 2 -> 3; matrix products, arithmetic and copies ran while one was open for 0% -> 0% of each run, Pallas kernels for 5% -> 6%
where the time goes in v9:
time: 55.7 us; the launch traced here: 55.1 us
  starting transfers between devices  28.9 us (52%)
  blocking collectives  14.5 us (26%)
  Pallas kernels  7.88 us (14%)
  waiting for transfers between devices  2.47 us (4%)
  between operations  1.38 us (2%)
    all_to_all x2, starting transfers between devices, exchange(): lax.all_to_all(blocks, axes, 0, 0, axis_index_groups=groups, tiled=True)  21.7 us
    all_to_all x1, blocking collectives, exchange(): lax.all_to_all(blocks, axes, 0, 0, axis_index_groups=groups, tiled=True)  14.5 us
    ppermute x1, starting transfers between devices, local(): near = lax.ppermute(own, 'x', swap_chips)  3.38 us
    pallas_call x1, Pallas kernels, finish(): pl.pallas_call(finish_kernel, out_shape=jax.ShapeDtypeStruct((SRC * SLOT_...  1.92 us
    ppermute x1, starting transfers between devices, local(): got = lax.ppermute(own, 'core', swap_cores)  1.92 us
    ppermute x1, starting transfers between devices, local(): far = lax.ppermute(near, 'core', swap_cores)  1.91 us
    all_to_all x2, waiting for transfers between devices, exchange(): lax.all_to_all(blocks, axes, 0, 0, axis_index_groups=groups, tiled=True)  1.9 us
    pallas_call x1, Pallas kernels, pack(): pl.pallas_call(pack_kernel, out_shape=(jax.ShapeDtypeStruct((NZ, PAIRS, H...  1.82 us
  transfers between devices with their start and end apart: 5, of which 3 were waited for; matrix products, arithmetic and copies ran while one was open for 0% of the time, Pallas kernels for 6%

profile of v9, /device:TPU:6, one launch (start us, length us, event | category | flops | bytes accessed | tf_op | source)
XLA Modules:
  0.0 55.1 jit_solution(17387291133230817109)
XLA Ops:
  0.0 1.8 %query_spread.1 = (bf16[8,32,128]{2,1,0:T(8,128)(2,1)}, bf16[2064,128]{1,0:T(8,128)(2,1)}) custom-call(bf16[32,128]{1,0:T(8,128)(2,1)} %query_ref.1, bf16[1024,128]{1,0:T(8,128)(2,1)} %key_ref.1, bf16[1024,128]{1,0:T(8,128)(2,1)} %value_ref.1), custom_call_target="tpu_custom_call" | custom-call | tf_op jit(solution)/shard_map/query_spread/pallas_call | solution.py:239
  1.8 12.6 %all-to-all-start = ((bf16[32,8,128]{2,1,0:T(8,128)(2,1)}), bf16[32,8,128]{2,1,0:T(8,128)(2,1)S(1)}, u32[]{:S(2)}, u32[]{:S(2)}) async-start(bf16[32,8,128]{2,1,0:T(8,128)(2,1)} %bitcast.11), calls=%async_computation | async-start | bytes 131072 | tf_op jit(solution)/shard_map/query_spread/all_to_all | solution.py:63
  15.7 0.6 %block_exchange.1.own_ref = bf16[2064,128]{1,0:T(8,128)(2,1)} custom-call(s32[1]{0:T(128)S(6)} %copy.8.count_ref, s32[1]{0:T(128)S(6)} %copy.9.resp_ref, bf16[2064,128]{1,0:T(8,128)(2,1)} %get-tuple-element.10._), custom_call_target="tpu_custom_call", output_to_operand_aliasing={{}: (2, {})} | custom-call | tf_op jit(solution)/shard_map/block_exchange/pallas_call | solution.py:258
  16.3 3.4 %collective-permute-start.1 = (bf16[2064,128]{1,0:T(8,128)(2,1)}, bf16[2064,128]{1,0:T(8,128)(2,1)S(1)}, u32[]{:S(2)}, u32[]{:S(2)}) collective-permute-start(bf16[2064,128]{1,0:T(8,128)(2,1)} %block_exchange.1.own_ref), channel_id=1, source_target_pairs={{0,16},{16,0},{48,32},{32,48},{1,17},{17,1},{49,33},{33,49},{2,18}... | collective-permute-start | bytes 1585160 | tf_op jit(solution)/shard_map/block_exchange/ppermute | solution.py:321
  19.7 0.5 all-to-all-done
  20.2 0.0 copy-start
  20.2 0.7 %query_turn.1 = bf16[2,8,32,128]{3,2,1,0:T(8,128)(2,1)} custom-call(bf16[8,32,128]{2,1,0:T(8,128)(2,1)S(1)} %bitcast.10), custom_call_target="tpu_custom_call" | custom-call | flops 68719476736 | bytes 2097152 | tf_op jit(solution)/shard_map/query_turn/pallas_call | solution.py:270
  20.9 9.1 %all-to-all-start.1 = ((bf16[16,32,128]{2,1,0:T(8,128)(2,1)}), bf16[16,32,128]{2,1,0:T(8,128)(2,1)S(1)}, u32[]{:S(2)}, u32[]{:S(2)}) async-start(bf16[16,32,128]{2,1,0:T(8,128)(2,1)} %bitcast.2), calls=%async_computation.1 | async-start | bytes 262144 | tf_op jit(solution)/shard_map/query_turn/all_to_all | solution.py:63
  30.0 0.0 copy-done
  30.0 1.9 %collective-permute-start = (bf16[2064,128]{1,0:T(8,128)(2,1)S(1)}, bf16[2064,128]{1,0:T(8,128)(2,1)S(1)}, u32[]{:S(2)}, u32[]{:S(2)}) collective-permute-start(bf16[2064,128]{1,0:T(8,128)(2,1)S(1)} %copy-done), channel_id=1, source_target_pairs={{0,8},{8,0},{1,9},{9,1},{2,10},{10,2},{3,11},{11,3},{4,12},{12,4},... | collective-permute-start | bytes 1585160 | tf_op jit(solution)/shard_map/block_exchange/ppermute | solution.py:322
  31.9 0.6 %collective-permute-done.1.near_ref = bf16[2064,128]{1,0:T(8,128)(2,1)S(1)} collective-permute-done((bf16[2064,128]{1,0:T(8,128)(2,1)}, bf16[2064,128]{1,0:T(8,128)(2,1)S(1)}, u32[]{:S(2)}, u32[]{:S(2)}) %collective-permute-start.1) | collective-permute-done | bytes 528416 | tf_op jit(solution)/shard_map/block_exchange/ppermute | solution.py:321
  32.5 1.9 %collective-permute-start.2 = (bf16[2064,128]{1,0:T(8,128)(2,1)S(1)}, bf16[2064,128]{1,0:T(8,128)(2,1)S(1)}, u32[]{:S(2)}, u32[]{:S(2)}) collective-permute-start(bf16[2064,128]{1,0:T(8,128)(2,1)S(1)} %collective-permute-done.1.near_ref), channel_id=1, source_target_pairs={{0,8},{8,0},{1,9},{9,1},{2,10},{10,2},{3,11},{11,3},{4,12},{12,4},... | collective-permute-start | bytes 1585160 | tf_op jit(solution)/shard_map/block_exchange/ppermute | solution.py:323
  34.4 1.4 %all-to-all-done.1 = bf16[16,32,128]{2,1,0:T(8,128)(2,1)S(1)} async-done(((bf16[16,32,128]{2,1,0:T(8,128)(2,1)}), bf16[16,32,128]{2,1,0:T(8,128)(2,1)S(1)}, u32[]{:S(2)}, u32[]{:S(2)}) %all-to-all-start.1) | async-done | bytes 131104 | tf_op jit(solution)/shard_map/query_turn/all_to_all | solution.py:63
  35.8 1.8 %attend.2.so_far_ref = f32[3,4,128,128]{3,2,1,0:T(8,128)S(1)} custom-call(bf16[2,8,32,128]{3,2,1,0:T(8,128)(2,1)S(1)} %bitcast.8, bf16[2064,128]{1,0:T(8,128)(2,1)S(1)} %copy-done, bf16[2064,128]{1,0:T(8,128)(2,1)S(1)} %collective-permute-done.1.near_ref), custom_call_target="tpu_custom_call" | custom-call | flops 17179869184 | bytes 2097152 | tf_op jit(solution)/shard_map/attend/pallas_call | solution.py:281
  37.6 0.0 collective-permute-done.got_ref
  37.6 0.0 collective-permute-done.2.far_ref
  37.7 1.9 %attend.3 = bf16[640,128]{1,0:T(8,128)(2,1)S(1)} custom-call(bf16[2,8,32,128]{3,2,1,0:T(8,128)(2,1)S(1)} %bitcast.9, bf16[2064,128]{1,0:T(8,128)(2,1)S(1)} %collective-permute-done.got_ref, bf16[2064,128]{1,0:T(8,128)(2,1)S(1)} %collective-permute-done.2.far_ref, f32[3,4,128,128]{3,2,1,0:T(8,128)S(1)} %attend.2.so_far_ref), custom_call_target="tpu_custom_call" | custom-call | tf_op jit(solution)/shard_map/attend/pallas_call | solution.py:293
  39.6 14.5 %all_to_all.15 = bf16[16,40,128]{2,1,0:T(8,128)(2,1)S(1)} all-to-all(bf16[16,40,128]{2,1,0:T(8,128)(2,1)S(1)} %bitcast.6), channel_id=1, replica_groups={{304,256,368,320,432,384,496,448,48,0,112,64,176,128,240,192},{288,272,..., dimensions={0} | all-to-all | bytes 327680 | tf_op jit(solution)/shard_map/merge/all_to_all | solution.py:63
  54.0 1.1 %merge.1 = bf16[4,1024]{1,0:T(4,128)(2,1)} custom-call(bf16[640,128]{1,0:T(8,128)(2,1)S(1)} %bitcast.7), custom_call_target="tpu_custom_call" | custom-call | tf_op jit(solution)/shard_map/merge/pallas_call | solution.py:304
Async XLA Ops:
  1.8 18.4 %all-to-all-start = ((bf16[32,8,128]{2,1,0:T(8,128)(2,1)}), bf16[32,8,128]{2,1,0:T(8,128)(2,1)S(1)}, u32[]{:S(2)}, u32[]{:S(2)}) async-start(bf16[32,8,128]{2,1,0:T(8,128)(2,1)} %bitcast.11), calls=%async_computation | async-start | bytes 131072 | tf_op jit(solution)/shard_map/query_spread/all_to_all | solution.py:63
  16.3 16.2 %collective-permute-start.1 = (bf16[2064,128]{1,0:T(8,128)(2,1)}, bf16[2064,128]{1,0:T(8,128)(2,1)S(1)}, u32[]{:S(2)}, u32[]{:S(2)}) collective-permute-start(bf16[2064,128]{1,0:T(8,128)(2,1)} %block_exchange.1.own_ref), channel_id=1, source_target_pairs={{0,16},{16,0},{48,32},{32,48},{1,17},{17,1},{49,33},{33,49},{2,18}... | collective-permute-start | bytes 1585160 | tf_op jit(solution)/shard_map/block_exchange/ppermute | solution.py:321
  20.2 9.8 %copy-start = (bf16[2064,128]{1,0:T(8,128)(2,1)S(1)}, bf16[2064,128]{1,0:T(8,128)(2,1)}, u32[]{:S(2)}) copy-start(bf16[2064,128]{1,0:T(8,128)(2,1)} %block_exchange.1.own_ref) | copy-start | bytes 1585156
  20.9 15.0 %all-to-all-start.1 = ((bf16[16,32,128]{2,1,0:T(8,128)(2,1)}), bf16[16,32,128]{2,1,0:T(8,128)(2,1)S(1)}, u32[]{:S(2)}, u32[]{:S(2)}) async-start(bf16[16,32,128]{2,1,0:T(8,128)(2,1)} %bitcast.2), calls=%async_computation.1 | async-start | bytes 262144 | tf_op jit(solution)/shard_map/query_turn/all_to_all | solution.py:63
  30.0 7.6 %collective-permute-start = (bf16[2064,128]{1,0:T(8,128)(2,1)S(1)}, bf16[2064,128]{1,0:T(8,128)(2,1)S(1)}, u32[]{:S(2)}, u32[]{:S(2)}) collective-permute-start(bf16[2064,128]{1,0:T(8,128)(2,1)S(1)} %copy-done), channel_id=1, source_target_pairs={{0,8},{8,0},{1,9},{9,1},{2,10},{10,2},{3,11},{11,3},{4,12},{12,4},... | collective-permute-start | bytes 1585160 | tf_op jit(solution)/shard_map/block_exchange/ppermute | solution.py:322
  32.5 5.2 %collective-permute-start.2 = (bf16[2064,128]{1,0:T(8,128)(2,1)S(1)}, bf16[2064,128]{1,0:T(8,128)(2,1)S(1)}, u32[]{:S(2)}, u32[]{:S(2)}) collective-permute-start(bf16[2064,128]{1,0:T(8,128)(2,1)S(1)} %collective-permute-done.1.near_ref), channel_id=1, source_target_pairs={{0,8},{8,0},{1,9},{9,1},{2,10},{10,2},{3,11},{11,3},{4,12},{12,4},... | collective-permute-start | bytes 1585160 | tf_op jit(solution)/shard_map/block_exchange/ppermute | solution.py:323

commit v10 on v9

--- a/solution.py
+++ b/solution.py
@@ -18,7 +18,7 @@
 SEND_ROWS = 2 * SLOTS + 16
 COUNT_BASE = 64
 MASKED = -1e30
-FIRST_Z, FIRST_Y, LAST_Z = 6, 4, 4
+FIRST_Z, FIRST_Y, LAST_Z = 5, 5, 5
 SHARERS = ((0, 1), (3, 2))
 CLASSES = ((3, 0), (2, 1))
 HEAD_X = (3, 2, 0, 1)
@@ -69,7 +69,9 @@
     return low, high
 
 
-def pack_kernel(query_ref, key_ref, value_ref, slots_ref, send_ref, rows, slots, both, sems):
+def pack_kernel(
+    count_ref, query_ref, key_ref, value_ref, slots_ref, send_ref, rows, slots, both, tail, sems
+):
     def copy(source, target, which):
         made = pltpu.make_async_copy(source, target, sems.at[which])
         made.start()
@@ -89,7 +91,11 @@
     block = jnp.concatenate(parts, axis=0).reshape(PAIRS, HS).astype(jnp.bfloat16)
     for z in range(NZ):
         slots[z] = block
-    stores = [copy(slots, slots_ref, 3)]
+    count = count_ref[0]
+    row = lax.broadcasted_iota(jnp.int32, (16, HS), 0)
+    high = count // COUNT_BASE
+    tail[...] = jnp.where(row == 0, high, count - high * COUNT_BASE).astype(jnp.float32).astype(jnp.bfloat16)
+    stores = [copy(slots, slots_ref, 3), copy(tail, send_ref.at[pl.ds(2 * SLOTS, 16)], 6)]
     for which, part in enumerate((first, second)):
         loads[1 + which].wait()
         stores.append(copy(both.at[part], send_ref.at[part], 4 + which))
@@ -97,18 +103,8 @@
         store.wait()
 
 
-def note_kernel(count_ref, resp_ref, _, send_ref, tail_ref, sem):
-    count = count_ref[0]
-    row = lax.broadcasted_iota(jnp.int32, (16, HS), 0)
-    high = count // COUNT_BASE
-    tail = jnp.where(row == 0, high, jnp.where(row == 1, count - high * COUNT_BASE, resp_ref[0]))
-    tail_ref[...] = tail.astype(jnp.float32).astype(jnp.bfloat16)
-    copy = pltpu.make_async_copy(tail_ref, send_ref.at[pl.ds(2 * SLOTS, 16)], sem)
-    copy.start()
-    copy.wait()
-
-
-def turn_kernel(groups_ref, turned_ref):
+def turn_kernel(resp_ref, groups_ref, turned_ref, noted_ref):
+    noted_ref[...] = jnp.full((8, HS), resp_ref[0], jnp.int32).astype(jnp.float32)
     for place in range(NY):
         block = groups_ref[(place + FIRST_Y - FIRST_Z) % NZ]
         for x in range(2):
@@ -170,11 +166,13 @@
         out_ref[2, step] = peak
 
 
-def finish_kernel(q_ref, got_ref, far_ref, so_far_ref, out_ref, got_wide_ref, far_wide_ref):
+def finish_kernel(
+    q_ref, got_ref, far_ref, so_far_ref, resp_ref, out_ref, got_wide_ref, far_wide_ref
+):
     widen_into(got_wide_ref, got_ref)
     widen_into(far_wide_ref, far_ref)
     got_bias, far_bias = bias_row(got_ref), bias_row(far_ref)
-    resp = tail_rows(far_ref)[2:3]
+    resp = resp_ref[0:1]
     part = lane_ids((TILE, HS)) // PAIRS
     pair = lax.broadcasted_iota(jnp.int32, (4, PAIRS, HS), 1)
     diagonal = lane_ids((4, PAIRS, HS)) % PAIRS == pair
@@ -235,46 +233,38 @@
 HBM = pl.BlockSpec(memory_space=pltpu.HBM)
 
 
-def pack(queries, keys, values):
+def pack(counts, queries, keys, values):
     return pl.pallas_call(
         pack_kernel,
         out_shape=(
             jax.ShapeDtypeStruct((NZ, PAIRS, HS), jnp.bfloat16),
             jax.ShapeDtypeStruct((SEND_ROWS, HS), jnp.bfloat16),
         ),
-        in_specs=[HBM] * 3,
+        in_specs=[SMEM, HBM, HBM, HBM],
         out_specs=(HBM, HBM),
         scratch_shapes=[
             pltpu.VMEM((PAIRS, HS), jnp.bfloat16),
             pltpu.VMEM((NZ, PAIRS, HS), jnp.bfloat16),
             pltpu.VMEM((2 * SLOTS, HS), jnp.bfloat16),
-            pltpu.SemaphoreType.DMA((6,)),
+            pltpu.VMEM((16, HS), jnp.bfloat16),
+            pltpu.SemaphoreType.DMA((7,)),
         ],
         compiler_params=pltpu.CompilerParams(vmem_limit_bytes=60 * 2**20),
-    )(queries, keys, values)
-
-
-def note(counts, resp_len, own):
-    return pl.pallas_call(
-        note_kernel,
-        out_shape=jax.ShapeDtypeStruct((SEND_ROWS, HS), jnp.bfloat16),
-        in_specs=[SMEM, SMEM, HBM],
-        out_specs=HBM,
-        input_output_aliases={2: 0},
-        scratch_shapes=[pltpu.VMEM((16, HS), jnp.bfloat16), pltpu.SemaphoreType.DMA],
-        compiler_params=pltpu.CompilerParams(vmem_limit_bytes=60 * 2**20),
-    )(counts, resp_len, own)
-
-
-def turn(groups):
+    )(counts, queries, keys, values)
+
+
+def turn(resp_len, groups):
     return pl.pallas_call(
         turn_kernel,
-        out_shape=jax.ShapeDtypeStruct((2, NY, PAIRS, HS), jnp.bfloat16),
-        in_specs=[VMEM],
-        out_specs=VMEM,
+        out_shape=(
+            jax.ShapeDtypeStruct((2, NY, PAIRS, HS), jnp.bfloat16),
+            jax.ShapeDtypeStruct((8, HS), jnp.float32),
+        ),
+        in_specs=[SMEM, VMEM],
+        out_specs=(VMEM, VMEM),
         compiler_params=pltpu.CompilerParams(vmem_limit_bytes=2**20),
         cost_estimate=pl.CostEstimate(flops=2**36, bytes_accessed=2**21, transcendentals=0),
-    )(groups)
+    )(resp_len, groups)
 
 
 def attend(spread, own, near):
@@ -289,15 +279,15 @@
     )(spread, own, near)
 
 
-def finish(spread, got, far, so_far):
+def finish(spread, got, far, so_far, resp):
     return pl.pallas_call(
         finish_kernel,
         out_shape=jax.ShapeDtypeStruct((SRC * SLOT_ROWS, HS), jnp.bfloat16),
-        in_specs=[VMEM] * 4,
+        in_specs=[VMEM] * 5,
         out_specs=VMEM,
         scratch_shapes=[pltpu.VMEM((SLOTS, 2 * HS), jnp.bfloat16)] * 2,
         compiler_params=pltpu.CompilerParams(vmem_limit_bytes=8 * 2**20),
-    )(spread, got, far, so_far)
+    )(spread, got, far, so_far, resp)
 
 
 def merge(parts):
@@ -314,20 +304,19 @@
     swap_cores = [(0, 1), (1, 0)]
     swap_chips = [way for a, b in SHARERS for way in ((a, b), (b, a))]
     with jax.named_scope("query_spread"):
-        slots, own = pack(queries, keys, values)
+        slots, own = pack(counts, queries, keys, values)
         groups = exchange(slots.reshape(NZ * 4, 8, HS), groups_spread()).reshape(NZ, PAIRS, HS)
     with jax.named_scope("block_exchange"):
-        own = note(counts, resp_len, own)
         near = lax.ppermute(own, "x", swap_chips)
         got = lax.ppermute(own, "core", swap_cores)
         far = lax.ppermute(near, "core", swap_cores)
     groups, own = lax.optimization_barrier((groups, own))
     with jax.named_scope("query_turn"):
-        groups = turn(groups).reshape(SRC, PAIRS, HS)
-        spread = exchange(groups, groups_turn()).reshape(2, NY, PAIRS, HS)
+        turned, resp = turn(resp_len, groups)
+        spread = exchange(turned.reshape(SRC, PAIRS, HS), groups_turn()).reshape(2, NY, PAIRS, HS)
     with jax.named_scope("attend"):
         so_far = attend(spread, own, near)
-        parts = finish(spread, got, far, so_far)
+        parts = finish(spread, got, far, so_far, resp)
     with jax.named_scope("merge"):
         parts = exchange(parts.reshape(SRC, SLOT_ROWS, HS), groups_merge())
         return merge(parts.reshape(SRC * SLOT_ROWS, HS))

time: 55.7 us -> 55.2 us (level)
  waiting for transfers between devices: 2.47 us -> 3.61 us
  blocking collectives: 14.5 us -> 13.8 us
  Pallas kernels: 7.88 us -> 7.2 us
    all_to_all x2, waiting for transfers between devices: 1.9 us -> 3.2 us  [exchange(): lax.all_to_all(blocks, axes, 0, 0, axis_index_groups=groups, tiled=True)]
    all_to_all x1, blocking collectives: 14.5 us -> 13.8 us  [exchange(): lax.all_to_all(blocks, axes, 0, 0, axis_index_groups=groups, tiled=True)]
    pallas_call x2 -> x1, Pallas kernels: 1.28 us -> 0.66 us  [turn(): pl.pallas_call(turn_kernel, out_shape=(jax.ShapeDtypeStruct((2, NY, PAIRS...]
  transfers between devices with their start and end apart: 5 -> 5, of which waited for: 3 -> 3; matrix products, arithmetic and copies ran while one was open for 0% -> 0% of each run, Pallas kernels for 6% -> 4%
where the time goes in v10:
time: 55.2 us; the launch traced here: 54.7 us
  starting transfers between devices  28.8 us (52%)
  blocking collectives  13.8 us (25%)
  Pallas kernels  7.2 us (13%)
  waiting for transfers between devices  3.61 us (7%)
  between operations  1.38 us (2%)
    all_to_all x2, starting transfers between devices, exchange(): lax.all_to_all(blocks, axes, 0, 0, axis_index_groups=groups, tiled=True)  21.5 us
    all_to_all x1, blocking collectives, exchange(): lax.all_to_all(blocks, axes, 0, 0, axis_index_groups=groups, tiled=True)  13.8 us
    ppermute x1, starting transfers between devices, local(): near = lax.ppermute(own, 'x', swap_chips)  3.37 us
    all_to_all x2, waiting for transfers between devices, exchange(): lax.all_to_all(blocks, axes, 0, 0, axis_index_groups=groups, tiled=True)  3.2 us
    ppermute x1, starting transfers between devices, local(): far = lax.ppermute(near, 'core', swap_cores)  2.01 us
    ppermute x1, starting transfers between devices, local(): got = lax.ppermute(own, 'core', swap_cores)  1.92 us
    pallas_call x1, Pallas kernels, finish(): pl.pallas_call(finish_kernel, out_shape=jax.ShapeDtypeStruct((SRC * SLOT_...  1.86 us
    pallas_call x1, Pallas kernels, pack(): pl.pallas_call(pack_kernel, out_shape=(jax.ShapeDtypeStruct((NZ, PAIRS, H...  1.83 us
  transfers between devices with their start and end apart: 5, of which 3 were waited for; matrix products, arithmetic and copies ran while one was open for 0% of the time, Pallas kernels for 4%

profile of v10, /device:TPU:6, one launch (start us, length us, event | category | flops | bytes accessed | tf_op | source)
XLA Modules:
  0.0 54.7 jit_solution(3278308440472281843)
XLA Ops:
  0.7 1.8 %query_spread.1 = (bf16[8,32,128]{2,1,0:T(8,128)(2,1)}, bf16[2064,128]{1,0:T(8,128)(2,1)}) custom-call(s32[1]{0:T(128)S(6)} %copy.6.count_ref, bf16[32,128]{1,0:T(8,128)(2,1)} %query_ref.1, bf16[1024,128]{1,0:T(8,128)(2,1)} %key_ref.1, bf16[1024,128]{1,0:T(8,128)(2,1)} %value_ref.1), custom_call_target="tpu_custom_call" | custom-call | tf_op jit(solution)/shard_map/query_spread/pallas_call | solution.py:237
  2.5 13.1 %all-to-all-start = ((bf16[32,8,128]{2,1,0:T(8,128)(2,1)}), bf16[32,8,128]{2,1,0:T(8,128)(2,1)S(1)}, u32[]{:S(2)}, u32[]{:S(2)}) async-start(bf16[32,8,128]{2,1,0:T(8,128)(2,1)} %bitcast.11), calls=%async_computation | async-start | bytes 131072 | tf_op jit(solution)/shard_map/query_spread/all_to_all | solution.py:63
  15.6 3.4 %collective-permute-start.1 = (bf16[2064,128]{1,0:T(8,128)(2,1)}, bf16[2064,128]{1,0:T(8,128)(2,1)S(1)}, u32[]{:S(2)}, u32[]{:S(2)}) collective-permute-start(bf16[2064,128]{1,0:T(8,128)(2,1)} %get-tuple-element.15.own_ref), channel_id=1, source_target_pairs={{0,16},{16,0},{48,32},{32,48},{1,17},{17,1},{49,33},{33,49},{2,18}... | collective-permute-start | bytes 1585160 | tf_op jit(solution)/shard_map/block_exchange/ppermute | solution.py:310
  19.6 0.8 %all-to-all-done = bf16[32,8,128]{2,1,0:T(8,128)(2,1)S(1)} async-done(((bf16[32,8,128]{2,1,0:T(8,128)(2,1)}), bf16[32,8,128]{2,1,0:T(8,128)(2,1)S(1)}, u32[]{:S(2)}, u32[]{:S(2)}) %all-to-all-start) | async-done | bytes 65568 | tf_op jit(solution)/shard_map/query_spread/all_to_all | solution.py:63
  20.4 0.0 copy-start
  20.4 0.7 %query_turn.1 = (bf16[2,8,32,128]{3,2,1,0:T(8,128)(2,1)}, f32[8,128]{1,0:T(8,128)S(1)}) custom-call(s32[1]{0:T(128)S(6)} %copy.7.resp_ref, bf16[8,32,128]{2,1,0:T(8,128)(2,1)S(1)} %bitcast.10), custom_call_target="tpu_custom_call" | custom-call | flops 68719476736 | bytes 2097152 | tf_op jit(solution)/shard_map/query_turn/pallas_call | solution.py:257
  21.1 8.4 %all-to-all-start.1 = ((bf16[16,32,128]{2,1,0:T(8,128)(2,1)}), bf16[16,32,128]{2,1,0:T(8,128)(2,1)S(1)}, u32[]{:S(2)}, u32[]{:S(2)}) async-start(bf16[16,32,128]{2,1,0:T(8,128)(2,1)} %bitcast.2), calls=%async_computation.1 | async-start | bytes 262144 | tf_op jit(solution)/shard_map/query_turn/all_to_all | solution.py:63
  29.4 0.0 copy-done
  29.4 1.9 %collective-permute-start = (bf16[2064,128]{1,0:T(8,128)(2,1)S(1)}, bf16[2064,128]{1,0:T(8,128)(2,1)S(1)}, u32[]{:S(2)}, u32[]{:S(2)}) collective-permute-start(bf16[2064,128]{1,0:T(8,128)(2,1)S(1)} %copy-done), channel_id=1, source_target_pairs={{0,8},{8,0},{1,9},{9,1},{2,10},{10,2},{3,11},{11,3},{4,12},{12,4},... | collective-permute-start | bytes 1585160 | tf_op jit(solution)/shard_map/block_exchange/ppermute | solution.py:311
  31.4 0.4 collective-permute-done.1.near_ref
  31.8 2.0 %collective-permute-start.2 = (bf16[2064,128]{1,0:T(8,128)(2,1)S(1)}, bf16[2064,128]{1,0:T(8,128)(2,1)S(1)}, u32[]{:S(2)}, u32[]{:S(2)}) collective-permute-start(bf16[2064,128]{1,0:T(8,128)(2,1)S(1)} %collective-permute-done.1.near_ref), channel_id=1, source_target_pairs={{0,8},{8,0},{1,9},{9,1},{2,10},{10,2},{3,11},{11,3},{4,12},{12,4},... | collective-permute-start | bytes 1585160 | tf_op jit(solution)/shard_map/block_exchange/ppermute | solution.py:312
  33.8 2.4 %all-to-all-done.1 = bf16[16,32,128]{2,1,0:T(8,128)(2,1)S(1)} async-done(((bf16[16,32,128]{2,1,0:T(8,128)(2,1)}), bf16[16,32,128]{2,1,0:T(8,128)(2,1)S(1)}, u32[]{:S(2)}, u32[]{:S(2)}) %all-to-all-start.1) | async-done | bytes 131104 | tf_op jit(solution)/shard_map/query_turn/all_to_all | solution.py:63
  36.2 1.8 %attend.2.so_far_ref = f32[3,4,128,128]{3,2,1,0:T(8,128)S(1)} custom-call(bf16[2,8,32,128]{3,2,1,0:T(8,128)(2,1)S(1)} %bitcast.8, bf16[2064,128]{1,0:T(8,128)(2,1)S(1)} %copy-done, bf16[2064,128]{1,0:T(8,128)(2,1)S(1)} %collective-permute-done.1.near_ref), custom_call_target="tpu_custom_call" | custom-call | flops 17179869184 | bytes 2097152 | tf_op jit(solution)/shard_map/attend/pallas_call | solution.py:271
  38.0 0.0 collective-permute-done.got_ref
  38.0 0.0 collective-permute-done.2.far_ref
  38.0 1.9 %attend.3 = bf16[640,128]{1,0:T(8,128)(2,1)S(1)} custom-call(bf16[2,8,32,128]{3,2,1,0:T(8,128)(2,1)S(1)} %bitcast.9, bf16[2064,128]{1,0:T(8,128)(2,1)S(1)} %collective-permute-done.got_ref, bf16[2064,128]{1,0:T(8,128)(2,1)S(1)} %collective-permute-done.2.far_ref, f32[3,4,128,128]{3,2,1,0:T(8,128)S(1)} %attend.2.so_far_ref, ...), custom_call_target="tpu_custom_call" | custom-call | tf_op jit(solution)/shard_map/attend/pallas_call | solution.py:283
  39.9 13.8 %all_to_all.15 = bf16[16,40,128]{2,1,0:T(8,128)(2,1)S(1)} all-to-all(bf16[16,40,128]{2,1,0:T(8,128)(2,1)S(1)} %bitcast.6), channel_id=1, replica_groups={{368,320,432,384,496,448,48,0,112,64,176,128,240,192,304,256},{352,336,..., dimensions={0} | all-to-all | bytes 327680 | tf_op jit(solution)/shard_map/merge/all_to_all | solution.py:63
  53.7 1.1 %merge.1 = bf16[4,1024]{1,0:T(4,128)(2,1)} custom-call(bf16[640,128]{1,0:T(8,128)(2,1)S(1)} %bitcast.7), custom_call_target="tpu_custom_call" | custom-call | tf_op jit(solution)/shard_map/merge/pallas_call | solution.py:294
Async XLA Ops:
  2.5 17.9 %all-to-all-start = ((bf16[32,8,128]{2,1,0:T(8,128)(2,1)}), bf16[32,8,128]{2,1,0:T(8,128)(2,1)S(1)}, u32[]{:S(2)}, u32[]{:S(2)}) async-start(bf16[32,8,128]{2,1,0:T(8,128)(2,1)} %bitcast.11), calls=%async_computation | async-start | bytes 131072 | tf_op jit(solution)/shard_map/query_spread/all_to_all | solution.py:63
  15.6 16.2 %collective-permute-start.1 = (bf16[2064,128]{1,0:T(8,128)(2,1)}, bf16[2064,128]{1,0:T(8,128)(2,1)S(1)}, u32[]{:S(2)}, u32[]{:S(2)}) collective-permute-start(bf16[2064,128]{1,0:T(8,128)(2,1)} %get-tuple-element.15.own_ref), channel_id=1, source_target_pairs={{0,16},{16,0},{48,32},{32,48},{1,17},{17,1},{49,33},{33,49},{2,18}... | collective-permute-start | bytes 1585160 | tf_op jit(solution)/shard_map/block_exchange/ppermute | solution.py:310
  20.4 9.0 %copy-start = (bf16[2064,128]{1,0:T(8,128)(2,1)S(1)}, bf16[2064,128]{1,0:T(8,128)(2,1)}, u32[]{:S(2)}) copy-start(bf16[2064,128]{1,0:T(8,128)(2,1)} %get-tuple-element.15.own_ref) | copy-start | bytes 1585156
  21.1 15.1 %all-to-all-start.1 = ((bf16[16,32,128]{2,1,0:T(8,128)(2,1)}), bf16[16,32,128]{2,1,0:T(8,128)(2,1)S(1)}, u32[]{:S(2)}, u32[]{:S(2)}) async-start(bf16[16,32,128]{2,1,0:T(8,128)(2,1)} %bitcast.2), calls=%async_computation.1 | async-start | bytes 262144 | tf_op jit(solution)/shard_map/query_turn/all_to_all | solution.py:63
  29.4 8.6 %collective-permute-start = (bf16[2064,128]{1,0:T(8,128)(2,1)S(1)}, bf16[2064,128]{1,0:T(8,128)(2,1)S(1)}, u32[]{:S(2)}, u32[]{:S(2)}) collective-permute-start(bf16[2064,128]{1,0:T(8,128)(2,1)S(1)} %copy-done), channel_id=1, source_target_pairs={{0,8},{8,0},{1,9},{9,1},{2,10},{10,2},{3,11},{11,3},{4,12},{12,4},... | collective-permute-start | bytes 1585160 | tf_op jit(solution)/shard_map/block_exchange/ppermute | solution.py:311
  31.8 6.2 %collective-permute-start.2 = (bf16[2064,128]{1,0:T(8,128)(2,1)S(1)}, bf16[2064,128]{1,0:T(8,128)(2,1)S(1)}, u32[]{:S(2)}, u32[]{:S(2)}) collective-permute-start(bf16[2064,128]{1,0:T(8,128)(2,1)S(1)} %collective-permute-done.1.near_ref), channel_id=1, source_target_pairs={{0,8},{8,0},{1,9},{9,1},{2,10},{10,2},{3,11},{11,3},{4,12},{12,4},... | collective-permute-start | bytes 1585160 | tf_op jit(solution)/shard_map/block_exchange/ppermute | solution.py:312

commit v11 on v10

--- a/solution.py
+++ b/solution.py
@@ -18,7 +18,7 @@
 SEND_ROWS = 2 * SLOTS + 16
 COUNT_BASE = 64
 MASKED = -1e30
-FIRST_Z, FIRST_Y, LAST_Z = 5, 5, 5
+FIRST_Z, FIRST_Y, LAST_Z = 5, 6, 4
 SHARERS = ((0, 1), (3, 2))
 CLASSES = ((3, 0), (2, 1))
 HEAD_X = (3, 2, 0, 1)

time: 55.2 us -> 55.2 us (level)
  no operation moved by 1% of the time
where the time goes in v11:
time: 55.2 us; the launch traced here: 54.8 us
  starting transfers between devices  28.6 us (52%)
  blocking collectives  13.5 us (24%)
  Pallas kernels  7.2 us (13%)
  waiting for transfers between devices  4.12 us (7%)
  between operations  1.38 us (2%)
    all_to_all x2, starting transfers between devices, exchange(): lax.all_to_all(blocks, axes, 0, 0, axis_index_groups=groups, tiled=True)  21.4 us
    all_to_all x1, blocking collectives, exchange(): lax.all_to_all(blocks, axes, 0, 0, axis_index_groups=groups, tiled=True)  13.5 us
    all_to_all x2, waiting for transfers between devices, exchange(): lax.all_to_all(blocks, axes, 0, 0, axis_index_groups=groups, tiled=True)  3.61 us
    ppermute x1, starting transfers between devices, local(): near = lax.ppermute(own, 'x', swap_chips)  3.37 us
    ppermute x1, starting transfers between devices, local(): got = lax.ppermute(own, 'core', swap_cores)  1.92 us
    ppermute x1, starting transfers between devices, local(): far = lax.ppermute(near, 'core', swap_cores)  1.91 us
    pallas_call x1, Pallas kernels, finish(): pl.pallas_call(finish_kernel, out_shape=jax.ShapeDtypeStruct((SRC * SLOT_...  1.86 us
    pallas_call x1, Pallas kernels, pack(): pl.pallas_call(pack_kernel, out_shape=(jax.ShapeDtypeStruct((NZ, PAIRS, H...  1.83 us
  transfers between devices with their start and end apart: 5, of which 3 were waited for; matrix products, arithmetic and copies ran while one was open for 0% of the time, Pallas kernels for 4%

profile of v11, /device:TPU:6, one launch (start us, length us, event | category | flops | bytes accessed | tf_op | source)
XLA Modules:
  0.0 54.8 jit_solution(9105495877910736694)
XLA Ops:
  0.7 1.8 %query_spread.1 = (bf16[8,32,128]{2,1,0:T(8,128)(2,1)}, bf16[2064,128]{1,0:T(8,128)(2,1)}) custom-call(s32[1]{0:T(128)S(6)} %copy.6.count_ref, bf16[32,128]{1,0:T(8,128)(2,1)} %query_ref.1, bf16[1024,128]{1,0:T(8,128)(2,1)} %key_ref.1, bf16[1024,128]{1,0:T(8,128)(2,1)} %value_ref.1), custom_call_target="tpu_custom_call" | custom-call | tf_op jit(solution)/shard_map/query_spread/pallas_call | solution.py:237
  2.5 13.1 %all-to-all-start = ((bf16[32,8,128]{2,1,0:T(8,128)(2,1)}), bf16[32,8,128]{2,1,0:T(8,128)(2,1)S(1)}, u32[]{:S(2)}, u32[]{:S(2)}) async-start(bf16[32,8,128]{2,1,0:T(8,128)(2,1)} %bitcast.11), calls=%async_computation | async-start | bytes 131072 | tf_op jit(solution)/shard_map/query_spread/all_to_all | solution.py:63
  15.6 3.4 %collective-permute-start.1 = (bf16[2064,128]{1,0:T(8,128)(2,1)}, bf16[2064,128]{1,0:T(8,128)(2,1)S(1)}, u32[]{:S(2)}, u32[]{:S(2)}) collective-permute-start(bf16[2064,128]{1,0:T(8,128)(2,1)} %get-tuple-element.15.own_ref), channel_id=1, source_target_pairs={{0,16},{16,0},{48,32},{32,48},{1,17},{17,1},{49,33},{33,49},{2,18}... | collective-permute-start | bytes 1585160 | tf_op jit(solution)/shard_map/block_exchange/ppermute | solution.py:310
  19.6 0.8 %all-to-all-done = bf16[32,8,128]{2,1,0:T(8,128)(2,1)S(1)} async-done(((bf16[32,8,128]{2,1,0:T(8,128)(2,1)}), bf16[32,8,128]{2,1,0:T(8,128)(2,1)S(1)}, u32[]{:S(2)}, u32[]{:S(2)}) %all-to-all-start) | async-done | bytes 65568 | tf_op jit(solution)/shard_map/query_spread/all_to_all | solution.py:63
  20.4 0.0 copy-start
  20.4 0.7 %query_turn.1 = (bf16[2,8,32,128]{3,2,1,0:T(8,128)(2,1)}, f32[8,128]{1,0:T(8,128)S(1)}) custom-call(s32[1]{0:T(128)S(6)} %copy.7.resp_ref, bf16[8,32,128]{2,1,0:T(8,128)(2,1)S(1)} %bitcast.10), custom_call_target="tpu_custom_call" | custom-call | flops 68719476736 | bytes 2097152 | tf_op jit(solution)/shard_map/query_turn/pallas_call | solution.py:257
  21.1 8.3 %all-to-all-start.1 = ((bf16[16,32,128]{2,1,0:T(8,128)(2,1)}), bf16[16,32,128]{2,1,0:T(8,128)(2,1)S(1)}, u32[]{:S(2)}, u32[]{:S(2)}) async-start(bf16[16,32,128]{2,1,0:T(8,128)(2,1)} %bitcast.2), calls=%async_computation.1 | async-start | bytes 262144 | tf_op jit(solution)/shard_map/query_turn/all_to_all | solution.py:63
  29.3 0.0 copy-done
  29.3 1.9 %collective-permute-start = (bf16[2064,128]{1,0:T(8,128)(2,1)S(1)}, bf16[2064,128]{1,0:T(8,128)(2,1)S(1)}, u32[]{:S(2)}, u32[]{:S(2)}) collective-permute-start(bf16[2064,128]{1,0:T(8,128)(2,1)S(1)} %copy-done), channel_id=1, source_target_pairs={{0,8},{8,0},{1,9},{9,1},{2,10},{10,2},{3,11},{11,3},{4,12},{12,4},... | collective-permute-start | bytes 1585160 | tf_op jit(solution)/shard_map/block_exchange/ppermute | solution.py:311
  31.3 0.5 collective-permute-done.1.near_ref
  31.8 1.9 %collective-permute-start.2 = (bf16[2064,128]{1,0:T(8,128)(2,1)S(1)}, bf16[2064,128]{1,0:T(8,128)(2,1)S(1)}, u32[]{:S(2)}, u32[]{:S(2)}) collective-permute-start(bf16[2064,128]{1,0:T(8,128)(2,1)S(1)} %collective-permute-done.1.near_ref), channel_id=1, source_target_pairs={{0,8},{8,0},{1,9},{9,1},{2,10},{10,2},{3,11},{11,3},{4,12},{12,4},... | collective-permute-start | bytes 1585160 | tf_op jit(solution)/shard_map/block_exchange/ppermute | solution.py:312
  33.7 2.8 %all-to-all-done.1 = bf16[16,32,128]{2,1,0:T(8,128)(2,1)S(1)} async-done(((bf16[16,32,128]{2,1,0:T(8,128)(2,1)}), bf16[16,32,128]{2,1,0:T(8,128)(2,1)S(1)}, u32[]{:S(2)}, u32[]{:S(2)}) %all-to-all-start.1) | async-done | bytes 131104 | tf_op jit(solution)/shard_map/query_turn/all_to_all | solution.py:63
  36.5 1.8 %attend.2.so_far_ref = f32[3,4,128,128]{3,2,1,0:T(8,128)S(1)} custom-call(bf16[2,8,32,128]{3,2,1,0:T(8,128)(2,1)S(1)} %bitcast.8, bf16[2064,128]{1,0:T(8,128)(2,1)S(1)} %copy-done, bf16[2064,128]{1,0:T(8,128)(2,1)S(1)} %collective-permute-done.1.near_ref), custom_call_target="tpu_custom_call" | custom-call | flops 17179869184 | bytes 2097152 | tf_op jit(solution)/shard_map/attend/pallas_call | solution.py:271
  38.3 0.0 collective-permute-done.got_ref
  38.3 0.0 collective-permute-done.2.far_ref
  38.3 1.9 %attend.3 = bf16[640,128]{1,0:T(8,128)(2,1)S(1)} custom-call(bf16[2,8,32,128]{3,2,1,0:T(8,128)(2,1)S(1)} %bitcast.9, bf16[2064,128]{1,0:T(8,128)(2,1)S(1)} %collective-permute-done.got_ref, bf16[2064,128]{1,0:T(8,128)(2,1)S(1)} %collective-permute-done.2.far_ref, f32[3,4,128,128]{3,2,1,0:T(8,128)S(1)} %attend.2.so_far_ref, ...), custom_call_target="tpu_custom_call" | custom-call | tf_op jit(solution)/shard_map/attend/pallas_call | solution.py:283
  40.2 13.5 %all_to_all.15 = bf16[16,40,128]{2,1,0:T(8,128)(2,1)S(1)} all-to-all(bf16[16,40,128]{2,1,0:T(8,128)(2,1)S(1)} %bitcast.6), channel_id=1, replica_groups={{304,256,368,320,432,384,496,448,48,0,112,64,176,128,240,192},{288,272,..., dimensions={0} | all-to-all | bytes 327680 | tf_op jit(solution)/shard_map/merge/all_to_all | solution.py:63
  53.7 1.1 %merge.1 = bf16[4,1024]{1,0:T(4,128)(2,1)} custom-call(bf16[640,128]{1,0:T(8,128)(2,1)S(1)} %bitcast.7), custom_call_target="tpu_custom_call" | custom-call | tf_op jit(solution)/shard_map/merge/pallas_call | solution.py:294
Async XLA Ops:
  2.5 17.9 %all-to-all-start = ((bf16[32,8,128]{2,1,0:T(8,128)(2,1)}), bf16[32,8,128]{2,1,0:T(8,128)(2,1)S(1)}, u32[]{:S(2)}, u32[]{:S(2)}) async-start(bf16[32,8,128]{2,1,0:T(8,128)(2,1)} %bitcast.11), calls=%async_computation | async-start | bytes 131072 | tf_op jit(solution)/shard_map/query_spread/all_to_all | solution.py:63
  15.6 16.2 %collective-permute-start.1 = (bf16[2064,128]{1,0:T(8,128)(2,1)}, bf16[2064,128]{1,0:T(8,128)(2,1)S(1)}, u32[]{:S(2)}, u32[]{:S(2)}) collective-permute-start(bf16[2064,128]{1,0:T(8,128)(2,1)} %get-tuple-element.15.own_ref), channel_id=1, source_target_pairs={{0,16},{16,0},{48,32},{32,48},{1,17},{17,1},{49,33},{33,49},{2,18}... | collective-permute-start | bytes 1585160 | tf_op jit(solution)/shard_map/block_exchange/ppermute | solution.py:310
  20.4 8.9 %copy-start = (bf16[2064,128]{1,0:T(8,128)(2,1)S(1)}, bf16[2064,128]{1,0:T(8,128)(2,1)}, u32[]{:S(2)}) copy-start(bf16[2064,128]{1,0:T(8,128)(2,1)} %get-tuple-element.15.own_ref) | copy-start | bytes 1585156
  21.1 15.4 %all-to-all-start.1 = ((bf16[16,32,128]{2,1,0:T(8,128)(2,1)}), bf16[16,32,128]{2,1,0:T(8,128)(2,1)S(1)}, u32[]{:S(2)}, u32[]{:S(2)}) async-start(bf16[16,32,128]{2,1,0:T(8,128)(2,1)} %bitcast.2), calls=%async_computation.1 | async-start | bytes 262144 | tf_op jit(solution)/shard_map/query_turn/all_to_all | solution.py:63
  29.3 9.0 %collective-permute-start = (bf16[2064,128]{1,0:T(8,128)(2,1)S(1)}, bf16[2064,128]{1,0:T(8,128)(2,1)S(1)}, u32[]{:S(2)}, u32[]{:S(2)}) collective-permute-start(bf16[2064,128]{1,0:T(8,128)(2,1)S(1)} %copy-done), channel_id=1, source_target_pairs={{0,8},{8,0},{1,9},{9,1},{2,10},{10,2},{3,11},{11,3},{4,12},{12,4},... | collective-permute-start | bytes 1585160 | tf_op jit(solution)/shard_map/block_exchange/ppermute | solution.py:311
  31.8 6.6 %collective-permute-start.2 = (bf16[2064,128]{1,0:T(8,128)(2,1)S(1)}, bf16[2064,128]{1,0:T(8,128)(2,1)S(1)}, u32[]{:S(2)}, u32[]{:S(2)}) collective-permute-start(bf16[2064,128]{1,0:T(8,128)(2,1)S(1)} %collective-permute-done.1.near_ref), channel_id=1, source_target_pairs={{0,8},{8,0},{1,9},{9,1},{2,10},{10,2},{3,11},{11,3},{4,12},{12,4},... | collective-permute-start | bytes 1585160 | tf_op jit(solution)/shard_map/block_exchange/ppermute | solution.py:312

commit v12 on v10

--- a/solution.py
+++ b/solution.py
@@ -151,8 +151,11 @@
     return q_ref[:, 2 * step : 2 * step + 2].reshape(TILE, HS)
 
 
-def attend_kernel(q_ref, own_ref, near_ref, out_ref, own_wide_ref, near_wide_ref):
-    widen_into(own_wide_ref, own_ref)
+def widen_kernel(own_ref, wide_ref):
+    widen_into(wide_ref, own_ref)
+
+
+def attend_kernel(q_ref, own_ref, own_wide_ref, near_ref, out_ref, near_wide_ref):
     widen_into(near_wide_ref, near_ref)
     blocks = ((own_ref, own_wide_ref), (near_ref, near_wide_ref))
     biases = [bias_row(ref) for ref, _ in blocks]
@@ -267,16 +270,26 @@
     )(resp_len, groups)
 
 
-def attend(spread, own, near):
+def widen(own):
+    return pl.pallas_call(
+        widen_kernel,
+        out_shape=jax.ShapeDtypeStruct((SLOTS, 2 * HS), jnp.bfloat16),
+        in_specs=[VMEM],
+        out_specs=VMEM,
+        compiler_params=pltpu.CompilerParams(vmem_limit_bytes=2**20),
+    )(own)
+
+
+def attend(spread, own, own_wide, near):
     return pl.pallas_call(
         attend_kernel,
         out_shape=jax.ShapeDtypeStruct((3, TILES, TILE, HS), jnp.float32),
-        in_specs=[VMEM] * 3,
+        in_specs=[VMEM] * 4,
         out_specs=VMEM,
-        scratch_shapes=[pltpu.VMEM((SLOTS, 2 * HS), jnp.bfloat16)] * 2,
+        scratch_shapes=[pltpu.VMEM((SLOTS, 2 * HS), jnp.bfloat16)],
         compiler_params=pltpu.CompilerParams(vmem_limit_bytes=12 * 2**20),
         cost_estimate=pl.CostEstimate(flops=2**34, bytes_accessed=2**21, transcendentals=0),
-    )(spread, own, near)
+    )(spread, own, own_wide, near)
 
 
 def finish(spread, got, far, so_far, resp):
@@ -315,7 +328,7 @@
         turned, resp = turn(resp_len, groups)
         spread = exchange(turned.reshape(SRC, PAIRS, HS), groups_turn()).reshape(2, NY, PAIRS, HS)
     with jax.named_scope("attend"):
-        so_far = attend(spread, own, near)
+        so_far = attend(spread, own, widen(own), near)
         parts = finish(spread, got, far, so_far, resp)
     with jax.named_scope("merge"):
         parts = exchange(parts.reshape(SRC, SLOT_ROWS, HS), groups_merge())

time: 55.2 us -> 55.2 us (level)
  transfers between devices with their start and end apart: 5 -> 5, of which waited for: 3 -> 3; matrix products, arithmetic and copies ran while one was open for 0% -> 0% of each run, Pallas kernels for 4% -> 5%
where the time goes in v12:
time: 55.2 us; the launch traced here: 54.7 us
  starting transfers between devices  28.8 us (52%)
  blocking collectives  13.8 us (25%)
  Pallas kernels  7.29 us (13%)
  waiting for transfers between devices  3.46 us (6%)
  between operations  1.38 us (2%)
    all_to_all x2, starting transfers between devices, exchange(): lax.all_to_all(blocks, axes, 0, 0, axis_index_groups=groups, tiled=True)  21.5 us
    all_to_all x1, blocking collectives, exchange(): lax.all_to_all(blocks, axes, 0, 0, axis_index_groups=groups, tiled=True)  13.8 us
    ppermute x1, starting transfers between devices, local(): near = lax.ppermute(own, 'x', swap_chips)  3.37 us
    all_to_all x2, waiting for transfers between devices, exchange(): lax.all_to_all(blocks, axes, 0, 0, axis_index_groups=groups, tiled=True)  3.12 us
    ppermute x1, starting transfers between devices, local(): far = lax.ppermute(near, 'core', swap_cores)  2.09 us
    ppermute x1, starting transfers between devices, local(): got = lax.ppermute(own, 'core', swap_cores)  1.92 us
    pallas_call x1, Pallas kernels, finish(): pl.pallas_call(finish_kernel, out_shape=jax.ShapeDtypeStruct((SRC * SLOT_...  1.86 us
    pallas_call x1, Pallas kernels, pack(): pl.pallas_call(pack_kernel, out_shape=(jax.ShapeDtypeStruct((NZ, PAIRS, H...  1.83 us
  transfers between devices with their start and end apart: 5, of which 3 were waited for; matrix products, arithmetic and copies ran while one was open for 0% of the time, Pallas kernels for 5%

profile of v12, /device:TPU:6, one launch (start us, length us, event | category | flops | bytes accessed | tf_op | source)
XLA Modules:
  0.0 54.7 jit_solution(7910168945556571373)
XLA Ops:
  0.7 1.8 %query_spread.1 = (bf16[8,32,128]{2,1,0:T(8,128)(2,1)}, bf16[2064,128]{1,0:T(8,128)(2,1)}) custom-call(s32[1]{0:T(128)S(6)} %copy.6.count_ref, bf16[32,128]{1,0:T(8,128)(2,1)} %query_ref.1, bf16[1024,128]{1,0:T(8,128)(2,1)} %key_ref.1, bf16[1024,128]{1,0:T(8,128)(2,1)} %value_ref.1), custom_call_target="tpu_custom_call" | custom-call | tf_op jit(solution)/shard_map/query_spread/pallas_call | solution.py:240
  2.5 13.1 %all-to-all-start = ((bf16[32,8,128]{2,1,0:T(8,128)(2,1)}), bf16[32,8,128]{2,1,0:T(8,128)(2,1)S(1)}, u32[]{:S(2)}, u32[]{:S(2)}) async-start(bf16[32,8,128]{2,1,0:T(8,128)(2,1)} %bitcast.11), calls=%async_computation | async-start | bytes 131072 | tf_op jit(solution)/shard_map/query_spread/all_to_all | solution.py:63
  15.6 3.4 %collective-permute-start.1 = (bf16[2064,128]{1,0:T(8,128)(2,1)}, bf16[2064,128]{1,0:T(8,128)(2,1)S(1)}, u32[]{:S(2)}, u32[]{:S(2)}) collective-permute-start(bf16[2064,128]{1,0:T(8,128)(2,1)} %get-tuple-element.15.own_ref), channel_id=1, source_target_pairs={{0,16},{16,0},{48,32},{32,48},{1,17},{17,1},{49,33},{33,49},{2,18}... | collective-permute-start | bytes 1585160 | tf_op jit(solution)/shard_map/block_exchange/ppermute | solution.py:323
  19.6 0.8 %all-to-all-done = bf16[32,8,128]{2,1,0:T(8,128)(2,1)S(1)} async-done(((bf16[32,8,128]{2,1,0:T(8,128)(2,1)}), bf16[32,8,128]{2,1,0:T(8,128)(2,1)S(1)}, u32[]{:S(2)}, u32[]{:S(2)}) %all-to-all-start) | async-done | bytes 65568 | tf_op jit(solution)/shard_map/query_spread/all_to_all | solution.py:63
  20.4 0.0 copy-start
  20.4 0.7 %query_turn.1 = (bf16[2,8,32,128]{3,2,1,0:T(8,128)(2,1)}, f32[8,128]{1,0:T(8,128)S(1)}) custom-call(s32[1]{0:T(128)S(6)} %copy.7.resp_ref, bf16[8,32,128]{2,1,0:T(8,128)(2,1)S(1)} %bitcast.10), custom_call_target="tpu_custom_call" | custom-call | flops 68719476736 | bytes 2097152 | tf_op jit(solution)/shard_map/query_turn/pallas_call | solution.py:260
  21.1 8.4 %all-to-all-start.1 = ((bf16[16,32,128]{2,1,0:T(8,128)(2,1)}), bf16[16,32,128]{2,1,0:T(8,128)(2,1)S(1)}, u32[]{:S(2)}, u32[]{:S(2)}) async-start(bf16[16,32,128]{2,1,0:T(8,128)(2,1)} %bitcast.2), calls=%async_computation.1 | async-start | bytes 262144 | tf_op jit(solution)/shard_map/query_turn/all_to_all | solution.py:63
  29.4 0.0 copy-done
  29.4 1.9 %collective-permute-start = (bf16[2064,128]{1,0:T(8,128)(2,1)S(1)}, bf16[2064,128]{1,0:T(8,128)(2,1)S(1)}, u32[]{:S(2)}, u32[]{:S(2)}) collective-permute-start(bf16[2064,128]{1,0:T(8,128)(2,1)S(1)} %copy-done), channel_id=1, source_target_pairs={{0,8},{8,0},{1,9},{9,1},{2,10},{10,2},{3,11},{11,3},{4,12},{12,4},... | collective-permute-start | bytes 1585160 | tf_op jit(solution)/shard_map/block_exchange/ppermute | solution.py:324
  31.4 0.1 attend.3.own_wide_ref
  31.4 0.3 collective-permute-done.1.near_ref
  31.8 2.1 %collective-permute-start.2 = (bf16[2064,128]{1,0:T(8,128)(2,1)S(1)}, bf16[2064,128]{1,0:T(8,128)(2,1)S(1)}, u32[]{:S(2)}, u32[]{:S(2)}) collective-permute-start(bf16[2064,128]{1,0:T(8,128)(2,1)S(1)} %collective-permute-done.1.near_ref), channel_id=1, source_target_pairs={{0,8},{8,0},{1,9},{9,1},{2,10},{10,2},{3,11},{11,3},{4,12},{12,4},... | collective-permute-start | bytes 1585160 | tf_op jit(solution)/shard_map/block_exchange/ppermute | solution.py:325
  33.9 2.3 %all-to-all-done.1 = bf16[16,32,128]{2,1,0:T(8,128)(2,1)S(1)} async-done(((bf16[16,32,128]{2,1,0:T(8,128)(2,1)}), bf16[16,32,128]{2,1,0:T(8,128)(2,1)S(1)}, u32[]{:S(2)}, u32[]{:S(2)}) %all-to-all-start.1) | async-done | bytes 131104 | tf_op jit(solution)/shard_map/query_turn/all_to_all | solution.py:63
  36.2 1.8 %attend.4.so_far_ref = f32[3,4,128,128]{3,2,1,0:T(8,128)S(1)} custom-call(bf16[2,8,32,128]{3,2,1,0:T(8,128)(2,1)S(1)} %bitcast.8, bf16[2064,128]{1,0:T(8,128)(2,1)S(1)} %copy-done, bf16[1024,256]{1,0:T(8,128)(2,1)S(1)} %attend.3.own_wide_ref, bf16[2064,128]{1,0:T(8,128)(2,1)S(1)} %collective-permute-done.1.near_ref), custom_call_target="tpu_custom_call" | custom-call | flops 17179869184 | bytes 2097152 | tf_op jit(solution)/shard_map/attend/pallas_call | solution.py:284
  38.0 0.0 collective-permute-done.got_ref
  38.0 0.0 collective-permute-done.2.far_ref
  38.0 1.9 %attend.5 = bf16[640,128]{1,0:T(8,128)(2,1)S(1)} custom-call(bf16[2,8,32,128]{3,2,1,0:T(8,128)(2,1)S(1)} %bitcast.9, bf16[2064,128]{1,0:T(8,128)(2,1)S(1)} %collective-permute-done.got_ref, bf16[2064,128]{1,0:T(8,128)(2,1)S(1)} %collective-permute-done.2.far_ref, f32[3,4,128,128]{3,2,1,0:T(8,128)S(1)} %attend.4.so_far_ref, ...), custom_call_target="tpu_custom_call" | custom-call | tf_op jit(solution)/shard_map/attend/pallas_call | solution.py:296
  39.9 13.8 %all_to_all.15 = bf16[16,40,128]{2,1,0:T(8,128)(2,1)S(1)} all-to-all(bf16[16,40,128]{2,1,0:T(8,128)(2,1)S(1)} %bitcast.6), channel_id=1, replica_groups={{368,320,432,384,496,448,48,0,112,64,176,128,240,192,304,256},{352,336,..., dimensions={0} | all-to-all | bytes 327680 | tf_op jit(solution)/shard_map/merge/all_to_all | solution.py:63
  53.7 1.1 %merge.1 = bf16[4,1024]{1,0:T(4,128)(2,1)} custom-call(bf16[640,128]{1,0:T(8,128)(2,1)S(1)} %bitcast.7), custom_call_target="tpu_custom_call" | custom-call | tf_op jit(solution)/shard_map/merge/pallas_call | solution.py:307
Async XLA Ops:
  2.5 17.9 %all-to-all-start = ((bf16[32,8,128]{2,1,0:T(8,128)(2,1)}), bf16[32,8,128]{2,1,0:T(8,128)(2,1)S(1)}, u32[]{:S(2)}, u32[]{:S(2)}) async-start(bf16[32,8,128]{2,1,0:T(8,128)(2,1)} %bitcast.11), calls=%async_computation | async-start | bytes 131072 | tf_op jit(solution)/shard_map/query_spread/all_to_all | solution.py:63
  15.6 16.2 %collective-permute-start.1 = (bf16[2064,128]{1,0:T(8,128)(2,1)}, bf16[2064,128]{1,0:T(8,128)(2,1)S(1)}, u32[]{:S(2)}, u32[]{:S(2)}) collective-permute-start(bf16[2064,128]{1,0:T(8,128)(2,1)} %get-tuple-element.15.own_ref), channel_id=1, source_target_pairs={{0,16},{16,0},{48,32},{32,48},{1,17},{17,1},{49,33},{33,49},{2,18}... | collective-permute-start | bytes 1585160 | tf_op jit(solution)/shard_map/block_exchange/ppermute | solution.py:323
  20.4 9.0 %copy-start = (bf16[2064,128]{1,0:T(8,128)(2,1)S(1)}, bf16[2064,128]{1,0:T(8,128)(2,1)}, u32[]{:S(2)}) copy-start(bf16[2064,128]{1,0:T(8,128)(2,1)} %get-tuple-element.15.own_ref) | copy-start | bytes 1585156
  21.1 15.1 %all-to-all-start.1 = ((bf16[16,32,128]{2,1,0:T(8,128)(2,1)}), bf16[16,32,128]{2,1,0:T(8,128)(2,1)S(1)}, u32[]{:S(2)}, u32[]{:S(2)}) async-start(bf16[16,32,128]{2,1,0:T(8,128)(2,1)} %bitcast.2), calls=%async_computation.1 | async-start | bytes 262144 | tf_op jit(solution)/shard_map/query_turn/all_to_all | solution.py:63
  29.4 8.6 %collective-permute-start = (bf16[2064,128]{1,0:T(8,128)(2,1)S(1)}, bf16[2064,128]{1,0:T(8,128)(2,1)S(1)}, u32[]{:S(2)}, u32[]{:S(2)}) collective-permute-start(bf16[2064,128]{1,0:T(8,128)(2,1)S(1)} %copy-done), channel_id=1, source_target_pairs={{0,8},{8,0},{1,9},{9,1},{2,10},{10,2},{3,11},{11,3},{4,12},{12,4},... | collective-permute-start | bytes 1585160 | tf_op jit(solution)/shard_map/block_exchange/ppermute | solution.py:324
  31.8 6.3 %collective-permute-start.2 = (bf16[2064,128]{1,0:T(8,128)(2,1)S(1)}, bf16[2064,128]{1,0:T(8,128)(2,1)S(1)}, u32[]{:S(2)}, u32[]{:S(2)}) collective-permute-start(bf16[2064,128]{1,0:T(8,128)(2,1)S(1)} %collective-permute-done.1.near_ref), channel_id=1, source_target_pairs={{0,8},{8,0},{1,9},{9,1},{2,10},{10,2},{3,11},{11,3},{4,12},{12,4},... | collective-permute-start | bytes 1585160 | tf_op jit(solution)/shard_map/block_exchange/ppermute | solution.py:325
